TPU v7x, 512 devices: a whole 4x8x8 slice. The times are simulated.
512 devices in a mesh: ctx: 64 (over x, y_lo, z), kv: 8 (over y_hi, core).
Axes of the slice: x: 4, y: 8 (y_hi: 4, y_lo: 2; y = y_hi * 2 + y_lo), z: 8, core: 2. Of those that a mesh axis runs over, the one named last changes fastest.
Arguments:
- queries: bfloat16 [8192, 4096], P('ctx', 'kv'), may hold values from -6 to 6
- key_rows: bfloat16 [8192, 1024], P('ctx', 'kv'), may hold values from -6 to 6
- value_rows: bfloat16 [8192, 1024], P('ctx', 'kv'), may hold values from -6 to 6
- grad_out: bfloat16 [8192, 4096], P('ctx', 'kv'), may hold values from -6 to 6
- fwd_out: bfloat16 [8192, 4096], P('ctx', 'kv'), may hold values from -0.59765625 to 0.59765625
- log_norm: float32 [32, 8192], P('kv', 'ctx'), may hold values from 3 to 6
- span_order: int32 [128], P('ctx'), may hold values from 0 to 127, as said below
- doc_lengths: int32 [2], replicated, may hold values from 1 to 5120, 8192 in all
- key_proj: bfloat16 [4096, 1024], P(None, 'kv'), may hold values from -0.1875 to 0.1875
- value_proj: bfloat16 [4096, 1024], P(None, 'kv'), may hold values from -0.1875 to 0.1875
Outputs:
- grad_query: bfloat16 [8192, 4096], P('ctx', 'kv')
- grad_key: bfloat16 [8192, 1024], P('ctx', 'kv')
- grad_value: bfloat16 [8192, 1024], P('ctx', 'kv')
- grad_hidden: bfloat16 [8192, 4096], P('ctx', 'kv')
Inputs may be any that keep to these rules, and one draw needn't show every extreme that they name: `span_order`: A permutation of the 128 spans in which slots 2i and 2i + 1 hold spans that sum to 127. `doc_lengths`: the two lengths sum to 8192; neither is more than 5120.
All inputs are finite; a program needn't handle non-finite values.
Results may differ from a plain program's by a relative error of at most 0.022.
Values may be sent and summed in bfloat16 or wider, within the bound.
No kernel may reach another device: no remote copies, remote signals or barrier semaphores. Data moves between devices by JAX's collectives and lax.ppermute only.
A program may use at most 64 MiB of HBM per device.

v0:
```python
import math

import jax
import jax.numpy as jnp
from jax import lax
from jax.sharding import PartitionSpec as P


def from_behind(block, axis, distance):
    devices = range(lax.axis_size(axis))
    route = [((i - distance) % len(devices), i) for i in devices]
    return lax.ppermute(block, axis, route)


def contract_rows(left, right):
    return lax.dot_general(
        left, right, (((1,), (1,)), ((), ())), preferred_element_type=jnp.float32
    )


def body(
    queries,
    key_rows,
    value_rows,
    grad_out,
    fwd_out,
    log_norm,
    span_order,
    doc_lengths,
    key_proj,
    value_proj,
):
    tok_rows = queries.shape[0]
    span_len = tok_rows // 2
    head_dim = key_rows.shape[1]
    head_count = log_norm.shape[0]
    score_scale = 1.0 / math.sqrt(head_dim)
    cycle_size = lax.axis_size("ctx")
    half_cycle = cycle_size // 2
    my_index = lax.axis_index("ctx")
    slot_table = lax.all_gather(span_order, "ctx", axis=0, tiled=True)
    offsets = jnp.arange(span_len, dtype=jnp.int32)

    def block_positions(owner):
        pair = lax.dynamic_slice_in_dim(slot_table, owner * 2, 2, 0)
        return (pair[:, None] * span_len + offsets[None, :]).reshape(tok_rows)

    query_pos = block_positions(my_index)
    boundary = doc_lengths[0]
    query_heads = queries.reshape(tok_rows, head_count, head_dim)
    grad_heads = grad_out.reshape(tok_rows, head_count, head_dim)
    out_heads = fwd_out.reshape(tok_rows, head_count, head_dim)
    row_delta = jnp.sum(grad_heads.astype(jnp.float32) * out_heads.astype(jnp.float32), axis=2).T

    def dense_tile(key_block, value_block, live_mask):
        score = (
            jnp.einsum("qhd,kd->hqk", query_heads, key_block, preferred_element_type=jnp.float32)
            * score_scale
        )
        prob = jnp.where(live_mask[None], jnp.exp(score - log_norm[:, :, None]), 0.0)
        dprob = jnp.einsum(
            "qhd,kd->hqk", grad_heads, value_block, preferred_element_type=jnp.float32
        )
        dscore = prob * (dprob - row_delta[:, :, None])
        prob_b = prob.astype(jnp.bfloat16)
        dscore_b = dscore.astype(jnp.bfloat16)
        part_query = jnp.einsum(
            "hqk,kd->qhd", dscore_b, key_block, preferred_element_type=jnp.float32
        )
        part_key = jnp.einsum(
            "hqk,qhd->kd", dscore_b, query_heads, preferred_element_type=jnp.float32
        )
        part_value = jnp.einsum(
            "hqk,qhd->kd", prob_b, grad_heads, preferred_element_type=jnp.float32
        )
        return (part_query, part_key, part_value)

    def attend(key_block, value_block, key_pos):
        same_doc = (key_pos[None, :] >= boundary) == (query_pos[:, None] >= boundary)
        live_mask = (key_pos[None, :] <= query_pos[:, None]) & same_doc
        return dense_tile(key_block, value_block, live_mask)

    pair_kv = jnp.stack([key_rows, value_rows])

    def clock_turn(carried_kv, grad_block):
        carried_kv = from_behind(carried_kv, "ctx", 1)
        grad_block = from_behind(grad_block, "ctx", 1)
        return (carried_kv, grad_block)

    def counter_turn(carried_kv, grad_block):
        carried_kv = from_behind(carried_kv, "ctx", -1)
        grad_block = from_behind(grad_block, "ctx", -1)
        return (carried_kv, grad_block)

    own_query, own_key, own_value = attend(key_rows, value_rows, query_pos)
    zero_grads = jnp.zeros((2, tok_rows, head_dim), jnp.float32)

    def advance(step_index, cycle_state):
        grad_queries, clock_kv, counter_kv, clock_grads, counter_grads = cycle_state
        clock_kv, clock_grads = clock_turn(clock_kv, clock_grads)
        counter_kv, counter_grads = counter_turn(counter_kv, counter_grads)
        clock_owner = (my_index - step_index) % cycle_size
        counter_owner = (my_index + step_index) % cycle_size
        key_block = jnp.concatenate([clock_kv[0], counter_kv[0]], axis=0)
        value_block = jnp.concatenate([clock_kv[1], counter_kv[1]], axis=0)
        key_pos = jnp.concatenate(
            [block_positions(clock_owner), block_positions(counter_owner)], axis=0
        )
        part_query, part_key, part_value = attend(key_block, value_block, key_pos)
        clock_grads = clock_grads + jnp.stack([part_key[:tok_rows], part_value[:tok_rows]])
        counter_grads = counter_grads + jnp.stack([part_key[tok_rows:], part_value[tok_rows:]])
        return (grad_queries + part_query, clock_kv, counter_kv, clock_grads, counter_grads)

    cycle_state = lax.fori_loop(
        1, half_cycle, advance, (own_query, pair_kv, pair_kv, zero_grads, zero_grads)
    )
    grad_queries, clock_kv, counter_kv, clock_grads, counter_grads = cycle_state
    clock_kv, clock_grads = clock_turn(clock_kv, clock_grads)
    last_owner = (my_index - half_cycle) % cycle_size
    part_query, part_key, part_value = attend(clock_kv[0], clock_kv[1], block_positions(last_owner))
    grad_queries = grad_queries + part_query
    clock_grads = clock_grads + jnp.stack([part_key, part_value])
    clock_home = from_behind(clock_grads.astype(jnp.bfloat16), "ctx", -half_cycle).astype(
        clock_grads.dtype
    )
    counter_home = from_behind(counter_grads.astype(jnp.bfloat16), "ctx", half_cycle - 1).astype(
        counter_grads.dtype
    )
    total_grads = clock_home + counter_home + jnp.stack([own_key, own_value])
    grad_query = (
        (grad_queries * score_scale).astype(jnp.bfloat16).reshape(tok_rows, head_count * head_dim)
    )
    grad_key = (total_grads[0] * score_scale).astype(jnp.bfloat16)
    grad_value = total_grads[1].astype(jnp.bfloat16)
    partial_hidden = contract_rows(grad_key, key_proj) + contract_rows(grad_value, value_proj)
    hidden_sum = lax.psum_scatter(
        partial_hidden.astype(jnp.bfloat16), "kv", scatter_dimension=1, tiled=True
    )
    return (grad_query, grad_key, grad_value, hidden_sum)


def solution(mesh):
    placed = (
        P("ctx", "kv"),
        P("ctx", "kv"),
        P("ctx", "kv"),
        P("ctx", "kv"),
        P("ctx", "kv"),
        P("kv", "ctx"),
        P("ctx"),
        P(),
        P(None, "kv"),
        P(None, "kv"),
    )
    return jax.shard_map(
        body,
        mesh=mesh,
        in_specs=placed,
        out_specs=(P("ctx", "kv"), P("ctx", "kv"), P("ctx", "kv"), P("ctx", "kv")),
        check_vma=False,
    )
```

profile of v0, /device:TPU:17, one launch (start us, length us, event | category | flops | bytes accessed | tf_op | source)
XLA Modules:
  0.0 838.3 jit_solution(14555594341152698159)
XLA Ops:
  10.2 24.2 %all-reduce = s32[128]{0:T(128)S(1)} all-reduce(s32[128]{0:T(128)S(1)} %dynamic-update-slice), channel_id=1, replica_groups=mesh['ctx'=64,'kv'=8] {'ctx'}, use_global_device_ids=true, to_apply=%add | all-reduce | flops 128 | bytes 1024
  42.0 666.3 %while.25 = (s32[]{:T(128)}, f32[128,4,128]{0,2,1:T(8,128)S(1)}, bf16[2,128,128]{2,1,0:T(8,128)(2,1)S(1)}, bf16[2,128,128]{2,1,0:T(8,128)(2,1)S(1)}, f32[2,128,1...) while((s32[]{:T(128)}, f32[128,4,128]{0,2,1:T(8,128)S(1)}, ...), condition=%wide.region_2.3_spmd.clone.clone, body=%wide.region_1.2_spmd.clone.clone.sunk | while | flops 169444128 | bytes 7879670 | solution.py:114
  59.0 7.8 collective-permute-start
  80.5 7.8 collective-permute-start
  102.0 7.8 collective-permute-start
  124.0 8.1 collective-permute-start
  145.7 7.8 collective-permute-start
  167.2 7.8 collective-permute-start
  188.7 7.8 collective-permute-start
  210.2 7.8 collective-permute-start
  231.7 7.8 collective-permute-start
  253.3 8.0 collective-permute-start
  275.7 8.3 collective-permute-start
  297.7 7.8 collective-permute-start
  319.2 7.8 collective-permute-start
  362.2 7.8 collective-permute-start
  383.7 7.8 collective-permute-start
  405.2 7.8 collective-permute-start
  427.2 8.0 collective-permute-start
  448.9 7.8 collective-permute-start
  470.4 7.8 collective-permute-start
  491.9 7.8 collective-permute-start
  513.4 7.8 collective-permute-start
  534.9 7.8 collective-permute-start
  556.4 8.0 collective-permute-start
  578.8 8.3 collective-permute-start
  600.8 7.8 collective-permute-start
  622.3 7.8 collective-permute-start
  643.8 7.8 collective-permute-start
  665.3 7.8 collective-permute-start
  686.8 7.8 collective-permute-start
  734.7 96.8 %reduce-scatter.2.cloned.1.call-done = bf16[128,512]{1,0:T(8,128)(2,1)} async-done(((bf16[128,4096]{1,0:T(8,128)(2,1)}), bf16[128,512]{1,0:T(8,128)(2,1)}) %reduce-scatter.2.cloned.1.call-update) | async-done | bytes 131088 | tf_op jit(solution)/shard_map/reduce_scatter | solution.py:136
  (1121 shorter events, 465.1 us)
Async XLA Ops:
  7.2 824.3 %reduce-scatter.2.cloned.1.call-start = ((), (), s32[]{:S(2)}) async-start(), calls=%async_computation.1 | async-start | bytes 1179648 | tf_op jit(solution)/shard_map/reduce_scatter | solution.py:136
  59.0 20.1 %collective-permute-start = (bf16[2,128,128]{2,1,0:T(8,128)(2,1)S(1)}, bf16[2,128,128]{2,1,0:T(8,128)(2,1)S(1)}, u32[]{:S(2)}, u32[]{:S(2)}) collective-permute-start(bf16[2,128,128]{2,1,0:T(8,128)(2,1)S(1)} %get-tuple-element.665), channel_id=1, source_target_pairs={{8,0},{16,8},{24,16},{32,24},{40,32},{48,40},{56,48},{64,56},{72,6... | collective-permute-start | bytes 196616 | tf_op jit(solution)/shard_map/while/body/eval_jaxpr/ppermute | solution.py:12
  80.5 20.1 %collective-permute-start = (bf16[2,128,128]{2,1,0:T(8,128)(2,1)S(1)}, bf16[2,128,128]{2,1,0:T(8,128)(2,1)S(1)}, u32[]{:S(2)}, u32[]{:S(2)}) collective-permute-start(bf16[2,128,128]{2,1,0:T(8,128)(2,1)S(1)} %get-tuple-element.665), channel_id=1, source_target_pairs={{8,0},{16,8},{24,16},{32,24},{40,32},{48,40},{56,48},{64,56},{72,6... | collective-permute-start | bytes 196616 | tf_op jit(solution)/shard_map/while/body/eval_jaxpr/ppermute | solution.py:12
  102.0 20.1 %collective-permute-start = (bf16[2,128,128]{2,1,0:T(8,128)(2,1)S(1)}, bf16[2,128,128]{2,1,0:T(8,128)(2,1)S(1)}, u32[]{:S(2)}, u32[]{:S(2)}) collective-permute-start(bf16[2,128,128]{2,1,0:T(8,128)(2,1)S(1)} %get-tuple-element.665), channel_id=1, source_target_pairs={{8,0},{16,8},{24,16},{32,24},{40,32},{48,40},{56,48},{64,56},{72,6... | collective-permute-start | bytes 196616 | tf_op jit(solution)/shard_map/while/body/eval_jaxpr/ppermute | solution.py:12
  124.0 20.4 %collective-permute-start = (bf16[2,128,128]{2,1,0:T(8,128)(2,1)S(1)}, bf16[2,128,128]{2,1,0:T(8,128)(2,1)S(1)}, u32[]{:S(2)}, u32[]{:S(2)}) collective-permute-start(bf16[2,128,128]{2,1,0:T(8,128)(2,1)S(1)} %get-tuple-element.665), channel_id=1, source_target_pairs={{8,0},{16,8},{24,16},{32,24},{40,32},{48,40},{56,48},{64,56},{72,6... | collective-permute-start | bytes 196616 | tf_op jit(solution)/shard_map/while/body/eval_jaxpr/ppermute | solution.py:12
  145.7 20.1 %collective-permute-start = (bf16[2,128,128]{2,1,0:T(8,128)(2,1)S(1)}, bf16[2,128,128]{2,1,0:T(8,128)(2,1)S(1)}, u32[]{:S(2)}, u32[]{:S(2)}) collective-permute-start(bf16[2,128,128]{2,1,0:T(8,128)(2,1)S(1)} %get-tuple-element.665), channel_id=1, source_target_pairs={{8,0},{16,8},{24,16},{32,24},{40,32},{48,40},{56,48},{64,56},{72,6... | collective-permute-start | bytes 196616 | tf_op jit(solution)/shard_map/while/body/eval_jaxpr/ppermute | solution.py:12
  167.2 20.1 %collective-permute-start = (bf16[2,128,128]{2,1,0:T(8,128)(2,1)S(1)}, bf16[2,128,128]{2,1,0:T(8,128)(2,1)S(1)}, u32[]{:S(2)}, u32[]{:S(2)}) collective-permute-start(bf16[2,128,128]{2,1,0:T(8,128)(2,1)S(1)} %get-tuple-element.665), channel_id=1, source_target_pairs={{8,0},{16,8},{24,16},{32,24},{40,32},{48,40},{56,48},{64,56},{72,6... | collective-permute-start | bytes 196616 | tf_op jit(solution)/shard_map/while/body/eval_jaxpr/ppermute | solution.py:12
  188.7 20.1 %collective-permute-start = (bf16[2,128,128]{2,1,0:T(8,128)(2,1)S(1)}, bf16[2,128,128]{2,1,0:T(8,128)(2,1)S(1)}, u32[]{:S(2)}, u32[]{:S(2)}) collective-permute-start(bf16[2,128,128]{2,1,0:T(8,128)(2,1)S(1)} %get-tuple-element.665), channel_id=1, source_target_pairs={{8,0},{16,8},{24,16},{32,24},{40,32},{48,40},{56,48},{64,56},{72,6... | collective-permute-start | bytes 196616 | tf_op jit(solution)/shard_map/while/body/eval_jaxpr/ppermute | solution.py:12
  210.2 20.1 %collective-permute-start = (bf16[2,128,128]{2,1,0:T(8,128)(2,1)S(1)}, bf16[2,128,128]{2,1,0:T(8,128)(2,1)S(1)}, u32[]{:S(2)}, u32[]{:S(2)}) collective-permute-start(bf16[2,128,128]{2,1,0:T(8,128)(2,1)S(1)} %get-tuple-element.665), channel_id=1, source_target_pairs={{8,0},{16,8},{24,16},{32,24},{40,32},{48,40},{56,48},{64,56},{72,6... | collective-permute-start | bytes 196616 | tf_op jit(solution)/shard_map/while/body/eval_jaxpr/ppermute | solution.py:12
  231.7 20.1 %collective-permute-start = (bf16[2,128,128]{2,1,0:T(8,128)(2,1)S(1)}, bf16[2,128,128]{2,1,0:T(8,128)(2,1)S(1)}, u32[]{:S(2)}, u32[]{:S(2)}) collective-permute-start(bf16[2,128,128]{2,1,0:T(8,128)(2,1)S(1)} %get-tuple-element.665), channel_id=1, source_target_pairs={{8,0},{16,8},{24,16},{32,24},{40,32},{48,40},{56,48},{64,56},{72,6... | collective-permute-start | bytes 196616 | tf_op jit(solution)/shard_map/while/body/eval_jaxpr/ppermute | solution.py:12
  253.3 20.4 %collective-permute-start = (bf16[2,128,128]{2,1,0:T(8,128)(2,1)S(1)}, bf16[2,128,128]{2,1,0:T(8,128)(2,1)S(1)}, u32[]{:S(2)}, u32[]{:S(2)}) collective-permute-start(bf16[2,128,128]{2,1,0:T(8,128)(2,1)S(1)} %get-tuple-element.665), channel_id=1, source_target_pairs={{8,0},{16,8},{24,16},{32,24},{40,32},{48,40},{56,48},{64,56},{72,6... | collective-permute-start | bytes 196616 | tf_op jit(solution)/shard_map/while/body/eval_jaxpr/ppermute | solution.py:12
  275.7 20.6 %collective-permute-start = (bf16[2,128,128]{2,1,0:T(8,128)(2,1)S(1)}, bf16[2,128,128]{2,1,0:T(8,128)(2,1)S(1)}, u32[]{:S(2)}, u32[]{:S(2)}) collective-permute-start(bf16[2,128,128]{2,1,0:T(8,128)(2,1)S(1)} %get-tuple-element.665), channel_id=1, source_target_pairs={{8,0},{16,8},{24,16},{32,24},{40,32},{48,40},{56,48},{64,56},{72,6... | collective-permute-start | bytes 196616 | tf_op jit(solution)/shard_map/while/body/eval_jaxpr/ppermute | solution.py:12
  297.7 20.1 %collective-permute-start = (bf16[2,128,128]{2,1,0:T(8,128)(2,1)S(1)}, bf16[2,128,128]{2,1,0:T(8,128)(2,1)S(1)}, u32[]{:S(2)}, u32[]{:S(2)}) collective-permute-start(bf16[2,128,128]{2,1,0:T(8,128)(2,1)S(1)} %get-tuple-element.665), channel_id=1, source_target_pairs={{8,0},{16,8},{24,16},{32,24},{40,32},{48,40},{56,48},{64,56},{72,6... | collective-permute-start | bytes 196616 | tf_op jit(solution)/shard_map/while/body/eval_jaxpr/ppermute | solution.py:12
  319.2 20.1 %collective-permute-start = (bf16[2,128,128]{2,1,0:T(8,128)(2,1)S(1)}, bf16[2,128,128]{2,1,0:T(8,128)(2,1)S(1)}, u32[]{:S(2)}, u32[]{:S(2)}) collective-permute-start(bf16[2,128,128]{2,1,0:T(8,128)(2,1)S(1)} %get-tuple-element.665), channel_id=1, source_target_pairs={{8,0},{16,8},{24,16},{32,24},{40,32},{48,40},{56,48},{64,56},{72,6... | collective-permute-start | bytes 196616 | tf_op jit(solution)/shard_map/while/body/eval_jaxpr/ppermute | solution.py:12
  340.7 20.1 %collective-permute-start = (bf16[2,128,128]{2,1,0:T(8,128)(2,1)S(1)}, bf16[2,128,128]{2,1,0:T(8,128)(2,1)S(1)}, u32[]{:S(2)}, u32[]{:S(2)}) collective-permute-start(bf16[2,128,128]{2,1,0:T(8,128)(2,1)S(1)} %get-tuple-element.665), channel_id=1, source_target_pairs={{8,0},{16,8},{24,16},{32,24},{40,32},{48,40},{56,48},{64,56},{72,6... | collective-permute-start | bytes 196616 | tf_op jit(solution)/shard_map/while/body/eval_jaxpr/ppermute | solution.py:12
  362.2 20.1 %collective-permute-start = (bf16[2,128,128]{2,1,0:T(8,128)(2,1)S(1)}, bf16[2,128,128]{2,1,0:T(8,128)(2,1)S(1)}, u32[]{:S(2)}, u32[]{:S(2)}) collective-permute-start(bf16[2,128,128]{2,1,0:T(8,128)(2,1)S(1)} %get-tuple-element.665), channel_id=1, source_target_pairs={{8,0},{16,8},{24,16},{32,24},{40,32},{48,40},{56,48},{64,56},{72,6... | collective-permute-start | bytes 196616 | tf_op jit(solution)/shard_map/while/body/eval_jaxpr/ppermute | solution.py:12
  383.7 20.1 %collective-permute-start = (bf16[2,128,128]{2,1,0:T(8,128)(2,1)S(1)}, bf16[2,128,128]{2,1,0:T(8,128)(2,1)S(1)}, u32[]{:S(2)}, u32[]{:S(2)}) collective-permute-start(bf16[2,128,128]{2,1,0:T(8,128)(2,1)S(1)} %get-tuple-element.665), channel_id=1, source_target_pairs={{8,0},{16,8},{24,16},{32,24},{40,32},{48,40},{56,48},{64,56},{72,6... | collective-permute-start | bytes 196616 | tf_op jit(solution)/shard_map/while/body/eval_jaxpr/ppermute | solution.py:12
  405.2 20.1 %collective-permute-start = (bf16[2,128,128]{2,1,0:T(8,128)(2,1)S(1)}, bf16[2,128,128]{2,1,0:T(8,128)(2,1)S(1)}, u32[]{:S(2)}, u32[]{:S(2)}) collective-permute-start(bf16[2,128,128]{2,1,0:T(8,128)(2,1)S(1)} %get-tuple-element.665), channel_id=1, source_target_pairs={{8,0},{16,8},{24,16},{32,24},{40,32},{48,40},{56,48},{64,56},{72,6... | collective-permute-start | bytes 196616 | tf_op jit(solution)/shard_map/while/body/eval_jaxpr/ppermute | solution.py:12
  427.2 20.3 %collective-permute-start = (bf16[2,128,128]{2,1,0:T(8,128)(2,1)S(1)}, bf16[2,128,128]{2,1,0:T(8,128)(2,1)S(1)}, u32[]{:S(2)}, u32[]{:S(2)}) collective-permute-start(bf16[2,128,128]{2,1,0:T(8,128)(2,1)S(1)} %get-tuple-element.665), channel_id=1, source_target_pairs={{8,0},{16,8},{24,16},{32,24},{40,32},{48,40},{56,48},{64,56},{72,6... | collective-permute-start | bytes 196616 | tf_op jit(solution)/shard_map/while/body/eval_jaxpr/ppermute | solution.py:12
  448.9 20.1 %collective-permute-start = (bf16[2,128,128]{2,1,0:T(8,128)(2,1)S(1)}, bf16[2,128,128]{2,1,0:T(8,128)(2,1)S(1)}, u32[]{:S(2)}, u32[]{:S(2)}) collective-permute-start(bf16[2,128,128]{2,1,0:T(8,128)(2,1)S(1)} %get-tuple-element.665), channel_id=1, source_target_pairs={{8,0},{16,8},{24,16},{32,24},{40,32},{48,40},{56,48},{64,56},{72,6... | collective-permute-start | bytes 196616 | tf_op jit(solution)/shard_map/while/body/eval_jaxpr/ppermute | solution.py:12
  470.4 20.1 %collective-permute-start = (bf16[2,128,128]{2,1,0:T(8,128)(2,1)S(1)}, bf16[2,128,128]{2,1,0:T(8,128)(2,1)S(1)}, u32[]{:S(2)}, u32[]{:S(2)}) collective-permute-start(bf16[2,128,128]{2,1,0:T(8,128)(2,1)S(1)} %get-tuple-element.665), channel_id=1, source_target_pairs={{8,0},{16,8},{24,16},{32,24},{40,32},{48,40},{56,48},{64,56},{72,6... | collective-permute-start | bytes 196616 | tf_op jit(solution)/shard_map/while/body/eval_jaxpr/ppermute | solution.py:12
  491.9 20.1 %collective-permute-start = (bf16[2,128,128]{2,1,0:T(8,128)(2,1)S(1)}, bf16[2,128,128]{2,1,0:T(8,128)(2,1)S(1)}, u32[]{:S(2)}, u32[]{:S(2)}) collective-permute-start(bf16[2,128,128]{2,1,0:T(8,128)(2,1)S(1)} %get-tuple-element.665), channel_id=1, source_target_pairs={{8,0},{16,8},{24,16},{32,24},{40,32},{48,40},{56,48},{64,56},{72,6... | collective-permute-start | bytes 196616 | tf_op jit(solution)/shard_map/while/body/eval_jaxpr/ppermute | solution.py:12
  513.4 20.1 %collective-permute-start = (bf16[2,128,128]{2,1,0:T(8,128)(2,1)S(1)}, bf16[2,128,128]{2,1,0:T(8,128)(2,1)S(1)}, u32[]{:S(2)}, u32[]{:S(2)}) collective-permute-start(bf16[2,128,128]{2,1,0:T(8,128)(2,1)S(1)} %get-tuple-element.665), channel_id=1, source_target_pairs={{8,0},{16,8},{24,16},{32,24},{40,32},{48,40},{56,48},{64,56},{72,6... | collective-permute-start | bytes 196616 | tf_op jit(solution)/shard_map/while/body/eval_jaxpr/ppermute | solution.py:12
  534.9 20.1 %collective-permute-start = (bf16[2,128,128]{2,1,0:T(8,128)(2,1)S(1)}, bf16[2,128,128]{2,1,0:T(8,128)(2,1)S(1)}, u32[]{:S(2)}, u32[]{:S(2)}) collective-permute-start(bf16[2,128,128]{2,1,0:T(8,128)(2,1)S(1)} %get-tuple-element.665), channel_id=1, source_target_pairs={{8,0},{16,8},{24,16},{32,24},{40,32},{48,40},{56,48},{64,56},{72,6... | collective-permute-start | bytes 196616 | tf_op jit(solution)/shard_map/while/body/eval_jaxpr/ppermute | solution.py:12
  556.4 20.3 %collective-permute-start = (bf16[2,128,128]{2,1,0:T(8,128)(2,1)S(1)}, bf16[2,128,128]{2,1,0:T(8,128)(2,1)S(1)}, u32[]{:S(2)}, u32[]{:S(2)}) collective-permute-start(bf16[2,128,128]{2,1,0:T(8,128)(2,1)S(1)} %get-tuple-element.665), channel_id=1, source_target_pairs={{8,0},{16,8},{24,16},{32,24},{40,32},{48,40},{56,48},{64,56},{72,6... | collective-permute-start | bytes 196616 | tf_op jit(solution)/shard_map/while/body/eval_jaxpr/ppermute | solution.py:12
  578.8 20.6 %collective-permute-start = (bf16[2,128,128]{2,1,0:T(8,128)(2,1)S(1)}, bf16[2,128,128]{2,1,0:T(8,128)(2,1)S(1)}, u32[]{:S(2)}, u32[]{:S(2)}) collective-permute-start(bf16[2,128,128]{2,1,0:T(8,128)(2,1)S(1)} %get-tuple-element.665), channel_id=1, source_target_pairs={{8,0},{16,8},{24,16},{32,24},{40,32},{48,40},{56,48},{64,56},{72,6... | collective-permute-start | bytes 196616 | tf_op jit(solution)/shard_map/while/body/eval_jaxpr/ppermute | solution.py:12
  600.8 20.1 %collective-permute-start = (bf16[2,128,128]{2,1,0:T(8,128)(2,1)S(1)}, bf16[2,128,128]{2,1,0:T(8,128)(2,1)S(1)}, u32[]{:S(2)}, u32[]{:S(2)}) collective-permute-start(bf16[2,128,128]{2,1,0:T(8,128)(2,1)S(1)} %get-tuple-element.665), channel_id=1, source_target_pairs={{8,0},{16,8},{24,16},{32,24},{40,32},{48,40},{56,48},{64,56},{72,6... | collective-permute-start | bytes 196616 | tf_op jit(solution)/shard_map/while/body/eval_jaxpr/ppermute | solution.py:12
  622.3 20.1 %collective-permute-start = (bf16[2,128,128]{2,1,0:T(8,128)(2,1)S(1)}, bf16[2,128,128]{2,1,0:T(8,128)(2,1)S(1)}, u32[]{:S(2)}, u32[]{:S(2)}) collective-permute-start(bf16[2,128,128]{2,1,0:T(8,128)(2,1)S(1)} %get-tuple-element.665), channel_id=1, source_target_pairs={{8,0},{16,8},{24,16},{32,24},{40,32},{48,40},{56,48},{64,56},{72,6... | collective-permute-start | bytes 196616 | tf_op jit(solution)/shard_map/while/body/eval_jaxpr/ppermute | solution.py:12
  643.8 20.1 %collective-permute-start = (bf16[2,128,128]{2,1,0:T(8,128)(2,1)S(1)}, bf16[2,128,128]{2,1,0:T(8,128)(2,1)S(1)}, u32[]{:S(2)}, u32[]{:S(2)}) collective-permute-start(bf16[2,128,128]{2,1,0:T(8,128)(2,1)S(1)} %get-tuple-element.665), channel_id=1, source_target_pairs={{8,0},{16,8},{24,16},{32,24},{40,32},{48,40},{56,48},{64,56},{72,6... | collective-permute-start | bytes 196616 | tf_op jit(solution)/shard_map/while/body/eval_jaxpr/ppermute | solution.py:12
  665.3 20.1 %collective-permute-start = (bf16[2,128,128]{2,1,0:T(8,128)(2,1)S(1)}, bf16[2,128,128]{2,1,0:T(8,128)(2,1)S(1)}, u32[]{:S(2)}, u32[]{:S(2)}) collective-permute-start(bf16[2,128,128]{2,1,0:T(8,128)(2,1)S(1)} %get-tuple-element.665), channel_id=1, source_target_pairs={{8,0},{16,8},{24,16},{32,24},{40,32},{48,40},{56,48},{64,56},{72,6... | collective-permute-start | bytes 196616 | tf_op jit(solution)/shard_map/while/body/eval_jaxpr/ppermute | solution.py:12
  686.8 20.1 %collective-permute-start = (bf16[2,128,128]{2,1,0:T(8,128)(2,1)S(1)}, bf16[2,128,128]{2,1,0:T(8,128)(2,1)S(1)}, u32[]{:S(2)}, u32[]{:S(2)}) collective-permute-start(bf16[2,128,128]{2,1,0:T(8,128)(2,1)S(1)} %get-tuple-element.665), channel_id=1, source_target_pairs={{8,0},{16,8},{24,16},{32,24},{40,32},{48,40},{56,48},{64,56},{72,6... | collective-permute-start | bytes 196616 | tf_op jit(solution)/shard_map/while/body/eval_jaxpr/ppermute | solution.py:12
  708.3 21.9 %collective-permute-start.7 = (bf16[2,128,128]{2,1,0:T(8,128)(2,1)S(1)}, bf16[2,128,128]{2,1,0:T(8,128)(2,1)S(1)}, u32[]{:S(2)}, u32[]{:S(2)}) collective-permute-start(bf16[2,128,128]{2,1,0:T(8,128)(2,1)S(1)} %convert_element_type.78), channel_id=1, source_target_pairs={{264,0},{272,8},{280,16},{288,24},{296,32},{304,40},{312,48},{320,... | collective-permute-start | bytes 196616 | tf_op jit(solution)/shard_map/ppermute | solution.py:12
  (105 other events, 1970.3 us)
Sparse Core Ops, SparseCore 0:
  733.8 97.5 reduce-scatter.1
where the time goes:
time: 843 us; the launch traced here: 838 us
  starting transfers between devices  607 us (72%)
  waiting for transfers between devices  108 us (13%)
  matrix products  39.7 us (5%)
  blocking collectives  24.2 us (3%)
  other arithmetic  17.9 us (2%)
  local copies, waits for them, and re-layouts  17 us (2%)
  between operations  15.1 us (2%)
  loops' own time  8.54 us (1%)
    ppermute x128, starting transfers between devices, from_behind(): return lax.ppermute(block, axis, route)  607 us
    reduce_scatter x1, waiting for transfers between devices, body(): lax.psum_scatter(partial_hidden.astype(jnp.bfloat16), 'kv', scatter_dimen...  96.8 us
    unnamed x1, blocking collectives  24.2 us
  transfers between devices with their start and end apart: 129, of which 9 were waited for; matrix products, arithmetic and copies ran while one was open for 7% of the time, Pallas kernels for 0%

commit v1 on v0

v1 whole, which is shorter than its diff:
```python
import math

import jax
import jax.numpy as jnp
from jax import lax
from jax.experimental import pallas as pl
from jax.experimental.pallas import tpu as pltpu
from jax.sharding import Mesh, PartitionSpec as P

AXES = ("x", "y_lo", "z", "y_hi", "core")
CTX = ("x", "y_lo", "z")
KEYS = ("y_lo", "z")
KV = ("y_hi", "core")
SPAN = 64
HD = 128
HQ = 4
TOK = 2 * SPAN
QROWS = HQ * SPAN
CHUNK = 256
PER = CHUNK // SPAN
QBLOCK = 2 * HQ * TOK + 32
KBLOCK = 2 * TOK + 16
BF = jnp.bfloat16
F32 = jnp.float32


def nt(a, b):
    return lax.dot_general(a, b, (((1,), (1,)), ((), ())), preferred_element_type=F32)


def nn(a, b):
    return lax.dot_general(a, b, (((1,), (0,)), ((), ())), preferred_element_type=F32)


def prep_kernel(span_ref, q_ref, g_ref, o_ref, lse_ref, out_ref):
    lse_rows, delta_rows = [], []
    for s in range(2):
        rows = slice(s * SPAN, (s + 1) * SPAN)
        for pair in range(HQ // 2):
            prods = []
            for h in (2 * pair, 2 * pair + 1):
                cols = slice(h * HD, (h + 1) * HD)
                at = s * QROWS + h * SPAN
                g = g_ref[rows, cols]
                out_ref[at : at + SPAN, :] = q_ref[rows, cols]
                out_ref[HQ * TOK + at : HQ * TOK + at + SPAN, :] = g
                prods.append(g.astype(F32) * o_ref[rows, cols].astype(F32))
            both = jnp.concatenate(prods, axis=0)
            delta_rows.append(jnp.sum(both.T, axis=0, keepdims=True))
            lse_rows.append(
                jnp.concatenate(
                    [lse_ref[2 * pair : 2 * pair + 1, rows], lse_ref[2 * pair + 1 : 2 * pair + 2, rows]],
                    axis=1,
                )
            )
    parts = []
    for rows in (lse_rows, delta_rows):
        rest = jnp.concatenate(rows, axis=0)
        for _ in range(3):
            piece = rest.astype(BF).astype(F32)
            rest = rest - piece
            parts.append(piece)
    line = lax.broadcasted_iota(jnp.int32, (8, HD), 0)
    spans = jnp.where(line == 0, span_ref[0], span_ref[1]).astype(F32)
    parts.append(spans)
    out_ref[2 * HQ * TOK :, :] = jnp.concatenate(parts, axis=0).astype(BF)


def tile_kernel(n_q, n_k, table, gq_ref, gkv_ref, dq_ref, dkv_ref, k_s, v_s, kt_s, dk_acc, dv_acc, dqt_acc, lse_s, del_s):
    spans_k = 2 * n_k
    scale = 1.0 / math.sqrt(HD)

    def rank_of(j):
        return table[j]

    def sorted_span(j):
        return table[spans_k + j]

    def q_info(i, what):
        return table[2 * spans_k + 4 * i + what]

    boundary = table[2 * spans_k + 8 * n_q]
    dk_acc[...] = jnp.zeros_like(dk_acc)
    dv_acc[...] = jnp.zeros_like(dv_acc)
    for w in range(n_k):
        for s in range(2):
            to = pl.ds(pl.multiple_of(rank_of(2 * w + s) * SPAN, SPAN), SPAN)
            k_s[to, :] = gkv_ref[w, s * SPAN : (s + 1) * SPAN, :]
            v_s[to, :] = gkv_ref[w, TOK + s * SPAN : TOK + (s + 1) * SPAN, :]
    for c in range(spans_k // PER):
        rows = slice(c * CHUNK, (c + 1) * CHUNK)
        kt_s[c] = k_s[rows, :].T
    for x in range(n_q):
        extra = gq_ref[x, 2 * HQ * TOK : 2 * HQ * TOK + 24, :].astype(F32)
        lse = extra[0:4] + extra[4:8] + extra[8:12]
        dlt = extra[12:16] + extra[16:20] + extra[20:24]
        for s in range(2):
            i = 2 * x + s
            lse_s[i] = jnp.broadcast_to(jnp.concatenate([lse[2 * s : 2 * s + 1], lse[2 * s + 1 : 2 * s + 2]], axis=1), (8, QROWS))
            del_s[i] = jnp.broadcast_to(jnp.concatenate([dlt[2 * s : 2 * s + 1], dlt[2 * s + 1 : 2 * s + 2]], axis=1), (8, QROWS))

    key_line = lax.broadcasted_iota(jnp.int32, (SPAN, QROWS), 0)
    row_off = lax.broadcasted_iota(jnp.int32, (1, QROWS), 1) % SPAN

    def q_step(i, _):
        x, s = i // 2, i % 2
        at = pl.multiple_of(s * QROWS, QROWS)
        q = gq_ref[x, pl.ds(at, QROWS), :]
        g = gq_ref[x, pl.ds(HQ * TOK + at, QROWS), :]
        lse = lse_s[i][0:1]
        dlt = del_s[i][0:1]
        q_pos = q_info(i, 0) * SPAN + row_off
        q_start = jnp.where(q_pos >= boundary, boundary, 0)
        dqt_acc[...] = jnp.zeros_like(dqt_acc)

        def k_step(c, _):
            rows = pl.ds(pl.multiple_of(c * CHUNK, CHUNK), CHUNK)
            k = k_s[rows, :]
            score = nt(k, q)
            dprob = nt(v_s[rows, :], g)
            probs, dscores = [], []
            for j in range(PER):
                part = slice(j * SPAN, (j + 1) * SPAN)
                base = sorted_span(c * PER + j) * SPAN
                live = (key_line <= q_pos - base) & (key_line >= q_start - base)
                prob = jnp.where(live, jnp.exp(score[part] * scale - lse), 0.0)
                probs.append(prob.astype(BF))
                dscores.append((prob * (dprob[part] - dlt)).astype(BF))
            prob_b = jnp.concatenate(probs, axis=0)
            dscore_b = jnp.concatenate(dscores, axis=0)
            dv_acc[rows, :] += nn(prob_b, g)
            dk_acc[rows, :] += nn(dscore_b, q)
            dqt_acc[...] += nn(kt_s[c], dscore_b)
            return 0

        lax.fori_loop(q_info(i, 1), q_info(i, 2), k_step, 0)
        dq = (dqt_acc[...] * scale).T.astype(BF)
        to = pl.ds(pl.multiple_of(i * SPAN, SPAN), SPAN)
        for h in range(HQ):
            dq_ref[to, h * HD : (h + 1) * HD] = dq[h * SPAN : (h + 1) * SPAN]
        return 0

    lax.fori_loop(0, 2 * n_q, q_step, 0)
    for w in range(n_k):
        for s in range(2):
            at = pl.ds(pl.multiple_of(rank_of(2 * w + s) * SPAN, SPAN), SPAN)
            dkv_ref[w, s * SPAN : (s + 1) * SPAN, :] = dk_acc[at, :].astype(BF)
            dkv_ref[w, TOK + s * SPAN : TOK + (s + 1) * SPAN, :] = dv_acc[at, :].astype(BF)


VMEM = pl.BlockSpec(memory_space=pltpu.VMEM)
SMEM = pl.BlockSpec(memory_space=pltpu.SMEM)


def tile_grads(table, gq, gkv):
    n_q, n_k = gq.shape[0], gkv.shape[0]
    keys = n_k * TOK
    return pl.pallas_call(
        lambda *refs: tile_kernel(n_q, n_k, *refs),
        out_shape=(
            jax.ShapeDtypeStruct((n_q * TOK, HQ * HD), BF),
            jax.ShapeDtypeStruct((n_k, 2 * TOK, HD), BF),
        ),
        in_specs=[SMEM, VMEM, VMEM],
        out_specs=(VMEM, VMEM),
        scratch_shapes=[
            pltpu.VMEM((keys, HD), BF),
            pltpu.VMEM((keys, HD), BF),
            pltpu.VMEM((keys // CHUNK, HD, CHUNK), BF),
            pltpu.VMEM((keys, HD), F32),
            pltpu.VMEM((keys, HD), F32),
            pltpu.VMEM((HD, QROWS), F32),
            pltpu.VMEM((2 * n_q, 8, QROWS), F32),
            pltpu.VMEM((2 * n_q, 8, QROWS), F32),
        ],
        compiler_params=pltpu.CompilerParams(vmem_limit_bytes=32 * 1024 * 1024),
        cost_estimate=pl.CostEstimate(flops=5_000_000_000, bytes_accessed=4_000_000, transcendentals=2_000_000),
        name="tile_grads",
    )(table, gq, gkv)


def prep(span_order, queries, grad_out, fwd_out, log_norm):
    return pl.pallas_call(
        prep_kernel,
        out_shape=jax.ShapeDtypeStruct((QBLOCK, HD), BF),
        in_specs=[SMEM, VMEM, VMEM, VMEM, VMEM],
        out_specs=VMEM,
        name="prep",
    )(span_order, queries, grad_out, fwd_out, log_norm)


def body(queries, key_rows, value_rows, grad_out, fwd_out, log_norm, span_order, doc_lengths, key_proj, value_proj):
    n_q, n_k = lax.axis_size("x"), lax.axis_size(KEYS)
    n_hi = lax.axis_size("y_hi")
    scale = 1.0 / math.sqrt(HD)
    core = lax.axis_index("core")
    y_hi = lax.axis_index("y_hi")

    tag = jnp.broadcast_to(jnp.pad(span_order, (0, 14))[:, None], (16, HD)).astype(BF)
    mine = jnp.concatenate([key_rows, value_rows, tag], axis=0)
    gkv = lax.all_to_all(jnp.broadcast_to(mine[None], (n_k, KBLOCK, HD)), KEYS, 0, 0)
    gq = lax.all_gather(prep(span_order, queries, grad_out, fwd_out, log_norm), "x", axis=0)

    cols = key_proj.shape[0] // (2 * n_hi)
    projs = jnp.stack([key_proj, value_proj], axis=0).reshape(2, n_hi, 2, cols, HD)
    kept = lax.dynamic_index_in_dim(projs, core, 2, keepdims=False)
    given = lax.dynamic_index_in_dim(projs, 1 - core, 2, keepdims=False)
    swapped = lax.ppermute(given, "core", [(0, 1), (1, 0)])
    both = jnp.stack([kept, swapped], axis=1)
    pieces = [lax.dynamic_index_in_dim(both, y_hi, 2, keepdims=False)]
    for shift in range(1, n_hi):
        out = lax.dynamic_index_in_dim(both, (y_hi + shift) % n_hi, 2, keepdims=False)
        pieces.append(lax.ppermute(out, "y_hi", [(i, (i + shift) % n_hi) for i in range(n_hi)]))

    q_span = gq[:, 2 * HQ * TOK + 24 : 2 * HQ * TOK + 26, 0].reshape(2 * n_q).astype(jnp.int32)
    k_span = gkv[:, 2 * TOK : 2 * TOK + 2, 0].reshape(2 * n_k).astype(jnp.int32)
    boundary = doc_lengths[0]
    rank = jnp.sum((k_span[None, :] < k_span[:, None]).astype(jnp.int32), axis=1)
    slots = jnp.arange(2 * n_k, dtype=jnp.int32)
    in_order = jnp.sum(jnp.where(rank[None, :] == slots[:, None], k_span[None, :], 0), axis=1)
    first = jnp.where(q_span * SPAN >= boundary, boundary // SPAN, 0)
    below = jnp.sum((k_span[None, :] < first[:, None]).astype(jnp.int32), axis=1)
    upto = jnp.sum((k_span[None, :] <= q_span[:, None]).astype(jnp.int32), axis=1)
    info = jnp.stack([q_span, below // PER, (upto + PER - 1) // PER, q_span], axis=1).reshape(8 * n_q)
    table = jnp.concatenate([rank, in_order, info, doc_lengths])

    dq, dkv = tile_grads(table, gq, gkv)
    grad_query = lax.psum_scatter(dq, "x", scatter_dimension=0, tiled=True)
    parts = lax.all_to_all(dkv, KEYS, 0, 0)
    total = jnp.sum(parts.astype(F32), axis=0)
    grad_key = (total[:TOK] * scale).astype(BF)
    grad_value = total[TOK:].astype(BF)

    groups = lax.all_gather(jnp.concatenate([grad_key, grad_value], axis=1), KV, axis=0)
    hidden = jnp.zeros((TOK, cols), F32)
    for shift in range(n_hi):
        for far in range(2):
            source = ((y_hi - shift) % n_hi) * 2 + (core if far == 0 else 1 - core)
            block = lax.dynamic_index_in_dim(groups, source, 0, keepdims=False)
            piece = pieces[shift]
            own_first = piece[:, far]
            weight = jnp.concatenate([own_first[0], own_first[1]], axis=1)
            hidden = hidden + nt(block, weight)
    return grad_query, grad_key, grad_value, hidden.astype(BF)


def solution(mesh):
    fine = Mesh(mesh.devices.reshape(4, 2, 8, 4, 2), AXES)
    placed = (
        P(CTX, KV),
        P(CTX, KV),
        P(CTX, KV),
        P(CTX, KV),
        P(CTX, KV),
        P(KV, CTX),
        P(CTX),
        P(),
        P(None, KV),
        P(None, KV),
    )
    return jax.shard_map(
        body,
        mesh=fine,
        in_specs=placed,
        out_specs=(P(CTX, KV), P(CTX, KV), P(CTX, KV), P(CTX, KV)),
        check_vma=False,
    )
```

time: 843 us -> 173 us (0.21)
  the two profiles are of different devices: /device:TPU:17 before, /device:TPU:8 now
where the time goes in v1:
time: 173 us
  waiting for transfers between devices  74.7 us (43%)
  starting transfers between devices  37.6 us (22%)
  Pallas kernels  15.9 us (9%)
  blocking collectives  15.1 us (9%)
  between operations  14.6 us (8%)
  other arithmetic  7.37 us (4%)
  local copies, waits for them, and re-layouts  4.78 us (3%)
  matrix products  2.46 us (1%)
    ppermute x3, waiting for transfers between devices, body(): lax.ppermute(out, 'y_hi', [(i, (i + shift) % n_hi) for i in range(n_hi)])  41.5 us
    all_gather x1, waiting for transfers between devices, body(): lax.all_gather(prep(span_order, queries, grad_out, fwd_out, log_norm), 'x...  25.9 us
    all_gather x1, blocking collectives, body(): lax.all_gather(jnp.concatenate([grad_key, grad_value], axis=1), KV, axis=0)  15.1 us
    ppermute x3, starting transfers between devices, body(): lax.ppermute(out, 'y_hi', [(i, (i + shift) % n_hi) for i in range(n_hi)])  14.4 us
    pallas_call x1, Pallas kernels, tile_grads(): pl.pallas_call(lambda *refs: tile_kernel(n_q, n_k, *refs), out_shape=(jax...  13.9 us
    all_to_all x1, starting transfers between devices, body(): lax.all_to_all(jnp.broadcast_to(mine[None], (n_k, KBLOCK, HD)), KEYS, 0, 0)  11.9 us
    all_to_all x1, starting transfers between devices, body(): parts = lax.all_to_all(dkv, KEYS, 0, 0)  9.32 us
    reduce_scatter x1, waiting for transfers between devices, body(): grad_query = lax.psum_scatter(dq, 'x', scatter_dimension=0, tiled=True)  7.24 us
  transfers between devices with their start and end apart: 8, of which 5 were waited for; matrix products, arithmetic and copies ran while one was open for 6% of the time, Pallas kernels for 9%

profile of v1, /device:TPU:8, one launch (start us, length us, event | category | flops | bytes accessed | tf_op | source)
XLA Modules:
  0.0 172.5 jit_solution(11240702683026681002)
XLA Ops:
  7.2 0.7 convert.10
  7.8 0.9 maximum_maximum_fusion
  8.7 1.1 broadcast_in_dim.25
  9.8 11.9 %all-to-all-start = ((bf16[16,272,128]{2,1,0:T(8,128)(2,1)}), bf16[16,272,128]{2,1,0:T(8,128)(2,1)S(1)}, u32[]{:S(2)}, u32[]{:S(2)}) async-start(bf16[16,272,128]{2,1,0:T(8,128)(2,1)} %broadcast_in_dim.25), calls=%async_computation | async-start | bytes 2228224 | tf_op jit(solution)/shard_map/all_to_all | solution.py:201
  21.8 1.9 %prep.1 = bf16[1056,128]{1,0:T(8,128)(2,1)} custom-call(s32[2]{0:T(128)} %span_ref.1, bf16[128,512]{1,0:T(8,128)(2,1)} %q_ref.1, bf16[128,512]{1,0:T(8,128)(2,1)} %g_ref.1, bf16[128,512]{1,0:T(8,128)(2,1)} %o_ref.1, f32[4,128]{1,0:T(4,128)} %lse_ref.1), custom_call_target="tpu_custom_call" | custom-call | tf_op jit(solution)/shard_map/prep/pallas_call | solution.py:183
  23.8 1.4 fusion.1
  25.2 1.1 copy.34
  26.3 1.9 %collective-permute-start = (bf16[2,4,512,128]{3,2,0,1:T(8,128)(2,1)}, bf16[2,4,512,128]{3,2,0,1:T(8,128)(2,1)}, u32[]{:S(2)}, u32[]{:S(2)}) collective-permute-start(bf16[2,4,512,128]{3,2,0,1:T(8,128)(2,1)} %bitcast.90), channel_id=1, source_target_pairs={{0,1},{1,0},{2,3},{3,2},{4,5},{5,4},{6,7},{7,6},{8,9},{9,8},{10,11... | collective-permute-start | bytes 3145736 | tf_op jit(solution)/shard_map/ppermute | solution.py:208
  28.4 25.9 %all-gather.4.cloned.1.call-done = bf16[4224,128]{1,0:T(8,128)(2,1)} async-done(((bf16[1056,128]{1,0:T(8,128)(2,1)}), bf16[4224,128]{1,0:T(8,128)(2,1)}) %all-gather.4.cloned.1.call-update) | async-done | bytes 1081360 | tf_op jit(solution)/shard_map/all_gather | solution.py:202
  54.2 0.8 convert_reduce_fusion.3
  55.3 0.3 convert_reduce_fusion.1
  55.9 0.2 convert_reduce_fusion.5
  56.6 1.2 copy-done
  57.8 13.9 %tile_grads.1 = (bf16[512,512]{1,0:T(8,128)(2,1)}, bf16[16,256,128]{2,1,0:T(8,128)(2,1)}) custom-call(s32[98]{0:T(128)S(1)} %pad_add_fusion.1.refs_0_, bf16[4,1056,128]{2,1,0:T(8,128)(2,1)S(1)} %bitcast.94, bf16[16,272,128]{2,1,0:T(8,128)(2,1)S(1)} %all-to-all-done.refs_2_), custom_call_target="tpu_custom_call" | custom-call | flops 5000000000 | bytes 4000000 | tf_op jit(solution)/shard_map/tile_grads/pallas_call | solution.py:158
  71.7 9.3 %all-to-all-start.1 = ((bf16[16,256,128]{2,1,0:T(8,128)(2,1)}), bf16[16,256,128]{2,1,0:T(8,128)(2,1)S(1)}, u32[]{:S(2)}, u32[]{:S(2)}) async-start(bf16[16,256,128]{2,1,0:T(8,128)(2,1)} %get-tuple-element.7), calls=%async_computation.2 | async-start | bytes 2097152 | tf_op jit(solution)/shard_map/all_to_all | solution.py:229
  81.3 2.4 %fusion.4 = (bf16[2,2,512,128]{3,2,1,0:T(8,128)(2,1)}, bf16[2,2,512,128]{3,2,1,0:T(8,128)(2,1)S(1)}, bf16[2,2,512,128]{3,2,1,0:T(8,128)(2,1)}, bf16[2,2,512,128]{3,2,1,0:T(8,128)(2,1)}) fusion(s32[]{:T(128)S(6)} %select_n.146, bf16[2,1,4,512,128]{4,3,1,0,2:T(8,128)(2,1)S(1)} %bitcast.95, bf16[2,1,4,512,128]{4,3,1,0,2:T(8,128)(2,1)} %bitcast.10, ...), kind=kLoop, calls=%fused_computation.26 | loop fusion | flops 1048576 | bytes 4194320 | tf_op jit(solution)/shard_map/jit(dynamic_index_in_dim)/squeeze | solution.py:212
  83.7 4.3 %collective-permute-start.1 = (bf16[2,2,512,128]{3,2,1,0:T(8,128)(2,1)}, bf16[2,2,512,128]{3,2,1,0:T(8,128)(2,1)S(1)}, u32[]{:S(2)}, u32[]{:S(2)}) collective-permute-start(bf16[2,2,512,128]{3,2,1,0:T(8,128)(2,1)} %get-tuple-element.12), channel_id=1, source_target_pairs={{0,2},{2,4},{4,6},{6,0},{1,3},{3,5},{5,7},{7,1},{8,10},{10,12},{12... | collective-permute-start | bytes 1572872 | tf_op jit(solution)/shard_map/ppermute | solution.py:213
  88.0 4.7 %collective-permute-start.2 = (bf16[2,2,512,128]{3,2,1,0:T(8,128)(2,1)}, bf16[2,2,512,128]{3,2,1,0:T(8,128)(2,1)S(1)}, u32[]{:S(2)}, u32[]{:S(2)}) collective-permute-start(bf16[2,2,512,128]{3,2,1,0:T(8,128)(2,1)} %get-tuple-element.13), channel_id=1, source_target_pairs={{0,4},{2,6},{4,0},{6,2},{1,5},{3,7},{5,1},{7,3},{8,12},{10,14},{12... | collective-permute-start | bytes 1572872 | tf_op jit(solution)/shard_map/ppermute | solution.py:213
  92.8 5.4 %collective-permute-start.3 = (bf16[2,2,512,128]{3,2,1,0:T(8,128)(2,1)}, bf16[2,2,512,128]{3,2,1,0:T(8,128)(2,1)S(1)}, u32[]{:S(2)}, u32[]{:S(2)}) collective-permute-start(bf16[2,2,512,128]{3,2,1,0:T(8,128)(2,1)} %get-tuple-element.10), channel_id=1, source_target_pairs={{0,6},{2,0},{4,2},{6,4},{1,7},{3,1},{5,3},{7,5},{8,14},{10,8},{12,... | collective-permute-start | bytes 1572872 | tf_op jit(solution)/shard_map/ppermute | solution.py:213
  98.3 1.9 %collective-permute-done.1 = bf16[2,2,512,128]{3,2,1,0:T(8,128)(2,1)S(1)} collective-permute-done((bf16[2,2,512,128]{3,2,1,0:T(8,128)(2,1)}, bf16[2,2,512,128]{3,2,1,0:T(8,128)(2,1)S(1)}, u32[]{:S(2)}, u32[]{:S(2)}) %collective-permute-start.1) | collective-permute-done | bytes 524320 | tf_op jit(solution)/shard_map/ppermute | solution.py:213
  100.2 0.7 slice_bitcast_fusion.9
  100.9 32.8 %collective-permute-done.2 = bf16[2,2,512,128]{3,2,1,0:T(8,128)(2,1)S(1)} collective-permute-done((bf16[2,2,512,128]{3,2,1,0:T(8,128)(2,1)}, bf16[2,2,512,128]{3,2,1,0:T(8,128)(2,1)S(1)}, u32[]{:S(2)}, u32[]{:S(2)}) %collective-permute-start.2) | collective-permute-done | bytes 524320 | tf_op jit(solution)/shard_map/ppermute | solution.py:213
  133.7 6.8 %collective-permute-done.3 = bf16[2,2,512,128]{3,2,1,0:T(8,128)(2,1)S(1)} collective-permute-done((bf16[2,2,512,128]{3,2,1,0:T(8,128)(2,1)}, bf16[2,2,512,128]{3,2,1,0:T(8,128)(2,1)S(1)}, u32[]{:S(2)}, u32[]{:S(2)}) %collective-permute-start.3) | collective-permute-done | bytes 524320 | tf_op jit(solution)/shard_map/ppermute | solution.py:213
  140.8 15.1 %all-gather.1 = bf16[1024,256]{1,0:T(8,128)(2,1)S(1)} all-gather(bf16[128,256]{1,0:T(8,128)(2,1)S(1)} %pad_maximum_fusion), channel_id=3, replica_groups=mesh['x'=4,'y_lo'=2,'z'=8,'y_hi'=4,'core'=2] {'y_hi','core'}, dimensions={0}, use_global_device_ids=true | all-gather | bytes 589824 | tf_op jit(solution)/shard_map/all_gather | solution.py:234
  156.1 0.2 convolution_add_fusion.6
  156.4 0.2 convolution_add_fusion.5
  156.6 0.2 convolution_add_fusion.4
  156.9 0.2 convolution_add_fusion.3
  157.1 0.2 convolution_add_fusion.2
  157.3 0.2 convolution_add_fusion.1
  157.6 0.9 fusion
  158.4 7.2 %reduce-scatter.2.cloned.1.call-done = bf16[128,512]{1,0:T(8,128)(2,1)} async-done(((bf16[512,512]{1,0:T(8,128)(2,1)}), bf16[128,512]{1,0:T(8,128)(2,1)}) %reduce-scatter.2.cloned.1.call-update) | async-done | bytes 131088 | tf_op jit(solution)/shard_map/reduce_scatter | solution.py:228
  (39 shorter events, 1.6 us)
Async XLA Ops:
  9.8 13.9 %copy-start.1 = (bf16[4096,128]{1,0:T(8,128)(2,1)S(1)}, bf16[4096,128]{1,0:T(8,128)(2,1)}, u32[]{:S(2)}) copy-start(bf16[4096,128]{1,0:T(8,128)(2,1)} %param.18) | copy-start | bytes 3145732
  9.8 45.5 %all-to-all-start = ((bf16[16,272,128]{2,1,0:T(8,128)(2,1)}), bf16[16,272,128]{2,1,0:T(8,128)(2,1)S(1)}, u32[]{:S(2)}, u32[]{:S(2)}) async-start(bf16[16,272,128]{2,1,0:T(8,128)(2,1)} %broadcast_in_dim.25), calls=%async_computation | async-start | bytes 2228224 | tf_op jit(solution)/shard_map/all_to_all | solution.py:201
  21.8 32.5 %all-gather.4.cloned.1.call-start = ((), (), s32[]{:S(2)}) async-start(), calls=%async_computation.4 | async-start | bytes 1351680 | tf_op jit(solution)/shard_map/all_gather | solution.py:202
  25.2 3.0 %copy-start.5 = (s32[2]{0:T(128)S(1)}, s32[2]{0:T(128)}, u32[]{:S(2)}) copy-start(s32[2]{0:T(128)} %param.17) | copy-start | bytes 28
  26.3 55.0 %collective-permute-start = (bf16[2,4,512,128]{3,2,0,1:T(8,128)(2,1)}, bf16[2,4,512,128]{3,2,0,1:T(8,128)(2,1)}, u32[]{:S(2)}, u32[]{:S(2)}) collective-permute-start(bf16[2,4,512,128]{3,2,0,1:T(8,128)(2,1)} %bitcast.90), channel_id=1, source_target_pairs={{0,1},{1,0},{2,3},{3,2},{4,5},{5,4},{6,7},{7,6},{8,9},{9,8},{10,11... | collective-permute-start | bytes 3145736 | tf_op jit(solution)/shard_map/ppermute | solution.py:208
  56.6 1.2 copy-start
  71.7 68.8 %all-to-all-start.1 = ((bf16[16,256,128]{2,1,0:T(8,128)(2,1)}), bf16[16,256,128]{2,1,0:T(8,128)(2,1)S(1)}, u32[]{:S(2)}, u32[]{:S(2)}) async-start(bf16[16,256,128]{2,1,0:T(8,128)(2,1)} %get-tuple-element.7), calls=%async_computation.2 | async-start | bytes 2097152 | tf_op jit(solution)/shard_map/all_to_all | solution.py:229
  81.1 84.6 %reduce-scatter.2.cloned.1.call-start = ((), (), s32[]{:S(2)}) async-start(), calls=%async_computation.3 | async-start | bytes 655360 | tf_op jit(solution)/shard_map/reduce_scatter | solution.py:228
  83.7 16.5 %collective-permute-start.1 = (bf16[2,2,512,128]{3,2,1,0:T(8,128)(2,1)}, bf16[2,2,512,128]{3,2,1,0:T(8,128)(2,1)S(1)}, u32[]{:S(2)}, u32[]{:S(2)}) collective-permute-start(bf16[2,2,512,128]{3,2,1,0:T(8,128)(2,1)} %get-tuple-element.12), channel_id=1, source_target_pairs={{0,2},{2,4},{4,6},{6,0},{1,3},{3,5},{5,7},{7,1},{8,10},{10,12},{12... | collective-permute-start | bytes 1572872 | tf_op jit(solution)/shard_map/ppermute | solution.py:213
  88.0 45.7 %collective-permute-start.2 = (bf16[2,2,512,128]{3,2,1,0:T(8,128)(2,1)}, bf16[2,2,512,128]{3,2,1,0:T(8,128)(2,1)S(1)}, u32[]{:S(2)}, u32[]{:S(2)}) collective-permute-start(bf16[2,2,512,128]{3,2,1,0:T(8,128)(2,1)} %get-tuple-element.13), channel_id=1, source_target_pairs={{0,4},{2,6},{4,0},{6,2},{1,5},{3,7},{5,1},{7,3},{8,12},{10,14},{12... | collective-permute-start | bytes 1572872 | tf_op jit(solution)/shard_map/ppermute | solution.py:213
  92.8 47.7 %collective-permute-start.3 = (bf16[2,2,512,128]{3,2,1,0:T(8,128)(2,1)}, bf16[2,2,512,128]{3,2,1,0:T(8,128)(2,1)S(1)}, u32[]{:S(2)}, u32[]{:S(2)}) collective-permute-start(bf16[2,2,512,128]{3,2,1,0:T(8,128)(2,1)} %get-tuple-element.10), channel_id=1, source_target_pairs={{0,6},{2,0},{4,2},{6,4},{1,7},{3,1},{5,3},{7,5},{8,14},{10,8},{12,... | collective-permute-start | bytes 1572872 | tf_op jit(solution)/shard_map/ppermute | solution.py:213
  140.7 15.7 %copy-start.3 = (bf16[128,128]{1,0:T(8,128)(2,1)}, bf16[128,128]{1,0:T(8,128)(2,1)S(1)}, u32[]{:S(2)}) copy-start(bf16[128,128]{1,0:T(8,128)(2,1)S(1)} %fusion.36) | copy-start | bytes 98308
  140.7 15.7 %copy-start.2 = (bf16[512,128]{1,0:T(8,128)(2,1)S(1)}, bf16[512,128]{1,0:T(8,128)(2,1)}, u32[]{:S(2)}) copy-start(bf16[512,128]{1,0:T(8,128)(2,1)} %get-tuple-element.27) | copy-start | bytes 393220
  140.7 15.9 %copy-start.4 = (bf16[128,128]{1,0:T(8,128)(2,1)}, bf16[128,128]{1,0:T(8,128)(2,1)S(1)}, u32[]{:S(2)}) copy-start(bf16[128,128]{1,0:T(8,128)(2,1)S(1)} %slice.167) | copy-start | bytes 98308
Sparse Core Ops, SparseCore 0:
  24.7 29.4 all-gather.3
  140.6 24.9 reduce-scatter.1

commit v2 on v1

v2 whole, which is shorter than its diff:
```python
import math

import jax
import jax.numpy as jnp
from jax import lax
from jax.experimental import pallas as pl
from jax.experimental.pallas import tpu as pltpu
from jax.sharding import Mesh, PartitionSpec as P

AXES = ("x", "y_lo", "z", "y_hi", "core")
CTX = ("x", "y_lo", "z")
KEYS = ("y_lo", "z")
KV = ("y_hi", "core")
SPAN = 64
HD = 128
HQ = 4
TOK = 2 * SPAN
QROWS = HQ * SPAN
CHUNK = 256
UNROLL = 4
PER = CHUNK // SPAN
QBLOCK = 2 * HQ * TOK + 32
KBLOCK = 2 * TOK + 16
BF = jnp.bfloat16
F32 = jnp.float32
VMEM = pl.BlockSpec(memory_space=pltpu.VMEM)
SMEM = pl.BlockSpec(memory_space=pltpu.SMEM)


def nt(a, b):
    return lax.dot_general(a, b, (((1,), (1,)), ((), ())), preferred_element_type=F32)


def nn(a, b):
    return lax.dot_general(a, b, (((1,), (0,)), ((), ())), preferred_element_type=F32)


def span_lines(span_ref, lines):
    line = lax.broadcasted_iota(jnp.int32, (lines, HD), 0)
    return jnp.where(line == 0, span_ref[0], span_ref[1]).astype(F32)


def pack_kernel(span_ref, k_ref, v_ref, out_ref):
    k, v, tag = k_ref[...], v_ref[...], span_lines(span_ref, KBLOCK - 2 * TOK).astype(BF)
    for w in range(out_ref.shape[0]):
        out_ref[w, :TOK, :] = k
        out_ref[w, TOK : 2 * TOK, :] = v
        out_ref[w, 2 * TOK :, :] = tag


def prep_kernel(span_ref, q_ref, g_ref, o_ref, lse_ref, out_ref):
    lse_rows, delta_rows = [], []
    for s in range(2):
        rows = slice(s * SPAN, (s + 1) * SPAN)
        for pair in range(HQ // 2):
            prods = []
            for h in (2 * pair, 2 * pair + 1):
                cols = slice(h * HD, (h + 1) * HD)
                at = s * QROWS + h * SPAN
                g = g_ref[rows, cols]
                out_ref[at : at + SPAN, :] = q_ref[rows, cols]
                out_ref[HQ * TOK + at : HQ * TOK + at + SPAN, :] = g
                prods.append(g.astype(F32) * o_ref[rows, cols].astype(F32))
            both = jnp.concatenate(prods, axis=0)
            delta_rows.append(jnp.sum(both.T, axis=0, keepdims=True))
            lse_rows.append(
                jnp.concatenate(
                    [lse_ref[2 * pair : 2 * pair + 1, rows], lse_ref[2 * pair + 1 : 2 * pair + 2, rows]],
                    axis=1,
                )
            )
    parts = []
    for rows in (lse_rows, delta_rows):
        rest = jnp.concatenate(rows, axis=0)
        for _ in range(3):
            piece = rest.astype(BF).astype(F32)
            rest = rest - piece
            parts.append(piece)
    parts.append(span_lines(span_ref, 8))
    out_ref[2 * HQ * TOK :, :] = jnp.concatenate(parts, axis=0).astype(BF)


def tile_kernel(n_q, n_k, table, *refs):
    q_refs, (gkv_ref,), refs = refs[:n_q], refs[n_q : n_q + 1], refs[n_q + 1 :]
    dq_refs, (dkv_ref,), refs = refs[:n_q], refs[n_q : n_q + 1], refs[n_q + 1 :]
    q_s, g_s, k_s, v_s, kt_s, dk_acc, dv_acc, dqt_acc, lse_s, del_s = refs
    spans_k, most = 2 * n_k, 2 * n_q * 2 * n_k // PER
    scale = 1.0 / math.sqrt(HD)
    log2e = 1.0 / math.log(2.0)
    boundary, n_tiles = table[2 * spans_k + 3 * most], table[2 * spans_k + 3 * most + 1]

    dk_acc[...] = jnp.zeros_like(dk_acc)
    dv_acc[...] = jnp.zeros_like(dv_acc)
    dqt_acc[...] = jnp.zeros_like(dqt_acc)
    for w in range(n_k):
        for s in range(2):
            to = pl.ds(pl.multiple_of(table[2 * w + s] * SPAN, SPAN), SPAN)
            k_s[to, :] = gkv_ref[w, s * SPAN : (s + 1) * SPAN, :]
            v_s[to, :] = gkv_ref[w, TOK + s * SPAN : TOK + (s + 1) * SPAN, :]
    for c in range(spans_k // PER):
        kt_s[c] = k_s[c * CHUNK : (c + 1) * CHUNK, :].T
    for x in range(n_q):
        q_s[x * 2 * QROWS : (x + 1) * 2 * QROWS, :] = q_refs[x][: HQ * TOK, :]
        g_s[x * 2 * QROWS : (x + 1) * 2 * QROWS, :] = q_refs[x][HQ * TOK : 2 * HQ * TOK, :]
        extra = q_refs[x][2 * HQ * TOK : 2 * HQ * TOK + 24, :].astype(F32)
        lse = (extra[0:4] + extra[4:8] + extra[8:12]) * log2e
        dlt = extra[12:16] + extra[16:20] + extra[20:24]
        for s in range(2):
            i = 2 * x + s
            lse_s[i] = jnp.broadcast_to(jnp.concatenate([lse[2 * s : 2 * s + 1], lse[2 * s + 1 : 2 * s + 2]], axis=1), (8, QROWS))
            del_s[i] = jnp.broadcast_to(jnp.concatenate([dlt[2 * s : 2 * s + 1], dlt[2 * s + 1 : 2 * s + 2]], axis=1), (8, QROWS))

    key_line = lax.broadcasted_iota(jnp.int32, (SPAN, QROWS), 0)
    row_off = lax.broadcasted_iota(jnp.int32, (1, QROWS), 1) % SPAN

    def open_tile(t):
        at = 2 * spans_k + 3 * t
        span, i, c = table[at], table[at + 1], table[at + 2]
        q_rows = pl.ds(pl.multiple_of(i * QROWS, QROWS), QROWS)
        k_rows = pl.ds(pl.multiple_of(c * CHUNK, CHUNK), CHUNK)
        score = nt(k_s[k_rows, :], q_s[q_rows, :])
        dprob = nt(v_s[k_rows, :], g_s[q_rows, :])
        lse, dlt = lse_s[i][0:1], del_s[i][0:1]
        q_pos = span * SPAN + row_off
        q_start = jnp.where(q_pos >= boundary, boundary, 0)
        probs, dscores = [], []
        for j in range(PER):
            part = slice(j * SPAN, (j + 1) * SPAN)
            base = table[spans_k + c * PER + j] * SPAN
            live = (key_line <= q_pos - base) & (key_line >= q_start - base)
            prob = jnp.where(live, jnp.exp2(score[part] * (scale * log2e) - lse), 0.0)
            probs.append(prob.astype(BF))
            dscores.append((prob * (dprob[part] - dlt)).astype(BF))
        return i, c, q_rows, k_rows, jnp.concatenate(probs, axis=0), jnp.concatenate(dscores, axis=0)

    def close_tile(i, c, q_rows, k_rows, prob_b, dscore_b):
        dv_acc[k_rows, :] += nn(prob_b, g_s[q_rows, :])
        dk_acc[k_rows, :] += nn(dscore_b, q_s[q_rows, :])
        dqt_acc[i] += nn(kt_s[c], dscore_b)

    def step(t, _):
        for u in range(0, UNROLL, 2):
            for opened in [open_tile(UNROLL * t + u), open_tile(UNROLL * t + u + 1)]:
                close_tile(*opened)
        return 0

    lax.fori_loop(0, (n_tiles + UNROLL - 1) // UNROLL, step, 0)
    for i in range(2 * n_q):
        dq = (dqt_acc[i] * scale).astype(BF).T
        for h in range(HQ):
            dq_refs[i // 2][(i % 2) * SPAN : (i % 2 + 1) * SPAN, h * HD : (h + 1) * HD] = dq[h * SPAN : (h + 1) * SPAN]
    for w in range(n_k):
        for s in range(2):
            at = pl.ds(pl.multiple_of(table[2 * w + s] * SPAN, SPAN), SPAN)
            dkv_ref[w, s * SPAN : (s + 1) * SPAN, :] = dk_acc[at, :].astype(BF)
            dkv_ref[w, TOK + s * SPAN : TOK + (s + 1) * SPAN, :] = dv_acc[at, :].astype(BF)


def tile_grads(table, q_blocks, gkv):
    n_q, n_k = len(q_blocks), gkv.shape[0]
    keys, rows = n_k * TOK, 2 * n_q * QROWS
    outs = pl.pallas_call(
        lambda *refs: tile_kernel(n_q, n_k, *refs),
        out_shape=[jax.ShapeDtypeStruct((TOK, HQ * HD), BF)] * n_q + [jax.ShapeDtypeStruct((n_k, 2 * TOK, HD), BF)],
        in_specs=[SMEM] + [VMEM] * (n_q + 1),
        out_specs=[VMEM] * (n_q + 1),
        scratch_shapes=[
            pltpu.VMEM((rows, HD), BF),
            pltpu.VMEM((rows, HD), BF),
            pltpu.VMEM((keys, HD), BF),
            pltpu.VMEM((keys, HD), BF),
            pltpu.VMEM((keys // CHUNK, HD, CHUNK), BF),
            pltpu.VMEM((keys, HD), F32),
            pltpu.VMEM((keys, HD), F32),
            pltpu.VMEM((2 * n_q, HD, QROWS), F32),
            pltpu.VMEM((2 * n_q, 8, QROWS), F32),
            pltpu.VMEM((2 * n_q, 8, QROWS), F32),
        ],
        compiler_params=pltpu.CompilerParams(vmem_limit_bytes=32 * 1024 * 1024),
        cost_estimate=pl.CostEstimate(flops=5_000_000_000, bytes_accessed=4_000_000, transcendentals=2_000_000),
        name="tile_grads",
    )(table, *q_blocks, gkv)
    return outs[:n_q], outs[n_q]


def partial_kernel(own_ref, other_ref, kept_ref, swapped_ref, out_ref):
    cols = out_ref.shape[2]
    for h in range(out_ref.shape[0]):
        rows = slice(h * cols, (h + 1) * cols)
        part = nt(own_ref[...], kept_ref[rows, :]) + nt(other_ref[...], swapped_ref[rows, :])
        out_ref[h] = part.astype(BF)


def partial_hidden(own, other, kept, swapped, n_hi):
    return pl.pallas_call(
        partial_kernel,
        out_shape=jax.ShapeDtypeStruct((n_hi, own.shape[0], kept.shape[0] // n_hi), BF),
        in_specs=[VMEM] * 4,
        out_specs=VMEM,
        compiler_params=pltpu.CompilerParams(vmem_limit_bytes=16 * 1024 * 1024),
        name="partial_hidden",
    )(own, other, kept, swapped)


def prep(span_order, queries, grad_out, fwd_out, log_norm):
    return pl.pallas_call(
        prep_kernel,
        out_shape=jax.ShapeDtypeStruct((QBLOCK, HD), BF),
        in_specs=[SMEM, VMEM, VMEM, VMEM, VMEM],
        out_specs=VMEM,
        name="prep",
    )(span_order, queries, grad_out, fwd_out, log_norm)


def pack(span_order, key_rows, value_rows, copies):
    return pl.pallas_call(
        pack_kernel,
        out_shape=jax.ShapeDtypeStruct((copies, KBLOCK, HD), BF),
        in_specs=[SMEM, VMEM, VMEM],
        out_specs=VMEM,
        name="pack",
    )(span_order, key_rows, value_rows)


def hop(block, axis, shift):
    n = lax.axis_size(axis)
    return lax.ppermute(block, axis, [(i, (i + shift) % n) for i in range(n)])


def make_table(q_span, k_span, doc_lengths):
    boundary = doc_lengths[0]
    spans_k, spans_q = k_span.shape[0], q_span.shape[0]
    rank = jnp.sum((k_span[None, :] < k_span[:, None]).astype(jnp.int32), axis=1)
    slots = jnp.arange(spans_k, dtype=jnp.int32)
    in_order = jnp.sum(jnp.where(rank[None, :] == slots[:, None], k_span[None, :], 0), axis=1)
    first = jnp.where(q_span * SPAN >= boundary, boundary // SPAN, 0)
    low = jnp.sum((k_span[None, :] < first[:, None]).astype(jnp.int32), axis=1) // PER
    high = (jnp.sum((k_span[None, :] <= q_span[:, None]).astype(jnp.int32), axis=1) + PER - 1) // PER
    count = high - low
    places = jnp.arange(spans_q, dtype=jnp.int32)
    end = jnp.sum(jnp.where(places[None, :] <= places[:, None], count[None, :], 0), axis=1)
    tiles = jnp.arange(spans_q * spans_k // PER, dtype=jnp.int32)
    place = jnp.sum((tiles[:, None] >= end[None, :]).astype(jnp.int32), axis=1)
    mine = place[:, None] == places[None, :]
    chunk = jnp.sum(jnp.where(mine, tiles[:, None] + (high - end)[None, :], 0), axis=1)
    span = jnp.sum(jnp.where(mine, q_span[None, :], 0), axis=1)
    unused = place == spans_q
    span = jnp.where(unused, -SPAN * spans_k * 1024, span)
    work = jnp.stack([span, jnp.where(unused, 0, place), chunk], axis=1).reshape(-1)
    return jnp.concatenate([rank, in_order, work, boundary[None], end[-1:]])


def body(queries, key_rows, value_rows, grad_out, fwd_out, log_norm, span_order, doc_lengths, key_proj, value_proj):
    n_q, n_k = lax.axis_size("x"), lax.axis_size(KEYS)
    n_hi = lax.axis_size("y_hi")
    scale = 1.0 / math.sqrt(HD)
    core = lax.axis_index("core")
    y_hi = lax.axis_index("y_hi")

    gkv = lax.all_to_all(pack(span_order, key_rows, value_rows, n_k), KEYS, 0, 0)
    mine = prep(span_order, queries, grad_out, fwd_out, log_norm)
    q_blocks = [mine] + [hop(mine, "x", shift) for shift in range(1, n_q)]

    cols = key_proj.shape[0] // (2 * n_hi)
    projs = jnp.concatenate([key_proj, value_proj], axis=1).reshape(n_hi, 2, cols, 2 * HD)
    kept = lax.dynamic_index_in_dim(projs, core, 1, keepdims=False).reshape(n_hi * cols, 2 * HD)
    given = lax.dynamic_index_in_dim(projs, 1 - core, 1, keepdims=False).reshape(n_hi * cols, 2 * HD)
    swapped = hop(given, "core", 1)

    tags = jnp.stack([b[2 * HQ * TOK + 24 : 2 * HQ * TOK + 26, 0] for b in q_blocks])
    q_span = tags.reshape(2 * n_q).astype(jnp.int32)
    k_span = gkv[:, 2 * TOK : 2 * TOK + 2, 0].reshape(2 * n_k).astype(jnp.int32)
    dqs, dkv = tile_grads(make_table(q_span, k_span, doc_lengths), q_blocks, gkv)

    parts = lax.all_to_all(dkv, KEYS, 0, 0)
    homes = [dqs[0]] + [hop(dqs[shift], "x", -shift) for shift in range(1, n_q)]
    parts, homes, swapped = lax.optimization_barrier((parts, homes, swapped))
    grad_query = sum(h.astype(F32) for h in homes).astype(BF)
    total = jnp.sum(parts.astype(F32), axis=0)
    grad_key = (total[:TOK] * scale).astype(BF)
    grad_value = total[TOK:].astype(BF)

    both = jnp.concatenate([grad_key, grad_value], axis=1)
    partial = partial_hidden(both, hop(both, "core", 1), kept, swapped, n_hi)
    shares = lax.all_to_all(partial, "y_hi", 0, 0)
    hidden = jnp.sum(shares.astype(F32), axis=0).astype(BF)
    return grad_query, grad_key, grad_value, hidden


def solution(mesh):
    fine = Mesh(mesh.devices.reshape(4, 2, 8, 4, 2), AXES)
    placed = (
        P(CTX, KV),
        P(CTX, KV),
        P(CTX, KV),
        P(CTX, KV),
        P(CTX, KV),
        P(KV, CTX),
        P(CTX),
        P(),
        P(None, KV),
        P(None, KV),
    )
    return jax.shard_map(
        body,
        mesh=fine,
        in_specs=placed,
        out_specs=(P(CTX, KV), P(CTX, KV), P(CTX, KV), P(CTX, KV)),
        check_vma=False,
    )
```

time: 173 us -> 117 us (0.68)
  the two profiles are of different devices: /device:TPU:8 before, /device:TPU:76 now
where the time goes in v2:
time: 117 us; the launch traced here: 116 us
  waiting for transfers between devices  49.8 us (43%)
  starting transfers between devices  44.3 us (38%)
  Pallas kernels  12.5 us (11%)
  other arithmetic  4.34 us (4%)
  local copies, waits for them, and re-layouts  4.05 us (3%)
    ppermute x8, starting transfers between devices, hop(): return lax.ppermute(block, axis, [(i, (i + shift) % n) for i in range(n)])  21.8 us
    all_to_all x1, waiting for transfers between devices, body(): shares = lax.all_to_all(partial, 'y_hi', 0, 0)  16.1 us
    ppermute x8, waiting for transfers between devices, hop(): return lax.ppermute(block, axis, [(i, (i + shift) % n) for i in range(n)])  15.6 us
    all_to_all x1, starting transfers between devices, body(): lax.all_to_all(pack(span_order, key_rows, value_rows, n_k), KEYS, 0, 0)  10.9 us
    all_to_all x1, waiting for transfers between devices, body(): parts = lax.all_to_all(dkv, KEYS, 0, 0)  10.8 us
    all_to_all x1, waiting for transfers between devices, body(): lax.all_to_all(pack(span_order, key_rows, value_rows, n_k), KEYS, 0, 0)  7.27 us
    pallas_call x1, Pallas kernels, tile_grads(): pl.pallas_call(lambda *refs: tile_kernel(n_q, n_k, *refs), out_shape=[jax...  7.08 us
    all_to_all x1, starting transfers between devices, body(): shares = lax.all_to_all(partial, 'y_hi', 0, 0)  6.2 us
  transfers between devices with their start and end apart: 11, of which 9 were waited for; matrix products, arithmetic and copies ran while one was open for 2% of the time, Pallas kernels for 2%

profile of v2, /device:TPU:76, one launch (start us, length us, event | category | flops | bytes accessed | tf_op | source)
XLA Modules:
  0.0 116.0 jit_solution(3261419484808771472)
XLA Ops:
  0.6 1.9 %pack.1 = bf16[16,272,128]{2,1,0:T(8,128)(2,1)} custom-call(s32[2]{0:T(128)} %span_ref.3, bf16[128,128]{1,0:T(8,128)(2,1)} %k_ref.1, bf16[128,128]{1,0:T(8,128)(2,1)} %v_ref.1), custom_call_target="tpu_custom_call" | custom-call | tf_op jit(solution)/shard_map/pack/pallas_call | solution.py:216
  2.6 10.9 %all-to-all-start = ((bf16[16,272,128]{2,1,0:T(8,128)(2,1)}), bf16[16,272,128]{2,1,0:T(8,128)(2,1)S(1)}, u32[]{:S(2)}, u32[]{:S(2)}) async-start(bf16[16,272,128]{2,1,0:T(8,128)(2,1)} %pack.1), calls=%async_computation | async-start | bytes 2228224 | tf_op jit(solution)/shard_map/all_to_all | solution.py:260
  13.5 1.9 %prep.1.refs_1_ = bf16[1056,128]{1,0:T(8,128)(2,1)} custom-call(s32[2]{0:T(128)} %span_ref.3, bf16[128,512]{1,0:T(8,128)(2,1)} %q_ref.1, bf16[128,512]{1,0:T(8,128)(2,1)} %g_ref.1, bf16[128,512]{1,0:T(8,128)(2,1)} %o_ref.1, f32[4,128]{1,0:T(4,128)} %lse_ref.1), custom_call_target="tpu_custom_call" | custom-call | tf_op jit(solution)/shard_map/prep/pallas_call | solution.py:206
  15.4 2.4 %collective-permute-start.2 = (bf16[1056,128]{1,0:T(8,128)(2,1)}, bf16[1056,128]{1,0:T(8,128)(2,1)S(1)}, u32[]{:S(2)}, u32[]{:S(2)}) collective-permute-start(bf16[1056,128]{1,0:T(8,128)(2,1)} %prep.1.refs_1_), channel_id=1, source_target_pairs={{0,384},{128,0},{256,128},{384,256},{1,385},{129,1},{257,129},{385... | collective-permute-start | bytes 811016 | tf_op jit(solution)/shard_map/ppermute | solution.py:227
  17.8 4.6 %collective-permute-start.1 = (bf16[1056,128]{1,0:T(8,128)(2,1)}, bf16[1056,128]{1,0:T(8,128)(2,1)S(1)}, u32[]{:S(2)}, u32[]{:S(2)}) collective-permute-start(bf16[1056,128]{1,0:T(8,128)(2,1)} %prep.1.refs_1_), channel_id=1, source_target_pairs={{0,256},{128,384},{256,0},{384,128},{1,257},{129,385},{257,1},{385... | collective-permute-start | bytes 811016 | tf_op jit(solution)/shard_map/ppermute | solution.py:227
  22.5 1.9 %collective-permute-start = (bf16[1056,128]{1,0:T(8,128)(2,1)}, bf16[1056,128]{1,0:T(8,128)(2,1)S(1)}, u32[]{:S(2)}, u32[]{:S(2)}) collective-permute-start(bf16[1056,128]{1,0:T(8,128)(2,1)} %prep.1.refs_1_), channel_id=1, source_target_pairs={{0,128},{128,256},{256,384},{384,0},{1,129},{129,257},{257,385},{3... | collective-permute-start | bytes 811016 | tf_op jit(solution)/shard_map/ppermute | solution.py:227
  24.4 0.8 slice_reduce_fusion.3
  25.4 1.5 %collective-permute-done.2.refs_4_ = bf16[1056,128]{1,0:T(8,128)(2,1)S(1)} collective-permute-done((bf16[1056,128]{1,0:T(8,128)(2,1)}, bf16[1056,128]{1,0:T(8,128)(2,1)S(1)}, u32[]{:S(2)}, u32[]{:S(2)}) %collective-permute-start.2) | collective-permute-done | bytes 270368 | tf_op jit(solution)/shard_map/ppermute | solution.py:227
  27.0 3.8 %collective-permute-done.1.refs_3_ = bf16[1056,128]{1,0:T(8,128)(2,1)S(1)} collective-permute-done((bf16[1056,128]{1,0:T(8,128)(2,1)}, bf16[1056,128]{1,0:T(8,128)(2,1)S(1)}, u32[]{:S(2)}, u32[]{:S(2)}) %collective-permute-start.1) | collective-permute-done | bytes 270368 | tf_op jit(solution)/shard_map/ppermute | solution.py:227
  31.0 3.6 %collective-permute-done.refs_2_ = bf16[1056,128]{1,0:T(8,128)(2,1)S(1)} collective-permute-done((bf16[1056,128]{1,0:T(8,128)(2,1)}, bf16[1056,128]{1,0:T(8,128)(2,1)S(1)}, u32[]{:S(2)}, u32[]{:S(2)}) %collective-permute-start) | collective-permute-done | bytes 270368 | tf_op jit(solution)/shard_map/ppermute | solution.py:227
  34.9 7.3 %all-to-all-done.refs_5_ = bf16[16,272,128]{2,1,0:T(8,128)(2,1)S(1)} async-done(((bf16[16,272,128]{2,1,0:T(8,128)(2,1)}), bf16[16,272,128]{2,1,0:T(8,128)(2,1)S(1)}, u32[]{:S(2)}, u32[]{:S(2)}) %all-to-all-start) | async-done | bytes 1114144 | tf_op jit(solution)/shard_map/all_to_all | solution.py:260
  42.1 0.3 convert_reduce_fusion.1
  43.1 0.6 slice.34
  44.3 0.8 concatenate.9.refs_0_
  45.0 1.0 copy-done
  46.0 7.1 %tile_grads.1 = (bf16[128,512]{1,0:T(8,128)(2,1)S(1)}, bf16[128,512]{1,0:T(8,128)(2,1)S(1)}, bf16[128,512]{1,0:T(8,128)(2,1)S(1)}, bf16[128,512]{1,0:T(8,128)(2,1)S(1)}, bf16[16,256,128]{2,1,0:T(8,128)(2,1)}) custom-call(s32[258]{0:T(512)S(1)} %concatenate.9.refs_0_, bf16[1056,128]{1,0:T(8,128)(2,1)S(1)} %copy-done, ...), custom_call_target="tpu_custom_call" | custom-call | flops 5000000000 | bytes 4000000 | tf_op jit(solution)/shard_map/tile_grads/pallas_call | solution.py:162
  53.1 5.4 %all-to-all-start.1 = ((bf16[16,256,128]{2,1,0:T(8,128)(2,1)}), bf16[16,256,128]{2,1,0:T(8,128)(2,1)}, u32[]{:S(2)}, u32[]{:S(2)}) async-start(bf16[16,256,128]{2,1,0:T(8,128)(2,1)} %get-tuple-element.15), calls=%async_computation.1 | async-start | bytes 2097152 | tf_op jit(solution)/shard_map/all_to_all | solution.py:275
  58.8 1.9 %collective-permute-start.6 = (bf16[2048,256]{1,0:T(8,128)(2,1)S(1)}, bf16[2048,256]{1,0:T(8,128)(2,1)S(1)}, u32[]{:S(2)}, u32[]{:S(2)}) collective-permute-start(bf16[2048,256]{1,0:T(8,128)(2,1)S(1)} %bitcast.21), channel_id=1, source_target_pairs={{0,1},{1,0},{2,3},{3,2},{4,5},{5,4},{6,7},{7,6},{8,9},{9,8},{10,11... | collective-permute-start | bytes 3145736 | tf_op jit(solution)/shard_map/ppermute | solution.py:227
  60.7 2.4 %collective-permute-start.3 = (bf16[128,512]{1,0:T(8,128)(2,1)S(1)}, bf16[128,512]{1,0:T(8,128)(2,1)S(1)}, u32[]{:S(2)}, u32[]{:S(2)}) collective-permute-start(bf16[128,512]{1,0:T(8,128)(2,1)S(1)} %get-tuple-element.17), channel_id=1, source_target_pairs={{0,384},{128,0},{256,128},{384,256},{1,385},{129,1},{257,129},{385... | collective-permute-start | bytes 393224 | tf_op jit(solution)/shard_map/ppermute | solution.py:227
  63.2 4.6 %collective-permute-start.4 = (bf16[128,512]{1,0:T(8,128)(2,1)S(1)}, bf16[128,512]{1,0:T(8,128)(2,1)S(1)}, u32[]{:S(2)}, u32[]{:S(2)}) collective-permute-start(bf16[128,512]{1,0:T(8,128)(2,1)S(1)} %get-tuple-element.18), channel_id=1, source_target_pairs={{0,256},{128,384},{256,0},{384,128},{1,257},{129,385},{257,1},{385... | collective-permute-start | bytes 393224 | tf_op jit(solution)/shard_map/ppermute | solution.py:227
  67.8 1.9 %collective-permute-start.5 = (bf16[128,512]{1,0:T(8,128)(2,1)S(1)}, bf16[128,512]{1,0:T(8,128)(2,1)S(1)}, u32[]{:S(2)}, u32[]{:S(2)}) collective-permute-start(bf16[128,512]{1,0:T(8,128)(2,1)S(1)} %get-tuple-element.19), channel_id=1, source_target_pairs={{0,128},{128,256},{256,384},{384,0},{1,129},{129,257},{257,385},{3... | collective-permute-start | bytes 393224 | tf_op jit(solution)/shard_map/ppermute | solution.py:227
  69.8 2.6 %collective-permute-done.4 = bf16[128,512]{1,0:T(8,128)(2,1)S(1)} collective-permute-done((bf16[128,512]{1,0:T(8,128)(2,1)S(1)}, bf16[128,512]{1,0:T(8,128)(2,1)S(1)}, u32[]{:S(2)}, u32[]{:S(2)}) %collective-permute-start.4) | collective-permute-done | bytes 131104 | tf_op jit(solution)/shard_map/ppermute | solution.py:227
  72.4 2.7 %collective-permute-done.5 = bf16[128,512]{1,0:T(8,128)(2,1)S(1)} collective-permute-done((bf16[128,512]{1,0:T(8,128)(2,1)S(1)}, bf16[128,512]{1,0:T(8,128)(2,1)S(1)}, u32[]{:S(2)}, u32[]{:S(2)}) %collective-permute-start.5) | collective-permute-done | bytes 131104 | tf_op jit(solution)/shard_map/ppermute | solution.py:227
  75.2 10.8 %all-to-all-done.1 = bf16[16,256,128]{2,1,0:T(8,128)(2,1)} async-done(((bf16[16,256,128]{2,1,0:T(8,128)(2,1)}), bf16[16,256,128]{2,1,0:T(8,128)(2,1)}, u32[]{:S(2)}, u32[]{:S(2)}) %all-to-all-start.1) | async-done | bytes 1048608 | tf_op jit(solution)/shard_map/all_to_all | solution.py:275
  86.0 1.4 %convert_reduce_fusion = f32[256,128]{1,0:T(8,128)S(1)} fusion(bf16[16,256,128]{2,1,0:T(8,128)(2,1)} %all-to-all-done.1), kind=kLoop, calls=%fused_computation.1 | loop fusion | flops 1015808 | bytes 1179648 | tf_op jit(solution)/shard_map/reduce_sum | solution.py:279
  87.4 1.9 %collective-permute-start.7 = (bf16[128,256]{1,0:T(8,128)(2,1)S(1)}, bf16[128,256]{1,0:T(8,128)(2,1)S(1)}, u32[]{:S(2)}, u32[]{:S(2)}) collective-permute-start(bf16[128,256]{1,0:T(8,128)(2,1)S(1)} %pad_maximum_fusion.1.own_ref), channel_id=1, source_target_pairs={{0,1},{1,0},{2,3},{3,2},{4,5},{5,4},{6,7},{7,6},{8,9},{9,8},{10,11... | collective-permute-start | bytes 196616 | tf_op jit(solution)/shard_map/ppermute | solution.py:227
  89.3 1.2 %collective-permute-done.7.other_ref = bf16[128,256]{1,0:T(8,128)(2,1)S(1)} collective-permute-done((bf16[128,256]{1,0:T(8,128)(2,1)S(1)}, bf16[128,256]{1,0:T(8,128)(2,1)S(1)}, u32[]{:S(2)}, u32[]{:S(2)}) %collective-permute-start.7) | collective-permute-done | bytes 65568 | tf_op jit(solution)/shard_map/ppermute | solution.py:227
  90.6 1.6 %partial_hidden.1 = bf16[4,128,512]{2,1,0:T(8,128)(2,1)} custom-call(bf16[128,256]{1,0:T(8,128)(2,1)S(1)} %pad_maximum_fusion.1.own_ref, bf16[128,256]{1,0:T(8,128)(2,1)S(1)} %collective-permute-done.7.other_ref, bf16[2048,256]{1,0:T(8,128)(2,1)S(1)} %bitcast.19, bf16[2048,256]{1,0:T(8,128)(2,1)S(1)} %collective-permute-done.6.swapped_ref), custom_call_target="tpu_custom_call" | custom-call | tf_op jit(solution)/shard_map/partial_hidden/pallas_call | solution.py:195
  92.2 6.2 %all-to-all-start.2 = ((bf16[4,128,512]{2,1,0:T(8,128)(2,1)}), bf16[4,128,512]{2,1,0:T(8,128)(2,1)S(1)}, u32[]{:S(2)}, u32[]{:S(2)}) async-start(bf16[4,128,512]{2,1,0:T(8,128)(2,1)} %partial_hidden.1), calls=%async_computation.2 | async-start | bytes 1048576 | tf_op jit(solution)/shard_map/all_to_all | solution.py:285
  98.4 0.7 add_convert_fusion
  99.1 16.1 %all-to-all-done.2 = bf16[4,128,512]{2,1,0:T(8,128)(2,1)S(1)} async-done(((bf16[4,128,512]{2,1,0:T(8,128)(2,1)}), bf16[4,128,512]{2,1,0:T(8,128)(2,1)S(1)}, u32[]{:S(2)}, u32[]{:S(2)}) %all-to-all-start.2) | async-done | bytes 524320 | tf_op jit(solution)/shard_map/all_to_all | solution.py:285
  115.2 0.7 reduce_sum.108
  (41 shorter events, 2.1 us)
Async XLA Ops:
  0.6 24.6 %copy-start.7 = (s32[2]{0:T(128)S(1)}, s32[2]{0:T(128)}, u32[]{:S(2)}) copy-start(s32[2]{0:T(128)} %param.17) | copy-start | bytes 28
  2.6 39.6 %all-to-all-start = ((bf16[16,272,128]{2,1,0:T(8,128)(2,1)}), bf16[16,272,128]{2,1,0:T(8,128)(2,1)S(1)}, u32[]{:S(2)}, u32[]{:S(2)}) async-start(bf16[16,272,128]{2,1,0:T(8,128)(2,1)} %pack.1), calls=%async_computation | async-start | bytes 2228224 | tf_op jit(solution)/shard_map/all_to_all | solution.py:260
  15.4 11.5 %collective-permute-start.2 = (bf16[1056,128]{1,0:T(8,128)(2,1)}, bf16[1056,128]{1,0:T(8,128)(2,1)S(1)}, u32[]{:S(2)}, u32[]{:S(2)}) collective-permute-start(bf16[1056,128]{1,0:T(8,128)(2,1)} %prep.1.refs_1_), channel_id=1, source_target_pairs={{0,384},{128,0},{256,128},{384,256},{1,385},{129,1},{257,129},{385... | collective-permute-start | bytes 811016 | tf_op jit(solution)/shard_map/ppermute | solution.py:227
  17.8 13.0 %collective-permute-start.1 = (bf16[1056,128]{1,0:T(8,128)(2,1)}, bf16[1056,128]{1,0:T(8,128)(2,1)S(1)}, u32[]{:S(2)}, u32[]{:S(2)}) collective-permute-start(bf16[1056,128]{1,0:T(8,128)(2,1)} %prep.1.refs_1_), channel_id=1, source_target_pairs={{0,256},{128,384},{256,0},{384,128},{1,257},{129,385},{257,1},{385... | collective-permute-start | bytes 811016 | tf_op jit(solution)/shard_map/ppermute | solution.py:227
  22.5 12.1 %collective-permute-start = (bf16[1056,128]{1,0:T(8,128)(2,1)}, bf16[1056,128]{1,0:T(8,128)(2,1)S(1)}, u32[]{:S(2)}, u32[]{:S(2)}) collective-permute-start(bf16[1056,128]{1,0:T(8,128)(2,1)} %prep.1.refs_1_), channel_id=1, source_target_pairs={{0,128},{128,256},{256,384},{384,0},{1,129},{129,257},{257,385},{3... | collective-permute-start | bytes 811016 | tf_op jit(solution)/shard_map/ppermute | solution.py:227
  45.0 1.0 copy-start
  53.1 5.4 %copy-start.1 = (bf16[4096,128]{1,0:T(8,128)(2,1)S(1)}, bf16[4096,128]{1,0:T(8,128)(2,1)}, u32[]{:S(2)}) copy-start(bf16[4096,128]{1,0:T(8,128)(2,1)} %param.19) | copy-start | bytes 3145732
  53.1 5.4 %copy-start.2 = (bf16[4096,128]{1,0:T(8,128)(2,1)S(1)}, bf16[4096,128]{1,0:T(8,128)(2,1)}, u32[]{:S(2)}) copy-start(bf16[4096,128]{1,0:T(8,128)(2,1)} %param.18) | copy-start | bytes 3145732
  53.1 32.9 %all-to-all-start.1 = ((bf16[16,256,128]{2,1,0:T(8,128)(2,1)}), bf16[16,256,128]{2,1,0:T(8,128)(2,1)}, u32[]{:S(2)}, u32[]{:S(2)}) async-start(bf16[16,256,128]{2,1,0:T(8,128)(2,1)} %get-tuple-element.15), calls=%async_computation.1 | async-start | bytes 2097152 | tf_op jit(solution)/shard_map/all_to_all | solution.py:275
  58.8 11.0 %collective-permute-start.6 = (bf16[2048,256]{1,0:T(8,128)(2,1)S(1)}, bf16[2048,256]{1,0:T(8,128)(2,1)S(1)}, u32[]{:S(2)}, u32[]{:S(2)}) collective-permute-start(bf16[2048,256]{1,0:T(8,128)(2,1)S(1)} %bitcast.21), channel_id=1, source_target_pairs={{0,1},{1,0},{2,3},{3,2},{4,5},{5,4},{6,7},{7,6},{8,9},{9,8},{10,11... | collective-permute-start | bytes 3145736 | tf_op jit(solution)/shard_map/ppermute | solution.py:227
  60.7 9.0 %collective-permute-start.3 = (bf16[128,512]{1,0:T(8,128)(2,1)S(1)}, bf16[128,512]{1,0:T(8,128)(2,1)S(1)}, u32[]{:S(2)}, u32[]{:S(2)}) collective-permute-start(bf16[128,512]{1,0:T(8,128)(2,1)S(1)} %get-tuple-element.17), channel_id=1, source_target_pairs={{0,384},{128,0},{256,128},{384,256},{1,385},{129,1},{257,129},{385... | collective-permute-start | bytes 393224 | tf_op jit(solution)/shard_map/ppermute | solution.py:227
  63.2 9.2 %collective-permute-start.4 = (bf16[128,512]{1,0:T(8,128)(2,1)S(1)}, bf16[128,512]{1,0:T(8,128)(2,1)S(1)}, u32[]{:S(2)}, u32[]{:S(2)}) collective-permute-start(bf16[128,512]{1,0:T(8,128)(2,1)S(1)} %get-tuple-element.18), channel_id=1, source_target_pairs={{0,256},{128,384},{256,0},{384,128},{1,257},{129,385},{257,1},{385... | collective-permute-start | bytes 393224 | tf_op jit(solution)/shard_map/ppermute | solution.py:227
  67.8 7.3 %collective-permute-start.5 = (bf16[128,512]{1,0:T(8,128)(2,1)S(1)}, bf16[128,512]{1,0:T(8,128)(2,1)S(1)}, u32[]{:S(2)}, u32[]{:S(2)}) collective-permute-start(bf16[128,512]{1,0:T(8,128)(2,1)S(1)} %get-tuple-element.19), channel_id=1, source_target_pairs={{0,128},{128,256},{256,384},{384,0},{1,129},{129,257},{257,385},{3... | collective-permute-start | bytes 393224 | tf_op jit(solution)/shard_map/ppermute | solution.py:227
  75.2 15.4 %copy-start.3 = (bf16[128,512]{1,0:T(8,128)(2,1)}, bf16[128,512]{1,0:T(8,128)(2,1)S(1)}, u32[]{:S(2)}) copy-start(bf16[128,512]{1,0:T(8,128)(2,1)S(1)} %collective-permute-done.5) | copy-start | bytes 393220
  87.4 11.8 %copy-start.6 = (bf16[128,128]{1,0:T(8,128)(2,1)}, bf16[128,128]{1,0:T(8,128)(2,1)S(1)}, u32[]{:S(2)}) copy-start(bf16[128,128]{1,0:T(8,128)(2,1)S(1)} %slice.53) | copy-start | bytes 98308
  87.4 11.7 %copy-start.5 = (bf16[128,128]{1,0:T(8,128)(2,1)}, bf16[128,128]{1,0:T(8,128)(2,1)S(1)}, u32[]{:S(2)}) copy-start(bf16[128,128]{1,0:T(8,128)(2,1)S(1)} %fusion) | copy-start | bytes 98308
  87.4 3.1 %collective-permute-start.7 = (bf16[128,256]{1,0:T(8,128)(2,1)S(1)}, bf16[128,256]{1,0:T(8,128)(2,1)S(1)}, u32[]{:S(2)}, u32[]{:S(2)}) collective-permute-start(bf16[128,256]{1,0:T(8,128)(2,1)S(1)} %pad_maximum_fusion.1.own_ref), channel_id=1, source_target_pairs={{0,1},{1,0},{2,3},{3,2},{4,5},{5,4},{6,7},{7,6},{8,9},{9,8},{10,11... | collective-permute-start | bytes 196616 | tf_op jit(solution)/shard_map/ppermute | solution.py:227
  90.6 7.8 %copy-start.4 = (bf16[128,512]{1,0:T(8,128)(2,1)S(1)}, bf16[128,512]{1,0:T(8,128)(2,1)}, u32[]{:S(2)}) copy-start(bf16[128,512]{1,0:T(8,128)(2,1)} %copy-done.3) | copy-start | bytes 393220
  92.2 23.0 %all-to-all-start.2 = ((bf16[4,128,512]{2,1,0:T(8,128)(2,1)}), bf16[4,128,512]{2,1,0:T(8,128)(2,1)S(1)}, u32[]{:S(2)}, u32[]{:S(2)}) async-start(bf16[4,128,512]{2,1,0:T(8,128)(2,1)} %partial_hidden.1), calls=%async_computation.2 | async-start | bytes 1048576 | tf_op jit(solution)/shard_map/all_to_all | solution.py:285

commit v3 on v2

v3 whole, which is shorter than its diff:
```python
import math

import jax
import jax.numpy as jnp
from jax import lax
from jax.experimental import pallas as pl
from jax.experimental.pallas import tpu as pltpu
from jax.sharding import Mesh, PartitionSpec as P

AXES = ("x", "y_lo", "z", "y_hi", "core")
CTX = ("x", "y_lo", "z")
KEYS = ("y_lo", "z")
KV = ("y_hi", "core")
SPAN = 64
HD = 128
HQ = 4
TOK = 2 * SPAN
QROWS = HQ * SPAN
CHUNK = 256
UNROLL = 4
PER = CHUNK // SPAN
QBLOCK = 2 * HQ * TOK + 32
KBLOCK = 2 * TOK + 16
BF = jnp.bfloat16
F32 = jnp.float32
VMEM = pl.BlockSpec(memory_space=pltpu.VMEM)
SMEM = pl.BlockSpec(memory_space=pltpu.SMEM)


def nt(a, b):
    return lax.dot_general(a, b, (((1,), (1,)), ((), ())), preferred_element_type=F32)


def nn(a, b):
    return lax.dot_general(a, b, (((1,), (0,)), ((), ())), preferred_element_type=F32)


def span_lines(span_ref, lines):
    line = lax.broadcasted_iota(jnp.int32, (lines, HD), 0)
    return jnp.where(line & 1 == 0, span_ref[0], span_ref[1]).astype(F32)


def pack_kernel(span_ref, k_ref, v_ref, out_ref, block, sem):
    block[:TOK, :] = k_ref[...]
    block[TOK : 2 * TOK, :] = v_ref[...]
    block[2 * TOK :, :] = span_lines(span_ref, KBLOCK - 2 * TOK).astype(BF)
    copies = [pltpu.make_async_copy(block, out_ref.at[w], sem.at[w]) for w in range(out_ref.shape[0])]
    for copy in copies:
        copy.start()
    for copy in copies:
        copy.wait()


def prep_kernel(span_ref, q_ref, g_ref, o_ref, lse_ref, out_ref, kept_ref):
    lse_rows, delta_rows = [], []
    for s in range(2):
        rows = slice(s * SPAN, (s + 1) * SPAN)
        for pair in range(HQ // 2):
            prods = []
            for h in (2 * pair, 2 * pair + 1):
                cols = slice(h * HD, (h + 1) * HD)
                at = s * QROWS + h * SPAN
                g = g_ref[rows, cols]
                out_ref[at : at + SPAN, :] = q_ref[rows, cols]
                out_ref[HQ * TOK + at : HQ * TOK + at + SPAN, :] = g
                prods.append(g.astype(F32) * o_ref[rows, cols].astype(F32))
            both = jnp.concatenate(prods, axis=0)
            delta_rows.append(jnp.sum(both.T, axis=0, keepdims=True))
            lse_rows.append(
                jnp.concatenate(
                    [lse_ref[2 * pair : 2 * pair + 1, rows], lse_ref[2 * pair + 1 : 2 * pair + 2, rows]],
                    axis=1,
                )
            )
    parts = []
    for rows in (lse_rows, delta_rows):
        rest = jnp.concatenate(rows, axis=0)
        for _ in range(3):
            piece = rest.astype(BF).astype(F32)
            rest = rest - piece
            parts.append(piece)
    parts.append(span_lines(span_ref, 8))
    out_ref[2 * HQ * TOK :, :] = jnp.concatenate(parts, axis=0).astype(BF)
    kept_ref[...] = jnp.concatenate(parts[:6], axis=0)


def plan_tiles(span_ref, other_blocks, gkv_ref, boundary):
    spans_q, spans_k = 2 * len(other_blocks) + 2, 2 * gkv_ref.shape[0]
    lines = max(spans_q, spans_k, 16)
    sub = lax.broadcasted_iota(jnp.int32, (lines, HD), 0)
    lane = lax.broadcasted_iota(jnp.int32, (lines, HD), 1)

    def column(tags):
        out = jnp.full((lines, HD), -1.0, F32)
        for b, tag in enumerate(tags):
            tag = tag.astype(F32)
            out = jnp.where(sub >> 1 == b, jnp.concatenate([tag] * (lines // tag.shape[0]), axis=0), out)
        return out.astype(jnp.int32)

    def total(rows):
        return jnp.sum(rows, axis=0, keepdims=True)

    k = column([gkv_ref[w, 2 * TOK : 2 * TOK + 16, :] for w in range(spans_k // 2)])
    q = column([span_lines(span_ref, 8)] + [block[2 * HQ * TOK + 16 : 2 * HQ * TOK + 32, :][8:] for block in other_blocks])
    first = jnp.where(q * SPAN >= boundary, boundary >> 6, 0)
    zero = jnp.zeros((lines, HD), jnp.int32)
    rank, below, upto = zero, zero, zero
    for j in range(spans_k):
        one = k[j : j + 1]
        rank = rank + (one < k).astype(jnp.int32)
        below = below + (one < first).astype(jnp.int32)
        upto = upto + (one <= q).astype(jnp.int32)
    real_k = sub < spans_k
    rank_line = total(jnp.where((lane == sub) & real_k, rank, 0))
    in_order = total(jnp.where((lane == rank) & real_k, k, 0))
    shift = PER.bit_length() - 1
    low, high = below >> shift, (upto + PER - 1) >> shift
    count = jnp.where(sub < spans_q, high - low, 0)
    end = zero
    for i in range(spans_q):
        end = end + jnp.where(sub >= i, count[i : i + 1], 0)
    place = total(jnp.where((lane >= end) & (sub < spans_q), 1, 0))
    mine = sub == place
    chunk = lane[:1] + total(jnp.where(mine, high - end, 0))
    span = total(jnp.where(mine, q, 0))
    unused = place >= spans_q
    span = jnp.where(unused, -(1 << 20), span)
    chunk = jnp.where(unused, 0, chunk)
    place = jnp.where(unused, 0, place)
    n_tiles = end[spans_q - 1 : spans_q]
    return jnp.concatenate([rank_line, in_order, span, place, chunk, n_tiles, n_tiles, n_tiles], axis=0)


def tile_kernel(n_q, n_x, n_k, doc_ref, span_ref, *refs):
    (own_q, own_g, own_rows), other_blocks, gkv_ref, refs = refs[:3], refs[3 : n_q + 2], refs[n_q + 2], refs[n_q + 3 :]
    dq_refs, dkv_out, refs = refs[:n_x], refs[n_x], refs[n_x + 1 :]
    dkv_ref, plan_v, plan_s, sems, q_s, g_s, k_s, v_s, kt_s, dk_acc, dv_acc, dqt_acc, lse_s, del_s = refs
    spans_k = 2 * n_k
    scale = 1.0 / math.sqrt(HD)
    log2e = 1.0 / math.log(2.0)
    boundary = doc_ref[0]

    plan_v[...] = plan_tiles(span_ref, other_blocks, gkv_ref, boundary)
    tell = pltpu.make_async_copy(plan_v, plan_s, sems.at[0])
    tell.start()
    dk_acc[...] = jnp.zeros_like(dk_acc)
    dv_acc[...] = jnp.zeros_like(dv_acc)
    dqt_acc[...] = jnp.zeros_like(dqt_acc)
    for s in range(2):
        for h in range(HQ):
            at = s * QROWS + h * SPAN
            rows, cols = slice(s * SPAN, (s + 1) * SPAN), slice(h * HD, (h + 1) * HD)
            q_s[at : at + SPAN, :] = own_q[rows, cols]
            g_s[at : at + SPAN, :] = own_g[rows, cols]
    for b in range(n_q):
        if b == 0:
            extra = own_rows[...]
        else:
            block = other_blocks[b - 1]
            q_s[b * 2 * QROWS : (b + 1) * 2 * QROWS, :] = block[: HQ * TOK, :]
            g_s[b * 2 * QROWS : (b + 1) * 2 * QROWS, :] = block[HQ * TOK : 2 * HQ * TOK, :]
            extra = block[2 * HQ * TOK : 2 * HQ * TOK + 24, :].astype(F32)
        lse = (extra[0:4] + extra[4:8] + extra[8:12]) * log2e
        dlt = extra[12:16] + extra[16:20] + extra[20:24]
        for s in range(2):
            i = 2 * b + s
            lse_s[i] = jnp.broadcast_to(jnp.concatenate([lse[2 * s : 2 * s + 1], lse[2 * s + 1 : 2 * s + 2]], axis=1), (8, QROWS))
            del_s[i] = jnp.broadcast_to(jnp.concatenate([dlt[2 * s : 2 * s + 1], dlt[2 * s + 1 : 2 * s + 2]], axis=1), (8, QROWS))
    tell.wait()
    n_tiles = plan_s[5, 0]
    for w in range(n_k):
        for s in range(2):
            to = pl.ds(pl.multiple_of(plan_s[0, 2 * w + s] * SPAN, SPAN), SPAN)
            k_s[to, :] = gkv_ref[w, s * SPAN : (s + 1) * SPAN, :]
            v_s[to, :] = gkv_ref[w, TOK + s * SPAN : TOK + (s + 1) * SPAN, :]
    for c in range(spans_k // PER):
        kt_s[c] = k_s[c * CHUNK : (c + 1) * CHUNK, :].T

    key_line = lax.broadcasted_iota(jnp.int32, (SPAN, QROWS), 0)
    row_off = lax.broadcasted_iota(jnp.int32, (1, QROWS), 1) % SPAN

    def open_tile(t):
        span, i, c = plan_s[2, t], plan_s[3, t], plan_s[4, t]
        q_rows = pl.ds(pl.multiple_of(i * QROWS, QROWS), QROWS)
        k_rows = pl.ds(pl.multiple_of(c * CHUNK, CHUNK), CHUNK)
        score = nt(k_s[k_rows, :], q_s[q_rows, :])
        dprob = nt(v_s[k_rows, :], g_s[q_rows, :])
        lse, dlt = lse_s[i][0:1], del_s[i][0:1]
        q_pos = span * SPAN + row_off
        q_start = jnp.where(q_pos >= boundary, boundary, 0)
        probs, dscores = [], []
        for j in range(PER):
            part = slice(j * SPAN, (j + 1) * SPAN)
            base = plan_s[1, c * PER + j] * SPAN
            live = (key_line <= q_pos - base) & (key_line >= q_start - base)
            prob = jnp.where(live, jnp.exp2(score[part] * (scale * log2e) - lse), 0.0)
            probs.append(prob.astype(BF))
            dscores.append((prob * (dprob[part] - dlt)).astype(BF))
        return i, c, q_rows, k_rows, jnp.concatenate(probs, axis=0), jnp.concatenate(dscores, axis=0)

    def close_tile(i, c, q_rows, k_rows, prob_b, dscore_b):
        dv_acc[k_rows, :] += nn(prob_b, g_s[q_rows, :])
        dk_acc[k_rows, :] += nn(dscore_b, q_s[q_rows, :])
        dqt_acc[i] += nn(kt_s[c], dscore_b)

    def step(t, _):
        for u in range(0, UNROLL, 2):
            for opened in [open_tile(UNROLL * t + u), open_tile(UNROLL * t + u + 1)]:
                close_tile(*opened)
        return 0

    lax.fori_loop(0, (n_tiles + UNROLL - 1) // UNROLL, step, 0)
    sends = []
    for w in range(n_k):
        for s in range(2):
            at = pl.ds(pl.multiple_of(plan_s[0, 2 * w + s] * SPAN, SPAN), SPAN)
            dkv_ref[w, s * SPAN : (s + 1) * SPAN, :] = dk_acc[at, :].astype(BF)
            dkv_ref[w, TOK + s * SPAN : TOK + (s + 1) * SPAN, :] = dv_acc[at, :].astype(BF)
        if w % 4 == 3:
            some = pl.ds(w - 3, 4)
            sends.append(pltpu.make_async_copy(dkv_ref.at[some], dkv_out.at[some], sems.at[1 + w // 4]))
            sends[-1].start()
    for i in range(2 * n_q):
        dq = (dqt_acc[i] * scale).astype(BF).T
        place, s = i // 2, i % 2
        at = place // n_x * TOK + s * SPAN
        for h in range(HQ):
            dq_refs[place % n_x][at : at + SPAN, h * HD : (h + 1) * HD] = dq[h * SPAN : (h + 1) * SPAN]
    for send in sends:
        send.wait()


def tile_grads(doc_lengths, span_order, own, q_blocks, gkv, n_x):
    n_q, n_k = len(q_blocks) + 1, gkv.shape[0]
    keys, rows = n_k * TOK, 2 * n_q * QROWS
    outs = pl.pallas_call(
        lambda *refs: tile_kernel(n_q, n_x, n_k, *refs),
        out_shape=[jax.ShapeDtypeStruct((n_q // n_x * TOK, HQ * HD), BF)] * n_x + [jax.ShapeDtypeStruct((n_k, 2 * TOK, HD), BF)],
        in_specs=[SMEM, SMEM] + [VMEM] * (n_q + 3),
        out_specs=[VMEM] * n_x + [pl.BlockSpec(memory_space=pl.ANY)],
        scratch_shapes=[
            pltpu.VMEM((n_k, 2 * TOK, HD), BF),
            pltpu.VMEM((8, HD), jnp.int32),
            pltpu.SMEM((8, HD), jnp.int32),
            pltpu.SemaphoreType.DMA((1 + n_k // 4,)),
            pltpu.VMEM((rows, HD), BF),
            pltpu.VMEM((rows, HD), BF),
            pltpu.VMEM((keys, HD), BF),
            pltpu.VMEM((keys, HD), BF),
            pltpu.VMEM((keys // CHUNK, HD, CHUNK), BF),
            pltpu.VMEM((keys, HD), F32),
            pltpu.VMEM((keys, HD), F32),
            pltpu.VMEM((2 * n_q, HD, QROWS), F32),
            pltpu.VMEM((2 * n_q, 8, QROWS), F32),
            pltpu.VMEM((2 * n_q, 8, QROWS), F32),
        ],
        compiler_params=pltpu.CompilerParams(vmem_limit_bytes=32 * 1024 * 1024),
        cost_estimate=pl.CostEstimate(flops=5_000_000_000, bytes_accessed=4_000_000, transcendentals=2_000_000),
        name="tile_grads",
    )(doc_lengths, span_order, *own, *q_blocks, gkv)
    return outs[:n_x], outs[n_x]


def partial_kernel(own_ref, other_ref, swapped_ref, out_ref):
    cols = out_ref.shape[2]
    for h in range(out_ref.shape[0]):
        at = slice(h * cols, (h + 1) * cols)
        out_ref[h] = (own_ref[:, at] + nt(other_ref[...], swapped_ref[at, :])).astype(BF)


def partial_hidden(own, other, swapped, n_hi):
    return pl.pallas_call(
        partial_kernel,
        out_shape=jax.ShapeDtypeStruct((n_hi, own.shape[0], own.shape[1] // n_hi), BF),
        in_specs=[VMEM] * 3,
        out_specs=VMEM,
        compiler_params=pltpu.CompilerParams(vmem_limit_bytes=16 * 1024 * 1024),
        name="partial_hidden",
    )(own, other, swapped)


def prep(span_order, queries, grad_out, fwd_out, log_norm):
    return pl.pallas_call(
        prep_kernel,
        out_shape=[jax.ShapeDtypeStruct((QBLOCK, HD), BF), jax.ShapeDtypeStruct((24, HD), F32)],
        in_specs=[SMEM, VMEM, VMEM, VMEM, VMEM],
        out_specs=[VMEM] * 2,
        name="prep",
    )(span_order, queries, grad_out, fwd_out, log_norm)


def pack(span_order, key_rows, value_rows, copies):
    return pl.pallas_call(
        pack_kernel,
        out_shape=jax.ShapeDtypeStruct((copies, KBLOCK, HD), BF),
        in_specs=[SMEM, VMEM, VMEM],
        out_specs=pl.BlockSpec(memory_space=pl.ANY),
        scratch_shapes=[pltpu.VMEM((KBLOCK, HD), BF), pltpu.SemaphoreType.DMA((copies,))],
        name="pack",
    )(span_order, key_rows, value_rows)


def hop(block, axis, shift):
    n = lax.axis_size(axis)
    return lax.ppermute(block, axis, [(i, (i + shift) % n) for i in range(n)])


def body(queries, key_rows, value_rows, grad_out, fwd_out, log_norm, span_order, doc_lengths, key_proj, value_proj):
    n_q, n_k = lax.axis_size("x"), lax.axis_size(KEYS)
    n_hi = lax.axis_size("y_hi")
    core = lax.axis_index("core")

    gkv = lax.all_to_all(pack(span_order, key_rows, value_rows, n_k), KEYS, 0, 0)
    mine, own_rows = prep(span_order, queries, grad_out, fwd_out, log_norm)
    q_blocks = [hop(mine, "x", shift) for shift in range(1, n_q)]

    cols = key_proj.shape[0] // (2 * n_hi)
    projs = jnp.concatenate([key_proj, value_proj], axis=1).reshape(n_hi, 2, cols, 2 * HD)
    kept = lax.dynamic_index_in_dim(projs, core, 1, keepdims=False).reshape(n_hi * cols, 2 * HD)
    given = lax.dynamic_index_in_dim(projs, 1 - core, 1, keepdims=False).reshape(n_hi * cols, 2 * HD)
    swapped = hop(given, "core", 1)

    dqs, dkv = tile_grads(doc_lengths, span_order, (queries, grad_out, own_rows), q_blocks, gkv, n_q)

    parts = lax.all_to_all(dkv, KEYS, 0, 0)
    homes = [dqs[0]] + [hop(dqs[shift], "x", -shift) for shift in range(1, n_q)]
    parts, homes, swapped = lax.optimization_barrier((parts, homes, swapped))
    grad_query = sum(h.astype(F32) for h in homes).astype(BF)
    total = jnp.sum(parts.astype(F32), axis=0)
    grad_key = (total[:TOK] * (1.0 / math.sqrt(HD))).astype(BF)
    grad_value = total[TOK:].astype(BF)
    both = jnp.concatenate([grad_key, grad_value], axis=1)

    partial = partial_hidden(nt(both, kept), hop(both, "core", 1), swapped, n_hi)
    shares = lax.all_to_all(partial, "y_hi", 0, 0)
    hidden = jnp.sum(shares.astype(F32), axis=0).astype(BF)
    return grad_query, grad_key, grad_value, hidden


def solution(mesh):
    fine = Mesh(mesh.devices.reshape(4, 2, 8, 4, 2), AXES)
    placed = (
        P(CTX, KV),
        P(CTX, KV),
        P(CTX, KV),
        P(CTX, KV),
        P(CTX, KV),
        P(KV, CTX),
        P(CTX),
        P(),
        P(None, KV),
        P(None, KV),
    )
    return jax.shard_map(
        body,
        mesh=fine,
        in_specs=placed,
        out_specs=(P(CTX, KV), P(CTX, KV), P(CTX, KV), P(CTX, KV)),
        check_vma=False,
    )
```

time: 117 us -> 114 us (0.974)
  the two profiles are of different devices: /device:TPU:76 before, /device:TPU:78 now
where the time goes in v3:
time: 114 us
  waiting for transfers between devices  51 us (45%)
  starting transfers between devices  43.3 us (38%)
  Pallas kernels  14 us (12%)
  other arithmetic  3.09 us (3%)
    ppermute x8, starting transfers between devices, hop(): return lax.ppermute(block, axis, [(i, (i + shift) % n) for i in range(n)])  21.7 us
    all_to_all x1, waiting for transfers between devices, body(): shares = lax.all_to_all(partial, 'y_hi', 0, 0)  16.3 us
    ppermute x8, waiting for transfers between devices, hop(): return lax.ppermute(block, axis, [(i, (i + shift) % n) for i in range(n)])  16.3 us
    all_to_all x1, starting transfers between devices, body(): lax.all_to_all(pack(span_order, key_rows, value_rows, n_k), KEYS, 0, 0)  10.9 us
    all_to_all x1, waiting for transfers between devices, body(): parts = lax.all_to_all(dkv, KEYS, 0, 0)  10.8 us
    pallas_call x1, Pallas kernels, tile_grads(): pl.pallas_call(lambda *refs: tile_kernel(n_q, n_x, n_k, *refs), out_shape...  8.81 us
    all_to_all x1, waiting for transfers between devices, body(): lax.all_to_all(pack(span_order, key_rows, value_rows, n_k), KEYS, 0, 0)  7.58 us
    all_to_all x1, starting transfers between devices, body(): shares = lax.all_to_all(partial, 'y_hi', 0, 0)  6.2 us
  transfers between devices with their start and end apart: 11, of which 9 were waited for; matrix products, arithmetic and copies ran while one was open for 1% of the time, Pallas kernels for 2%

profile of v3, /device:TPU:78, one launch (start us, length us, event | category | flops | bytes accessed | tf_op | source)
XLA Modules:
  0.0 113.7 jit_solution(2307374027258448358)
XLA Ops:
  0.6 0.0 copy-start.2
  0.7 2.0 %pack.1 = bf16[16,272,128]{2,1,0:T(8,128)(2,1)} custom-call(s32[2]{0:T(128)} %refs_1_.1, bf16[128,128]{1,0:T(8,128)(2,1)} %k_ref.1, bf16[128,128]{1,0:T(8,128)(2,1)} %v_ref.1), custom_call_target="tpu_custom_call" | custom-call | tf_op jit(solution)/shard_map/pack/pallas_call | solution.py:293
  2.7 10.9 %all-to-all-start = ((bf16[16,272,128]{2,1,0:T(8,128)(2,1)}), bf16[16,272,128]{2,1,0:T(8,128)(2,1)S(1)}, u32[]{:S(2)}, u32[]{:S(2)}) async-start(bf16[16,272,128]{2,1,0:T(8,128)(2,1)} %pack.1), calls=%async_computation | async-start | bytes 2228224 | tf_op jit(solution)/shard_map/all_to_all | solution.py:313
  13.6 1.9 %prep.1 = (bf16[1056,128]{1,0:T(8,128)(2,1)}, f32[24,128]{1,0:T(8,128)}) custom-call(s32[2]{0:T(128)} %refs_1_.1, bf16[128,512]{1,0:T(8,128)(2,1)} %refs_2_.1, bf16[128,512]{1,0:T(8,128)(2,1)} %refs_3_.1, bf16[128,512]{1,0:T(8,128)(2,1)} %o_ref.1, f32[4,128]{1,0:T(4,128)} %lse_ref.1), custom_call_target="tpu_custom_call" | custom-call | tf_op jit(solution)/shard_map/prep/pallas_call | solution.py:283
  15.5 2.4 %collective-permute-start = (bf16[1056,128]{1,0:T(8,128)(2,1)}, bf16[1056,128]{1,0:T(8,128)(2,1)S(1)}, u32[]{:S(2)}, u32[]{:S(2)}) collective-permute-start(bf16[1056,128]{1,0:T(8,128)(2,1)} %get-tuple-element.18), channel_id=1, source_target_pairs={{0,128},{128,256},{256,384},{384,0},{1,129},{129,257},{257,385},{3... | collective-permute-start | bytes 811016 | tf_op jit(solution)/shard_map/ppermute | solution.py:305
  17.9 4.3 %collective-permute-start.1 = (bf16[1056,128]{1,0:T(8,128)(2,1)}, bf16[1056,128]{1,0:T(8,128)(2,1)S(1)}, u32[]{:S(2)}, u32[]{:S(2)}) collective-permute-start(bf16[1056,128]{1,0:T(8,128)(2,1)} %get-tuple-element.18), channel_id=1, source_target_pairs={{0,256},{128,384},{256,0},{384,128},{1,257},{129,385},{257,1},{385... | collective-permute-start | bytes 811016 | tf_op jit(solution)/shard_map/ppermute | solution.py:305
  22.2 1.9 %collective-permute-start.2 = (bf16[1056,128]{1,0:T(8,128)(2,1)}, bf16[1056,128]{1,0:T(8,128)(2,1)S(1)}, u32[]{:S(2)}, u32[]{:S(2)}) collective-permute-start(bf16[1056,128]{1,0:T(8,128)(2,1)} %get-tuple-element.18), channel_id=1, source_target_pairs={{0,384},{128,0},{256,128},{384,256},{1,385},{129,1},{257,129},{385... | collective-permute-start | bytes 811016 | tf_op jit(solution)/shard_map/ppermute | solution.py:305
  24.1 2.9 %collective-permute-done.refs_5_ = bf16[1056,128]{1,0:T(8,128)(2,1)S(1)} collective-permute-done((bf16[1056,128]{1,0:T(8,128)(2,1)}, bf16[1056,128]{1,0:T(8,128)(2,1)S(1)}, u32[]{:S(2)}, u32[]{:S(2)}) %collective-permute-start) | collective-permute-done | bytes 270368 | tf_op jit(solution)/shard_map/ppermute | solution.py:305
  27.0 3.8 %collective-permute-done.1.refs_6_ = bf16[1056,128]{1,0:T(8,128)(2,1)S(1)} collective-permute-done((bf16[1056,128]{1,0:T(8,128)(2,1)}, bf16[1056,128]{1,0:T(8,128)(2,1)S(1)}, u32[]{:S(2)}, u32[]{:S(2)}) %collective-permute-start.1) | collective-permute-done | bytes 270368 | tf_op jit(solution)/shard_map/ppermute | solution.py:305
  30.8 3.9 %collective-permute-done.2.refs_7_ = bf16[1056,128]{1,0:T(8,128)(2,1)S(1)} collective-permute-done((bf16[1056,128]{1,0:T(8,128)(2,1)}, bf16[1056,128]{1,0:T(8,128)(2,1)S(1)}, u32[]{:S(2)}, u32[]{:S(2)}) %collective-permute-start.2) | collective-permute-done | bytes 270368 | tf_op jit(solution)/shard_map/ppermute | solution.py:305
  34.7 7.6 %all-to-all-done.refs_8_ = bf16[16,272,128]{2,1,0:T(8,128)(2,1)S(1)} async-done(((bf16[16,272,128]{2,1,0:T(8,128)(2,1)}), bf16[16,272,128]{2,1,0:T(8,128)(2,1)S(1)}, u32[]{:S(2)}, u32[]{:S(2)}) %all-to-all-start) | async-done | bytes 1114144 | tf_op jit(solution)/shard_map/all_to_all | solution.py:313
  42.3 0.7 copy-done.3
  43.0 8.8 %tile_grads.1 = (bf16[128,512]{1,0:T(8,128)(2,1)S(1)}, bf16[128,512]{1,0:T(8,128)(2,1)S(1)}, bf16[128,512]{1,0:T(8,128)(2,1)S(1)}, bf16[128,512]{1,0:T(8,128)(2,1)S(1)}, bf16[16,256,128]{2,1,0:T(8,128)(2,1)}) custom-call(s32[2]{0:T(128)S(1)} %copy-done.4, s32[2]{0:T(128)S(1)} %copy-done.2, bf16[128,512]{1,0:T(8,128)(2,1)S(1)} %copy-done, ...), custom_call_target="tpu_custom_call" | custom-call | flops 5000000000 | bytes 4000000 | tf_op jit(solution)/shard_map/tile_grads/pallas_call | solution.py:236
  51.8 4.5 %all-to-all-start.1 = ((bf16[16,256,128]{2,1,0:T(8,128)(2,1)}), bf16[16,256,128]{2,1,0:T(8,128)(2,1)}, u32[]{:S(2)}, u32[]{:S(2)}) async-start(bf16[16,256,128]{2,1,0:T(8,128)(2,1)} %get-tuple-element.19), calls=%async_computation.1 | async-start | bytes 2097152 | tf_op jit(solution)/shard_map/all_to_all | solution.py:325
  56.4 0.2 pad_maximum_fusion
  56.6 0.1 constant_dynamic-slice_fusion
  56.8 1.9 %collective-permute-start.6 = (bf16[2048,256]{1,0:T(8,128)(2,1)S(1)}, bf16[2048,256]{1,0:T(8,128)(2,1)S(1)}, u32[]{:S(2)}, u32[]{:S(2)}) collective-permute-start(bf16[2048,256]{1,0:T(8,128)(2,1)S(1)} %bitcast.8), channel_id=1, source_target_pairs={{0,1},{1,0},{2,3},{3,2},{4,5},{5,4},{6,7},{7,6},{8,9},{9,8},{10,11... | collective-permute-start | bytes 3145736 | tf_op jit(solution)/shard_map/ppermute | solution.py:305
  58.7 2.7 %collective-permute-start.3 = (bf16[128,512]{1,0:T(8,128)(2,1)S(1)}, bf16[128,512]{1,0:T(8,128)(2,1)S(1)}, u32[]{:S(2)}, u32[]{:S(2)}) collective-permute-start(bf16[128,512]{1,0:T(8,128)(2,1)S(1)} %get-tuple-element.21), channel_id=1, source_target_pairs={{0,384},{128,0},{256,128},{384,256},{1,385},{129,1},{257,129},{385... | collective-permute-start | bytes 393224 | tf_op jit(solution)/shard_map/ppermute | solution.py:305
  61.4 3.0 %collective-permute-start.4 = (bf16[128,512]{1,0:T(8,128)(2,1)S(1)}, bf16[128,512]{1,0:T(8,128)(2,1)S(1)}, u32[]{:S(2)}, u32[]{:S(2)}) collective-permute-start(bf16[128,512]{1,0:T(8,128)(2,1)S(1)} %get-tuple-element.22), channel_id=1, source_target_pairs={{0,256},{128,384},{256,0},{384,128},{1,257},{129,385},{257,1},{385... | collective-permute-start | bytes 393224 | tf_op jit(solution)/shard_map/ppermute | solution.py:305
  64.5 3.5 %collective-permute-start.5 = (bf16[128,512]{1,0:T(8,128)(2,1)S(1)}, bf16[128,512]{1,0:T(8,128)(2,1)S(1)}, u32[]{:S(2)}, u32[]{:S(2)}) collective-permute-start(bf16[128,512]{1,0:T(8,128)(2,1)S(1)} %get-tuple-element.23), channel_id=1, source_target_pairs={{0,128},{128,256},{256,384},{384,0},{1,129},{129,257},{257,385},{3... | collective-permute-start | bytes 393224 | tf_op jit(solution)/shard_map/ppermute | solution.py:305
  68.0 2.5 %collective-permute-done.4 = bf16[128,512]{1,0:T(8,128)(2,1)S(1)} collective-permute-done((bf16[128,512]{1,0:T(8,128)(2,1)S(1)}, bf16[128,512]{1,0:T(8,128)(2,1)S(1)}, u32[]{:S(2)}, u32[]{:S(2)}) %collective-permute-start.4) | collective-permute-done | bytes 131104 | tf_op jit(solution)/shard_map/ppermute | solution.py:305
  70.5 2.5 %collective-permute-done.5 = bf16[128,512]{1,0:T(8,128)(2,1)S(1)} collective-permute-done((bf16[128,512]{1,0:T(8,128)(2,1)S(1)}, bf16[128,512]{1,0:T(8,128)(2,1)S(1)}, u32[]{:S(2)}, u32[]{:S(2)}) %collective-permute-start.5) | collective-permute-done | bytes 131104 | tf_op jit(solution)/shard_map/ppermute | solution.py:305
  73.0 10.8 %all-to-all-done.1 = bf16[16,256,128]{2,1,0:T(8,128)(2,1)} async-done(((bf16[16,256,128]{2,1,0:T(8,128)(2,1)}), bf16[16,256,128]{2,1,0:T(8,128)(2,1)}, u32[]{:S(2)}, u32[]{:S(2)}) %all-to-all-start.1) | async-done | bytes 1048608 | tf_op jit(solution)/shard_map/all_to_all | solution.py:325
  83.9 1.4 %convert_reduce_fusion = f32[256,128]{1,0:T(8,128)S(1)} fusion(bf16[16,256,128]{2,1,0:T(8,128)(2,1)} %all-to-all-done.1), kind=kLoop, calls=%fused_computation.1 | loop fusion | flops 1015808 | bytes 1179648 | tf_op jit(solution)/shard_map/reduce_sum | solution.py:329
  85.3 1.9 %collective-permute-start.7 = (bf16[128,256]{1,0:T(8,128)(2,1)S(1)}, bf16[128,256]{1,0:T(8,128)(2,1)S(1)}, u32[]{:S(2)}, u32[]{:S(2)}) collective-permute-start(bf16[128,256]{1,0:T(8,128)(2,1)S(1)} %pad_maximum_fusion.1), channel_id=1, source_target_pairs={{0,1},{1,0},{2,3},{3,2},{4,5},{5,4},{6,7},{7,6},{8,9},{9,8},{10,11... | collective-permute-start | bytes 196616 | tf_op jit(solution)/shard_map/ppermute | solution.py:305
  87.2 0.5 fusion.1.own_ref
  87.7 0.7 collective-permute-done.7.other_ref
  88.5 1.3 %partial_hidden.1 = bf16[4,128,512]{2,1,0:T(8,128)(2,1)} custom-call(f32[128,2048]{1,0:T(8,128)S(1)} %fusion.1.own_ref, bf16[128,256]{1,0:T(8,128)(2,1)S(1)} %collective-permute-done.7.other_ref, bf16[2048,256]{1,0:T(8,128)(2,1)S(1)} %collective-permute-done.6.swapped_ref), custom_call_target="tpu_custom_call" | custom-call | tf_op jit(solution)/shard_map/partial_hidden/pallas_call | solution.py:272
  89.7 6.2 %all-to-all-start.2 = ((bf16[4,128,512]{2,1,0:T(8,128)(2,1)}), bf16[4,128,512]{2,1,0:T(8,128)(2,1)S(1)}, u32[]{:S(2)}, u32[]{:S(2)}) async-start(bf16[4,128,512]{2,1,0:T(8,128)(2,1)} %partial_hidden.1), calls=%async_computation.2 | async-start | bytes 1048576 | tf_op jit(solution)/shard_map/all_to_all | solution.py:335
  95.9 0.7 add_convert_fusion
  96.7 16.3 %all-to-all-done.2 = bf16[4,128,512]{2,1,0:T(8,128)(2,1)S(1)} async-done(((bf16[4,128,512]{2,1,0:T(8,128)(2,1)}), bf16[4,128,512]{2,1,0:T(8,128)(2,1)S(1)}, u32[]{:S(2)}, u32[]{:S(2)}) %all-to-all-start.2) | async-done | bytes 524320 | tf_op jit(solution)/shard_map/all_to_all | solution.py:335
  113.0 0.7 reduce_sum.22
  (21 shorter events, 0.1 us)
Async XLA Ops:
  0.6 41.6 %copy-start.2 = (s32[2]{0:T(128)S(1)}, s32[2]{0:T(128)}, u32[]{:S(2)}) copy-start(s32[2]{0:T(128)} %refs_1_.1) | copy-start | bytes 28
  0.6 41.6 %copy-start = (bf16[128,512]{1,0:T(8,128)(2,1)S(1)}, bf16[128,512]{1,0:T(8,128)(2,1)}, u32[]{:S(2)}) copy-start(bf16[128,512]{1,0:T(8,128)(2,1)} %refs_2_.1) | copy-start | bytes 393220
  0.7 41.6 %copy-start.1 = (bf16[128,512]{1,0:T(8,128)(2,1)S(1)}, bf16[128,512]{1,0:T(8,128)(2,1)}, u32[]{:S(2)}) copy-start(bf16[128,512]{1,0:T(8,128)(2,1)} %refs_3_.1) | copy-start | bytes 393220
  0.7 41.6 %copy-start.4 = (s32[2]{0:T(128)S(1)}, s32[2]{0:T(128)}, u32[]{:S(2)}) copy-start(s32[2]{0:T(128)} %refs_0_.1) | copy-start | bytes 28
  2.7 39.6 %all-to-all-start = ((bf16[16,272,128]{2,1,0:T(8,128)(2,1)}), bf16[16,272,128]{2,1,0:T(8,128)(2,1)S(1)}, u32[]{:S(2)}, u32[]{:S(2)}) async-start(bf16[16,272,128]{2,1,0:T(8,128)(2,1)} %pack.1), calls=%async_computation | async-start | bytes 2228224 | tf_op jit(solution)/shard_map/all_to_all | solution.py:313
  15.5 11.5 %collective-permute-start = (bf16[1056,128]{1,0:T(8,128)(2,1)}, bf16[1056,128]{1,0:T(8,128)(2,1)S(1)}, u32[]{:S(2)}, u32[]{:S(2)}) collective-permute-start(bf16[1056,128]{1,0:T(8,128)(2,1)} %get-tuple-element.18), channel_id=1, source_target_pairs={{0,128},{128,256},{256,384},{384,0},{1,129},{129,257},{257,385},{3... | collective-permute-start | bytes 811016 | tf_op jit(solution)/shard_map/ppermute | solution.py:305
  17.9 12.9 %collective-permute-start.1 = (bf16[1056,128]{1,0:T(8,128)(2,1)}, bf16[1056,128]{1,0:T(8,128)(2,1)S(1)}, u32[]{:S(2)}, u32[]{:S(2)}) collective-permute-start(bf16[1056,128]{1,0:T(8,128)(2,1)} %get-tuple-element.18), channel_id=1, source_target_pairs={{0,256},{128,384},{256,0},{384,128},{1,257},{129,385},{257,1},{385... | collective-permute-start | bytes 811016 | tf_op jit(solution)/shard_map/ppermute | solution.py:305
  22.2 12.4 %collective-permute-start.2 = (bf16[1056,128]{1,0:T(8,128)(2,1)}, bf16[1056,128]{1,0:T(8,128)(2,1)S(1)}, u32[]{:S(2)}, u32[]{:S(2)}) collective-permute-start(bf16[1056,128]{1,0:T(8,128)(2,1)} %get-tuple-element.18), channel_id=1, source_target_pairs={{0,384},{128,0},{256,128},{384,256},{1,385},{129,1},{257,129},{385... | collective-permute-start | bytes 811016 | tf_op jit(solution)/shard_map/ppermute | solution.py:305
  42.3 0.7 copy-start.3
  51.8 4.6 %copy-start.5 = (bf16[4096,128]{1,0:T(8,128)(2,1)S(1)}, bf16[4096,128]{1,0:T(8,128)(2,1)}, u32[]{:S(2)}) copy-start(bf16[4096,128]{1,0:T(8,128)(2,1)} %param.19) | copy-start | bytes 3145732
  51.8 4.6 %copy-start.6 = (bf16[4096,128]{1,0:T(8,128)(2,1)S(1)}, bf16[4096,128]{1,0:T(8,128)(2,1)}, u32[]{:S(2)}) copy-start(bf16[4096,128]{1,0:T(8,128)(2,1)} %param.18) | copy-start | bytes 3145732
  51.8 32.0 %all-to-all-start.1 = ((bf16[16,256,128]{2,1,0:T(8,128)(2,1)}), bf16[16,256,128]{2,1,0:T(8,128)(2,1)}, u32[]{:S(2)}, u32[]{:S(2)}) async-start(bf16[16,256,128]{2,1,0:T(8,128)(2,1)} %get-tuple-element.19), calls=%async_computation.1 | async-start | bytes 2097152 | tf_op jit(solution)/shard_map/all_to_all | solution.py:325
  56.8 11.2 %collective-permute-start.6 = (bf16[2048,256]{1,0:T(8,128)(2,1)S(1)}, bf16[2048,256]{1,0:T(8,128)(2,1)S(1)}, u32[]{:S(2)}, u32[]{:S(2)}) collective-permute-start(bf16[2048,256]{1,0:T(8,128)(2,1)S(1)} %bitcast.8), channel_id=1, source_target_pairs={{0,1},{1,0},{2,3},{3,2},{4,5},{5,4},{6,7},{7,6},{8,9},{9,8},{10,11... | collective-permute-start | bytes 3145736 | tf_op jit(solution)/shard_map/ppermute | solution.py:305
  58.7 9.3 %collective-permute-start.3 = (bf16[128,512]{1,0:T(8,128)(2,1)S(1)}, bf16[128,512]{1,0:T(8,128)(2,1)S(1)}, u32[]{:S(2)}, u32[]{:S(2)}) collective-permute-start(bf16[128,512]{1,0:T(8,128)(2,1)S(1)} %get-tuple-element.21), channel_id=1, source_target_pairs={{0,384},{128,0},{256,128},{384,256},{1,385},{129,1},{257,129},{385... | collective-permute-start | bytes 393224 | tf_op jit(solution)/shard_map/ppermute | solution.py:305
  61.4 9.1 %collective-permute-start.4 = (bf16[128,512]{1,0:T(8,128)(2,1)S(1)}, bf16[128,512]{1,0:T(8,128)(2,1)S(1)}, u32[]{:S(2)}, u32[]{:S(2)}) collective-permute-start(bf16[128,512]{1,0:T(8,128)(2,1)S(1)} %get-tuple-element.22), channel_id=1, source_target_pairs={{0,256},{128,384},{256,0},{384,128},{1,257},{129,385},{257,1},{385... | collective-permute-start | bytes 393224 | tf_op jit(solution)/shard_map/ppermute | solution.py:305
  64.5 8.5 %collective-permute-start.5 = (bf16[128,512]{1,0:T(8,128)(2,1)S(1)}, bf16[128,512]{1,0:T(8,128)(2,1)S(1)}, u32[]{:S(2)}, u32[]{:S(2)}) collective-permute-start(bf16[128,512]{1,0:T(8,128)(2,1)S(1)} %get-tuple-element.23), channel_id=1, source_target_pairs={{0,128},{128,256},{256,384},{384,0},{1,129},{129,257},{257,385},{3... | collective-permute-start | bytes 393224 | tf_op jit(solution)/shard_map/ppermute | solution.py:305
  85.3 4.5 %copy-start.7 = (bf16[128,128]{1,0:T(8,128)(2,1)}, bf16[128,128]{1,0:T(8,128)(2,1)S(1)}, u32[]{:S(2)}) copy-start(bf16[128,128]{1,0:T(8,128)(2,1)S(1)} %fusion) | copy-start | bytes 98308
  85.3 4.5 %copy-start.8 = (bf16[128,128]{1,0:T(8,128)(2,1)}, bf16[128,128]{1,0:T(8,128)(2,1)S(1)}, u32[]{:S(2)}) copy-start(bf16[128,128]{1,0:T(8,128)(2,1)S(1)} %slice.15) | copy-start | bytes 98308
  85.3 3.1 %collective-permute-start.7 = (bf16[128,256]{1,0:T(8,128)(2,1)S(1)}, bf16[128,256]{1,0:T(8,128)(2,1)S(1)}, u32[]{:S(2)}, u32[]{:S(2)}) collective-permute-start(bf16[128,256]{1,0:T(8,128)(2,1)S(1)} %pad_maximum_fusion.1), channel_id=1, source_target_pairs={{0,1},{1,0},{2,3},{3,2},{4,5},{5,4},{6,7},{7,6},{8,9},{9,8},{10,11... | collective-permute-start | bytes 196616 | tf_op jit(solution)/shard_map/ppermute | solution.py:305
  89.7 23.2 %all-to-all-start.2 = ((bf16[4,128,512]{2,1,0:T(8,128)(2,1)}), bf16[4,128,512]{2,1,0:T(8,128)(2,1)S(1)}, u32[]{:S(2)}, u32[]{:S(2)}) async-start(bf16[4,128,512]{2,1,0:T(8,128)(2,1)} %partial_hidden.1), calls=%async_computation.2 | async-start | bytes 1048576 | tf_op jit(solution)/shard_map/all_to_all | solution.py:335

commit v4 on v3

--- a/solution.py
+++ b/solution.py
@@ -9,7 +9,7 @@
 
 AXES = ("x", "y_lo", "z", "y_hi", "core")
 CTX = ("x", "y_lo", "z")
-KEYS = ("y_lo", "z")
+KEYS = ("z", "y_lo")
 KV = ("y_hi", "core")
 SPAN = 64
 HD = 128

time: 114 us -> 115 us (level)
  the two profiles are of different devices: /device:TPU:78 before, /device:TPU:14 now
where the time goes in v4:
time: 115 us; the launch traced here: 113 us
  waiting for transfers between devices  49.1 us (43%)
  starting transfers between devices  45.8 us (40%)
  Pallas kernels  13 us (11%)
  other arithmetic  3.09 us (3%)
    ppermute x8, starting transfers between devices, hop(): return lax.ppermute(block, axis, [(i, (i + shift) % n) for i in range(n)])  22.2 us
    all_to_all x1, waiting for transfers between devices, body(): shares = lax.all_to_all(partial, 'y_hi', 0, 0)  15.9 us
    ppermute x8, waiting for transfers between devices, hop(): return lax.ppermute(block, axis, [(i, (i + shift) % n) for i in range(n)])  15.8 us
    all_to_all x1, starting transfers between devices, body(): lax.all_to_all(pack(span_order, key_rows, value_rows, n_k), KEYS, 0, 0)  11.8 us
    all_to_all x1, waiting for transfers between devices, body(): parts = lax.all_to_all(dkv, KEYS, 0, 0)  9.75 us
    pallas_call x1, Pallas kernels, tile_grads(): pl.pallas_call(lambda *refs: tile_kernel(n_q, n_x, n_k, *refs), out_shape...  7.84 us
    all_to_all x1, waiting for transfers between devices, body(): lax.all_to_all(pack(span_order, key_rows, value_rows, n_k), KEYS, 0, 0)  7.69 us
    all_to_all x1, starting transfers between devices, body(): shares = lax.all_to_all(partial, 'y_hi', 0, 0)  6.19 us
  transfers between devices with their start and end apart: 11, of which 9 were waited for; matrix products, arithmetic and copies ran while one was open for 1% of the time, Pallas kernels for 2%

profile of v4, /device:TPU:14, one launch (start us, length us, event | category | flops | bytes accessed | tf_op | source)
XLA Modules:
  0.0 113.3 jit_solution(4270004209539724965)
XLA Ops:
  0.6 0.0 copy-start.2
  0.7 2.0 %pack.1 = bf16[16,272,128]{2,1,0:T(8,128)(2,1)} custom-call(s32[2]{0:T(128)} %refs_1_.1, bf16[128,128]{1,0:T(8,128)(2,1)} %k_ref.1, bf16[128,128]{1,0:T(8,128)(2,1)} %v_ref.1), custom_call_target="tpu_custom_call" | custom-call | tf_op jit(solution)/shard_map/pack/pallas_call | solution.py:293
  2.7 11.8 %all-to-all-start = ((bf16[16,272,128]{2,1,0:T(8,128)(2,1)}), bf16[16,272,128]{2,1,0:T(8,128)(2,1)S(1)}, u32[]{:S(2)}, u32[]{:S(2)}) async-start(bf16[16,272,128]{2,1,0:T(8,128)(2,1)} %pack.1), calls=%async_computation | async-start | bytes 2228224 | tf_op jit(solution)/shard_map/all_to_all | solution.py:313
  14.5 1.9 %prep.1 = (bf16[1056,128]{1,0:T(8,128)(2,1)}, f32[24,128]{1,0:T(8,128)}) custom-call(s32[2]{0:T(128)} %refs_1_.1, bf16[128,512]{1,0:T(8,128)(2,1)} %refs_2_.1, bf16[128,512]{1,0:T(8,128)(2,1)} %refs_3_.1, bf16[128,512]{1,0:T(8,128)(2,1)} %o_ref.1, f32[4,128]{1,0:T(4,128)} %lse_ref.1), custom_call_target="tpu_custom_call" | custom-call | tf_op jit(solution)/shard_map/prep/pallas_call | solution.py:283
  16.4 2.4 %collective-permute-start = (bf16[1056,128]{1,0:T(8,128)(2,1)}, bf16[1056,128]{1,0:T(8,128)(2,1)S(1)}, u32[]{:S(2)}, u32[]{:S(2)}) collective-permute-start(bf16[1056,128]{1,0:T(8,128)(2,1)} %get-tuple-element.18), channel_id=1, source_target_pairs={{0,128},{128,256},{256,384},{384,0},{1,129},{129,257},{257,385},{3... | collective-permute-start | bytes 811016 | tf_op jit(solution)/shard_map/ppermute | solution.py:305
  18.8 4.3 %collective-permute-start.1 = (bf16[1056,128]{1,0:T(8,128)(2,1)}, bf16[1056,128]{1,0:T(8,128)(2,1)S(1)}, u32[]{:S(2)}, u32[]{:S(2)}) collective-permute-start(bf16[1056,128]{1,0:T(8,128)(2,1)} %get-tuple-element.18), channel_id=1, source_target_pairs={{0,256},{128,384},{256,0},{384,128},{1,257},{129,385},{257,1},{385... | collective-permute-start | bytes 811016 | tf_op jit(solution)/shard_map/ppermute | solution.py:305
  23.1 1.9 %collective-permute-start.2 = (bf16[1056,128]{1,0:T(8,128)(2,1)}, bf16[1056,128]{1,0:T(8,128)(2,1)S(1)}, u32[]{:S(2)}, u32[]{:S(2)}) collective-permute-start(bf16[1056,128]{1,0:T(8,128)(2,1)} %get-tuple-element.18), channel_id=1, source_target_pairs={{0,384},{128,0},{256,128},{384,256},{1,385},{129,1},{257,129},{385... | collective-permute-start | bytes 811016 | tf_op jit(solution)/shard_map/ppermute | solution.py:305
  25.1 2.9 %collective-permute-done.refs_5_ = bf16[1056,128]{1,0:T(8,128)(2,1)S(1)} collective-permute-done((bf16[1056,128]{1,0:T(8,128)(2,1)}, bf16[1056,128]{1,0:T(8,128)(2,1)S(1)}, u32[]{:S(2)}, u32[]{:S(2)}) %collective-permute-start) | collective-permute-done | bytes 270368 | tf_op jit(solution)/shard_map/ppermute | solution.py:305
  27.9 3.8 %collective-permute-done.1.refs_6_ = bf16[1056,128]{1,0:T(8,128)(2,1)S(1)} collective-permute-done((bf16[1056,128]{1,0:T(8,128)(2,1)}, bf16[1056,128]{1,0:T(8,128)(2,1)S(1)}, u32[]{:S(2)}, u32[]{:S(2)}) %collective-permute-start.1) | collective-permute-done | bytes 270368 | tf_op jit(solution)/shard_map/ppermute | solution.py:305
  31.7 3.9 %collective-permute-done.2.refs_7_ = bf16[1056,128]{1,0:T(8,128)(2,1)S(1)} collective-permute-done((bf16[1056,128]{1,0:T(8,128)(2,1)}, bf16[1056,128]{1,0:T(8,128)(2,1)S(1)}, u32[]{:S(2)}, u32[]{:S(2)}) %collective-permute-start.2) | collective-permute-done | bytes 270368 | tf_op jit(solution)/shard_map/ppermute | solution.py:305
  35.6 7.7 %all-to-all-done.refs_8_ = bf16[16,272,128]{2,1,0:T(8,128)(2,1)S(1)} async-done(((bf16[16,272,128]{2,1,0:T(8,128)(2,1)}), bf16[16,272,128]{2,1,0:T(8,128)(2,1)S(1)}, u32[]{:S(2)}, u32[]{:S(2)}) %all-to-all-start) | async-done | bytes 1114144 | tf_op jit(solution)/shard_map/all_to_all | solution.py:313
  43.3 0.7 copy-done.3
  44.0 7.8 %tile_grads.1 = (bf16[128,512]{1,0:T(8,128)(2,1)S(1)}, bf16[128,512]{1,0:T(8,128)(2,1)S(1)}, bf16[128,512]{1,0:T(8,128)(2,1)S(1)}, bf16[128,512]{1,0:T(8,128)(2,1)S(1)}, bf16[16,256,128]{2,1,0:T(8,128)(2,1)}) custom-call(s32[2]{0:T(128)S(1)} %copy-done.4, s32[2]{0:T(128)S(1)} %copy-done.2, bf16[128,512]{1,0:T(8,128)(2,1)S(1)} %copy-done, ...), custom_call_target="tpu_custom_call" | custom-call | flops 5000000000 | bytes 4000000 | tf_op jit(solution)/shard_map/tile_grads/pallas_call | solution.py:236
  51.9 5.6 %all-to-all-start.1 = ((bf16[16,256,128]{2,1,0:T(8,128)(2,1)}), bf16[16,256,128]{2,1,0:T(8,128)(2,1)}, u32[]{:S(2)}, u32[]{:S(2)}) async-start(bf16[16,256,128]{2,1,0:T(8,128)(2,1)} %get-tuple-element.19), calls=%async_computation.1 | async-start | bytes 2097152 | tf_op jit(solution)/shard_map/all_to_all | solution.py:325
  57.5 0.2 pad_maximum_fusion
  57.7 0.1 constant_dynamic-slice_fusion
  57.9 1.9 %collective-permute-start.6 = (bf16[2048,256]{1,0:T(8,128)(2,1)S(1)}, bf16[2048,256]{1,0:T(8,128)(2,1)S(1)}, u32[]{:S(2)}, u32[]{:S(2)}) collective-permute-start(bf16[2048,256]{1,0:T(8,128)(2,1)S(1)} %bitcast.8), channel_id=1, source_target_pairs={{0,1},{1,0},{2,3},{3,2},{4,5},{5,4},{6,7},{7,6},{8,9},{9,8},{10,11... | collective-permute-start | bytes 3145736 | tf_op jit(solution)/shard_map/ppermute | solution.py:305
  59.8 2.7 %collective-permute-start.3 = (bf16[128,512]{1,0:T(8,128)(2,1)S(1)}, bf16[128,512]{1,0:T(8,128)(2,1)S(1)}, u32[]{:S(2)}, u32[]{:S(2)}) collective-permute-start(bf16[128,512]{1,0:T(8,128)(2,1)S(1)} %get-tuple-element.21), channel_id=1, source_target_pairs={{0,384},{128,0},{256,128},{384,256},{1,385},{129,1},{257,129},{385... | collective-permute-start | bytes 393224 | tf_op jit(solution)/shard_map/ppermute | solution.py:305
  62.5 3.0 %collective-permute-start.4 = (bf16[128,512]{1,0:T(8,128)(2,1)S(1)}, bf16[128,512]{1,0:T(8,128)(2,1)S(1)}, u32[]{:S(2)}, u32[]{:S(2)}) collective-permute-start(bf16[128,512]{1,0:T(8,128)(2,1)S(1)} %get-tuple-element.22), channel_id=1, source_target_pairs={{0,256},{128,384},{256,0},{384,128},{1,257},{129,385},{257,1},{385... | collective-permute-start | bytes 393224 | tf_op jit(solution)/shard_map/ppermute | solution.py:305
  65.6 4.0 %collective-permute-start.5 = (bf16[128,512]{1,0:T(8,128)(2,1)S(1)}, bf16[128,512]{1,0:T(8,128)(2,1)S(1)}, u32[]{:S(2)}, u32[]{:S(2)}) collective-permute-start(bf16[128,512]{1,0:T(8,128)(2,1)S(1)} %get-tuple-element.23), channel_id=1, source_target_pairs={{0,128},{128,256},{256,384},{384,0},{1,129},{129,257},{257,385},{3... | collective-permute-start | bytes 393224 | tf_op jit(solution)/shard_map/ppermute | solution.py:305
  69.6 2.0 %collective-permute-done.4 = bf16[128,512]{1,0:T(8,128)(2,1)S(1)} collective-permute-done((bf16[128,512]{1,0:T(8,128)(2,1)S(1)}, bf16[128,512]{1,0:T(8,128)(2,1)S(1)}, u32[]{:S(2)}, u32[]{:S(2)}) %collective-permute-start.4) | collective-permute-done | bytes 131104 | tf_op jit(solution)/shard_map/ppermute | solution.py:305
  71.6 2.5 %collective-permute-done.5 = bf16[128,512]{1,0:T(8,128)(2,1)S(1)} collective-permute-done((bf16[128,512]{1,0:T(8,128)(2,1)S(1)}, bf16[128,512]{1,0:T(8,128)(2,1)S(1)}, u32[]{:S(2)}, u32[]{:S(2)}) %collective-permute-start.5) | collective-permute-done | bytes 131104 | tf_op jit(solution)/shard_map/ppermute | solution.py:305
  74.1 9.8 %all-to-all-done.1 = bf16[16,256,128]{2,1,0:T(8,128)(2,1)} async-done(((bf16[16,256,128]{2,1,0:T(8,128)(2,1)}), bf16[16,256,128]{2,1,0:T(8,128)(2,1)}, u32[]{:S(2)}, u32[]{:S(2)}) %all-to-all-start.1) | async-done | bytes 1048608 | tf_op jit(solution)/shard_map/all_to_all | solution.py:325
  83.9 1.4 %convert_reduce_fusion = f32[256,128]{1,0:T(8,128)S(1)} fusion(bf16[16,256,128]{2,1,0:T(8,128)(2,1)} %all-to-all-done.1), kind=kLoop, calls=%fused_computation.1 | loop fusion | flops 1015808 | bytes 1179648 | tf_op jit(solution)/shard_map/reduce_sum | solution.py:329
  85.3 1.9 %collective-permute-start.7 = (bf16[128,256]{1,0:T(8,128)(2,1)S(1)}, bf16[128,256]{1,0:T(8,128)(2,1)S(1)}, u32[]{:S(2)}, u32[]{:S(2)}) collective-permute-start(bf16[128,256]{1,0:T(8,128)(2,1)S(1)} %pad_maximum_fusion.1), channel_id=1, source_target_pairs={{0,1},{1,0},{2,3},{3,2},{4,5},{5,4},{6,7},{7,6},{8,9},{9,8},{10,11... | collective-permute-start | bytes 196616 | tf_op jit(solution)/shard_map/ppermute | solution.py:305
  87.2 0.5 fusion.1.own_ref
  87.7 0.7 collective-permute-done.7.other_ref
  88.5 1.3 %partial_hidden.1 = bf16[4,128,512]{2,1,0:T(8,128)(2,1)} custom-call(f32[128,2048]{1,0:T(8,128)S(1)} %fusion.1.own_ref, bf16[128,256]{1,0:T(8,128)(2,1)S(1)} %collective-permute-done.7.other_ref, bf16[2048,256]{1,0:T(8,128)(2,1)S(1)} %collective-permute-done.6.swapped_ref), custom_call_target="tpu_custom_call" | custom-call | tf_op jit(solution)/shard_map/partial_hidden/pallas_call | solution.py:272
  89.7 6.2 %all-to-all-start.2 = ((bf16[4,128,512]{2,1,0:T(8,128)(2,1)}), bf16[4,128,512]{2,1,0:T(8,128)(2,1)S(1)}, u32[]{:S(2)}, u32[]{:S(2)}) async-start(bf16[4,128,512]{2,1,0:T(8,128)(2,1)} %partial_hidden.1), calls=%async_computation.2 | async-start | bytes 1048576 | tf_op jit(solution)/shard_map/all_to_all | solution.py:335
  95.9 0.7 add_convert_fusion
  96.7 15.9 %all-to-all-done.2 = bf16[4,128,512]{2,1,0:T(8,128)(2,1)S(1)} async-done(((bf16[4,128,512]{2,1,0:T(8,128)(2,1)}), bf16[4,128,512]{2,1,0:T(8,128)(2,1)S(1)}, u32[]{:S(2)}, u32[]{:S(2)}) %all-to-all-start.2) | async-done | bytes 524320 | tf_op jit(solution)/shard_map/all_to_all | solution.py:335
  112.5 0.7 reduce_sum.22
  (21 shorter events, 0.1 us)
Async XLA Ops:
  0.6 42.6 %copy-start.2 = (s32[2]{0:T(128)S(1)}, s32[2]{0:T(128)}, u32[]{:S(2)}) copy-start(s32[2]{0:T(128)} %refs_1_.1) | copy-start | bytes 28
  0.6 42.6 %copy-start = (bf16[128,512]{1,0:T(8,128)(2,1)S(1)}, bf16[128,512]{1,0:T(8,128)(2,1)}, u32[]{:S(2)}) copy-start(bf16[128,512]{1,0:T(8,128)(2,1)} %refs_2_.1) | copy-start | bytes 393220
  0.7 42.6 %copy-start.1 = (bf16[128,512]{1,0:T(8,128)(2,1)S(1)}, bf16[128,512]{1,0:T(8,128)(2,1)}, u32[]{:S(2)}) copy-start(bf16[128,512]{1,0:T(8,128)(2,1)} %refs_3_.1) | copy-start | bytes 393220
  0.7 42.6 %copy-start.4 = (s32[2]{0:T(128)S(1)}, s32[2]{0:T(128)}, u32[]{:S(2)}) copy-start(s32[2]{0:T(128)} %refs_0_.1) | copy-start | bytes 28
  2.7 40.6 %all-to-all-start = ((bf16[16,272,128]{2,1,0:T(8,128)(2,1)}), bf16[16,272,128]{2,1,0:T(8,128)(2,1)S(1)}, u32[]{:S(2)}, u32[]{:S(2)}) async-start(bf16[16,272,128]{2,1,0:T(8,128)(2,1)} %pack.1), calls=%async_computation | async-start | bytes 2228224 | tf_op jit(solution)/shard_map/all_to_all | solution.py:313
  16.4 11.5 %collective-permute-start = (bf16[1056,128]{1,0:T(8,128)(2,1)}, bf16[1056,128]{1,0:T(8,128)(2,1)S(1)}, u32[]{:S(2)}, u32[]{:S(2)}) collective-permute-start(bf16[1056,128]{1,0:T(8,128)(2,1)} %get-tuple-element.18), channel_id=1, source_target_pairs={{0,128},{128,256},{256,384},{384,0},{1,129},{129,257},{257,385},{3... | collective-permute-start | bytes 811016 | tf_op jit(solution)/shard_map/ppermute | solution.py:305
  18.8 12.9 %collective-permute-start.1 = (bf16[1056,128]{1,0:T(8,128)(2,1)}, bf16[1056,128]{1,0:T(8,128)(2,1)S(1)}, u32[]{:S(2)}, u32[]{:S(2)}) collective-permute-start(bf16[1056,128]{1,0:T(8,128)(2,1)} %get-tuple-element.18), channel_id=1, source_target_pairs={{0,256},{128,384},{256,0},{384,128},{1,257},{129,385},{257,1},{385... | collective-permute-start | bytes 811016 | tf_op jit(solution)/shard_map/ppermute | solution.py:305
  23.1 12.4 %collective-permute-start.2 = (bf16[1056,128]{1,0:T(8,128)(2,1)}, bf16[1056,128]{1,0:T(8,128)(2,1)S(1)}, u32[]{:S(2)}, u32[]{:S(2)}) collective-permute-start(bf16[1056,128]{1,0:T(8,128)(2,1)} %get-tuple-element.18), channel_id=1, source_target_pairs={{0,384},{128,0},{256,128},{384,256},{1,385},{129,1},{257,129},{385... | collective-permute-start | bytes 811016 | tf_op jit(solution)/shard_map/ppermute | solution.py:305
  43.3 0.7 copy-start.3
  51.8 5.6 %copy-start.5 = (bf16[4096,128]{1,0:T(8,128)(2,1)S(1)}, bf16[4096,128]{1,0:T(8,128)(2,1)}, u32[]{:S(2)}) copy-start(bf16[4096,128]{1,0:T(8,128)(2,1)} %param.19) | copy-start | bytes 3145732
  51.9 5.6 %copy-start.6 = (bf16[4096,128]{1,0:T(8,128)(2,1)S(1)}, bf16[4096,128]{1,0:T(8,128)(2,1)}, u32[]{:S(2)}) copy-start(bf16[4096,128]{1,0:T(8,128)(2,1)} %param.18) | copy-start | bytes 3145732
  51.9 32.0 %all-to-all-start.1 = ((bf16[16,256,128]{2,1,0:T(8,128)(2,1)}), bf16[16,256,128]{2,1,0:T(8,128)(2,1)}, u32[]{:S(2)}, u32[]{:S(2)}) async-start(bf16[16,256,128]{2,1,0:T(8,128)(2,1)} %get-tuple-element.19), calls=%async_computation.1 | async-start | bytes 2097152 | tf_op jit(solution)/shard_map/all_to_all | solution.py:325
  57.9 11.7 %collective-permute-start.6 = (bf16[2048,256]{1,0:T(8,128)(2,1)S(1)}, bf16[2048,256]{1,0:T(8,128)(2,1)S(1)}, u32[]{:S(2)}, u32[]{:S(2)}) collective-permute-start(bf16[2048,256]{1,0:T(8,128)(2,1)S(1)} %bitcast.8), channel_id=1, source_target_pairs={{0,1},{1,0},{2,3},{3,2},{4,5},{5,4},{6,7},{7,6},{8,9},{9,8},{10,11... | collective-permute-start | bytes 3145736 | tf_op jit(solution)/shard_map/ppermute | solution.py:305
  59.8 9.8 %collective-permute-start.3 = (bf16[128,512]{1,0:T(8,128)(2,1)S(1)}, bf16[128,512]{1,0:T(8,128)(2,1)S(1)}, u32[]{:S(2)}, u32[]{:S(2)}) collective-permute-start(bf16[128,512]{1,0:T(8,128)(2,1)S(1)} %get-tuple-element.21), channel_id=1, source_target_pairs={{0,384},{128,0},{256,128},{384,256},{1,385},{129,1},{257,129},{385... | collective-permute-start | bytes 393224 | tf_op jit(solution)/shard_map/ppermute | solution.py:305
  62.5 9.1 %collective-permute-start.4 = (bf16[128,512]{1,0:T(8,128)(2,1)S(1)}, bf16[128,512]{1,0:T(8,128)(2,1)S(1)}, u32[]{:S(2)}, u32[]{:S(2)}) collective-permute-start(bf16[128,512]{1,0:T(8,128)(2,1)S(1)} %get-tuple-element.22), channel_id=1, source_target_pairs={{0,256},{128,384},{256,0},{384,128},{1,257},{129,385},{257,1},{385... | collective-permute-start | bytes 393224 | tf_op jit(solution)/shard_map/ppermute | solution.py:305
  65.6 8.5 %collective-permute-start.5 = (bf16[128,512]{1,0:T(8,128)(2,1)S(1)}, bf16[128,512]{1,0:T(8,128)(2,1)S(1)}, u32[]{:S(2)}, u32[]{:S(2)}) collective-permute-start(bf16[128,512]{1,0:T(8,128)(2,1)S(1)} %get-tuple-element.23), channel_id=1, source_target_pairs={{0,128},{128,256},{256,384},{384,0},{1,129},{129,257},{257,385},{3... | collective-permute-start | bytes 393224 | tf_op jit(solution)/shard_map/ppermute | solution.py:305
  85.3 4.5 %copy-start.7 = (bf16[128,128]{1,0:T(8,128)(2,1)}, bf16[128,128]{1,0:T(8,128)(2,1)S(1)}, u32[]{:S(2)}) copy-start(bf16[128,128]{1,0:T(8,128)(2,1)S(1)} %fusion) | copy-start | bytes 98308
  85.3 4.5 %copy-start.8 = (bf16[128,128]{1,0:T(8,128)(2,1)}, bf16[128,128]{1,0:T(8,128)(2,1)S(1)}, u32[]{:S(2)}) copy-start(bf16[128,128]{1,0:T(8,128)(2,1)S(1)} %slice.15) | copy-start | bytes 98308
  85.3 3.1 %collective-permute-start.7 = (bf16[128,256]{1,0:T(8,128)(2,1)S(1)}, bf16[128,256]{1,0:T(8,128)(2,1)S(1)}, u32[]{:S(2)}, u32[]{:S(2)}) collective-permute-start(bf16[128,256]{1,0:T(8,128)(2,1)S(1)} %pad_maximum_fusion.1), channel_id=1, source_target_pairs={{0,1},{1,0},{2,3},{3,2},{4,5},{5,4},{6,7},{7,6},{8,9},{9,8},{10,11... | collective-permute-start | bytes 196616 | tf_op jit(solution)/shard_map/ppermute | solution.py:305
  89.7 22.8 %all-to-all-start.2 = ((bf16[4,128,512]{2,1,0:T(8,128)(2,1)}), bf16[4,128,512]{2,1,0:T(8,128)(2,1)S(1)}, u32[]{:S(2)}, u32[]{:S(2)}) async-start(bf16[4,128,512]{2,1,0:T(8,128)(2,1)} %partial_hidden.1), calls=%async_computation.2 | async-start | bytes 1048576 | tf_op jit(solution)/shard_map/all_to_all | solution.py:335

commit v5 on v4

--- a/solution.py
+++ b/solution.py
@@ -29,6 +29,10 @@
 
 def nt(a, b):
     return lax.dot_general(a, b, (((1,), (1,)), ((), ())), preferred_element_type=F32)
+
+
+def tn(a, b):
+    return lax.dot_general(a, b, (((0,), (0,)), ((), ())), preferred_element_type=F32)
 
 
 def nn(a, b):
@@ -112,16 +116,14 @@
         upto = upto + (one <= q).astype(jnp.int32)
     real_k = sub < spans_k
     rank_line = total(jnp.where((lane == sub) & real_k, rank, 0))
-    in_order = total(jnp.where((lane == rank) & real_k, k, 0))
-    shift = PER.bit_length() - 1
-    low, high = below >> shift, (upto + PER - 1) >> shift
-    count = jnp.where(sub < spans_q, high - low, 0)
+    in_order = total(jnp.where((lane == rank) & real_k, k, 0)) + jnp.where(lane[:1] >= spans_k, 1 << 20, 0)
+    count = jnp.where(sub < spans_q, (upto - below + PER - 1) >> (PER.bit_length() - 1), 0)
     end = zero
     for i in range(spans_q):
         end = end + jnp.where(sub >= i, count[i : i + 1], 0)
     place = total(jnp.where((lane >= end) & (sub < spans_q), 1, 0))
     mine = sub == place
-    chunk = lane[:1] + total(jnp.where(mine, high - end, 0))
+    chunk = total(jnp.where(mine, below + PER * (count - end), 0)) + PER * lane[:1]
     span = total(jnp.where(mine, q, 0))
     unused = place >= spans_q
     span = jnp.where(unused, -(1 << 20), span)
@@ -134,7 +136,7 @@
 def tile_kernel(n_q, n_x, n_k, doc_ref, span_ref, *refs):
     (own_q, own_g, own_rows), other_blocks, gkv_ref, refs = refs[:3], refs[3 : n_q + 2], refs[n_q + 2], refs[n_q + 3 :]
     dq_refs, dkv_out, refs = refs[:n_x], refs[n_x], refs[n_x + 1 :]
-    dkv_ref, plan_v, plan_s, sems, q_s, g_s, k_s, v_s, kt_s, dk_acc, dv_acc, dqt_acc, lse_s, del_s = refs
+    dkv_ref, plan_v, plan_s, sems, q_s, g_s, k_s, v_s, dk_acc, dv_acc, dqt_acc, lse_s, del_s = refs
     spans_k = 2 * n_k
     scale = 1.0 / math.sqrt(HD)
     log2e = 1.0 / math.log(2.0)
@@ -143,6 +145,8 @@
     plan_v[...] = plan_tiles(span_ref, other_blocks, gkv_ref, boundary)
     tell = pltpu.make_async_copy(plan_v, plan_s, sems.at[0])
     tell.start()
+    k_s[spans_k * SPAN :, :] = jnp.zeros((CHUNK - SPAN, HD), BF)
+    v_s[spans_k * SPAN :, :] = jnp.zeros((CHUNK - SPAN, HD), BF)
     dk_acc[...] = jnp.zeros_like(dk_acc)
     dv_acc[...] = jnp.zeros_like(dv_acc)
     dqt_acc[...] = jnp.zeros_like(dqt_acc)
@@ -173,8 +177,6 @@
             to = pl.ds(pl.multiple_of(plan_s[0, 2 * w + s] * SPAN, SPAN), SPAN)
             k_s[to, :] = gkv_ref[w, s * SPAN : (s + 1) * SPAN, :]
             v_s[to, :] = gkv_ref[w, TOK + s * SPAN : TOK + (s + 1) * SPAN, :]
-    for c in range(spans_k // PER):
-        kt_s[c] = k_s[c * CHUNK : (c + 1) * CHUNK, :].T
 
     key_line = lax.broadcasted_iota(jnp.int32, (SPAN, QROWS), 0)
     row_off = lax.broadcasted_iota(jnp.int32, (1, QROWS), 1) % SPAN
@@ -182,7 +184,7 @@
     def open_tile(t):
         span, i, c = plan_s[2, t], plan_s[3, t], plan_s[4, t]
         q_rows = pl.ds(pl.multiple_of(i * QROWS, QROWS), QROWS)
-        k_rows = pl.ds(pl.multiple_of(c * CHUNK, CHUNK), CHUNK)
+        k_rows = pl.ds(pl.multiple_of(c * SPAN, SPAN), CHUNK)
         score = nt(k_s[k_rows, :], q_s[q_rows, :])
         dprob = nt(v_s[k_rows, :], g_s[q_rows, :])
         lse, dlt = lse_s[i][0:1], del_s[i][0:1]
@@ -191,7 +193,7 @@
         probs, dscores = [], []
         for j in range(PER):
             part = slice(j * SPAN, (j + 1) * SPAN)
-            base = plan_s[1, c * PER + j] * SPAN
+            base = plan_s[1, c + j] * SPAN
             live = (key_line <= q_pos - base) & (key_line >= q_start - base)
             prob = jnp.where(live, jnp.exp2(score[part] * (scale * log2e) - lse), 0.0)
             probs.append(prob.astype(BF))
@@ -201,7 +203,7 @@
     def close_tile(i, c, q_rows, k_rows, prob_b, dscore_b):
         dv_acc[k_rows, :] += nn(prob_b, g_s[q_rows, :])
         dk_acc[k_rows, :] += nn(dscore_b, q_s[q_rows, :])
-        dqt_acc[i] += nn(kt_s[c], dscore_b)
+        dqt_acc[i] += tn(dscore_b, k_s[k_rows, :])
 
     def step(t, _):
         for u in range(0, UNROLL, 2):
@@ -221,7 +223,7 @@
             sends.append(pltpu.make_async_copy(dkv_ref.at[some], dkv_out.at[some], sems.at[1 + w // 4]))
             sends[-1].start()
     for i in range(2 * n_q):
-        dq = (dqt_acc[i] * scale).astype(BF).T
+        dq = (dqt_acc[i] * scale).astype(BF)
         place, s = i // 2, i % 2
         at = place // n_x * TOK + s * SPAN
         for h in range(HQ):
@@ -245,12 +247,11 @@
             pltpu.SemaphoreType.DMA((1 + n_k // 4,)),
             pltpu.VMEM((rows, HD), BF),
             pltpu.VMEM((rows, HD), BF),
-            pltpu.VMEM((keys, HD), BF),
-            pltpu.VMEM((keys, HD), BF),
-            pltpu.VMEM((keys // CHUNK, HD, CHUNK), BF),
-            pltpu.VMEM((keys, HD), F32),
-            pltpu.VMEM((keys, HD), F32),
-            pltpu.VMEM((2 * n_q, HD, QROWS), F32),
+            pltpu.VMEM((keys + CHUNK - SPAN, HD), BF),
+            pltpu.VMEM((keys + CHUNK - SPAN, HD), BF),
+            pltpu.VMEM((keys + CHUNK - SPAN, HD), F32),
+            pltpu.VMEM((keys + CHUNK - SPAN, HD), F32),
+            pltpu.VMEM((2 * n_q, QROWS, HD), F32),
             pltpu.VMEM((2 * n_q, 8, QROWS), F32),
             pltpu.VMEM((2 * n_q, 8, QROWS), F32),
         ],

time: 115 us -> 115 us (level); the launches traced: 113 us -> 115 us
  starting transfers between devices: 45.8 us -> 47 us
where the time goes in v5:
time: 115 us
  waiting for transfers between devices  50.2 us (44%)
  starting transfers between devices  47 us (41%)
  Pallas kernels  12.2 us (11%)
  other arithmetic  3.09 us (3%)
    ppermute x8, starting transfers between devices, hop(): return lax.ppermute(block, axis, [(i, (i + shift) % n) for i in range(n)])  22.2 us
    all_to_all x1, waiting for transfers between devices, body(): shares = lax.all_to_all(partial, 'y_hi', 0, 0)  16.2 us
    ppermute x8, waiting for transfers between devices, hop(): return lax.ppermute(block, axis, [(i, (i + shift) % n) for i in range(n)])  15.8 us
    all_to_all x1, starting transfers between devices, body(): lax.all_to_all(pack(span_order, key_rows, value_rows, n_k), KEYS, 0, 0)  11.8 us
    all_to_all x1, waiting for transfers between devices, body(): parts = lax.all_to_all(dkv, KEYS, 0, 0)  10.5 us
    all_to_all x1, waiting for transfers between devices, body(): lax.all_to_all(pack(span_order, key_rows, value_rows, n_k), KEYS, 0, 0)  7.69 us
    pallas_call x1, Pallas kernels, tile_grads(): pl.pallas_call(lambda *refs: tile_kernel(n_q, n_x, n_k, *refs), out_shape...  6.96 us
    all_to_all x1, starting transfers between devices, body(): parts = lax.all_to_all(dkv, KEYS, 0, 0)  6.75 us
  transfers between devices with their start and end apart: 11, of which 9 were waited for; matrix products, arithmetic and copies ran while one was open for 1% of the time, Pallas kernels for 2%

profile of v5, /device:TPU:14, one launch (start us, length us, event | category | flops | bytes accessed | tf_op | source)
XLA Modules:
  0.0 114.6 jit_solution(15206160693121668966)
XLA Ops:
  0.6 0.0 copy-start.2
  0.7 2.0 %pack.1 = bf16[16,272,128]{2,1,0:T(8,128)(2,1)} custom-call(s32[2]{0:T(128)} %refs_1_.1, bf16[128,128]{1,0:T(8,128)(2,1)} %k_ref.1, bf16[128,128]{1,0:T(8,128)(2,1)} %v_ref.1), custom_call_target="tpu_custom_call" | custom-call | tf_op jit(solution)/shard_map/pack/pallas_call | solution.py:294
  2.7 11.8 %all-to-all-start = ((bf16[16,272,128]{2,1,0:T(8,128)(2,1)}), bf16[16,272,128]{2,1,0:T(8,128)(2,1)S(1)}, u32[]{:S(2)}, u32[]{:S(2)}) async-start(bf16[16,272,128]{2,1,0:T(8,128)(2,1)} %pack.1), calls=%async_computation | async-start | bytes 2228224 | tf_op jit(solution)/shard_map/all_to_all | solution.py:314
  14.5 1.9 %prep.1 = (bf16[1056,128]{1,0:T(8,128)(2,1)}, f32[24,128]{1,0:T(8,128)}) custom-call(s32[2]{0:T(128)} %refs_1_.1, bf16[128,512]{1,0:T(8,128)(2,1)} %refs_2_.1, bf16[128,512]{1,0:T(8,128)(2,1)} %refs_3_.1, bf16[128,512]{1,0:T(8,128)(2,1)} %o_ref.1, f32[4,128]{1,0:T(4,128)} %lse_ref.1), custom_call_target="tpu_custom_call" | custom-call | tf_op jit(solution)/shard_map/prep/pallas_call | solution.py:284
  16.4 2.4 %collective-permute-start = (bf16[1056,128]{1,0:T(8,128)(2,1)}, bf16[1056,128]{1,0:T(8,128)(2,1)S(1)}, u32[]{:S(2)}, u32[]{:S(2)}) collective-permute-start(bf16[1056,128]{1,0:T(8,128)(2,1)} %get-tuple-element.18), channel_id=1, source_target_pairs={{0,128},{128,256},{256,384},{384,0},{1,129},{129,257},{257,385},{3... | collective-permute-start | bytes 811016 | tf_op jit(solution)/shard_map/ppermute | solution.py:306
  18.8 4.3 %collective-permute-start.1 = (bf16[1056,128]{1,0:T(8,128)(2,1)}, bf16[1056,128]{1,0:T(8,128)(2,1)S(1)}, u32[]{:S(2)}, u32[]{:S(2)}) collective-permute-start(bf16[1056,128]{1,0:T(8,128)(2,1)} %get-tuple-element.18), channel_id=1, source_target_pairs={{0,256},{128,384},{256,0},{384,128},{1,257},{129,385},{257,1},{385... | collective-permute-start | bytes 811016 | tf_op jit(solution)/shard_map/ppermute | solution.py:306
  23.1 1.9 %collective-permute-start.2 = (bf16[1056,128]{1,0:T(8,128)(2,1)}, bf16[1056,128]{1,0:T(8,128)(2,1)S(1)}, u32[]{:S(2)}, u32[]{:S(2)}) collective-permute-start(bf16[1056,128]{1,0:T(8,128)(2,1)} %get-tuple-element.18), channel_id=1, source_target_pairs={{0,384},{128,0},{256,128},{384,256},{1,385},{129,1},{257,129},{385... | collective-permute-start | bytes 811016 | tf_op jit(solution)/shard_map/ppermute | solution.py:306
  25.1 2.9 %collective-permute-done.refs_5_ = bf16[1056,128]{1,0:T(8,128)(2,1)S(1)} collective-permute-done((bf16[1056,128]{1,0:T(8,128)(2,1)}, bf16[1056,128]{1,0:T(8,128)(2,1)S(1)}, u32[]{:S(2)}, u32[]{:S(2)}) %collective-permute-start) | collective-permute-done | bytes 270368 | tf_op jit(solution)/shard_map/ppermute | solution.py:306
  27.9 3.8 %collective-permute-done.1.refs_6_ = bf16[1056,128]{1,0:T(8,128)(2,1)S(1)} collective-permute-done((bf16[1056,128]{1,0:T(8,128)(2,1)}, bf16[1056,128]{1,0:T(8,128)(2,1)S(1)}, u32[]{:S(2)}, u32[]{:S(2)}) %collective-permute-start.1) | collective-permute-done | bytes 270368 | tf_op jit(solution)/shard_map/ppermute | solution.py:306
  31.7 3.9 %collective-permute-done.2.refs_7_ = bf16[1056,128]{1,0:T(8,128)(2,1)S(1)} collective-permute-done((bf16[1056,128]{1,0:T(8,128)(2,1)}, bf16[1056,128]{1,0:T(8,128)(2,1)S(1)}, u32[]{:S(2)}, u32[]{:S(2)}) %collective-permute-start.2) | collective-permute-done | bytes 270368 | tf_op jit(solution)/shard_map/ppermute | solution.py:306
  35.6 7.7 %all-to-all-done.refs_8_ = bf16[16,272,128]{2,1,0:T(8,128)(2,1)S(1)} async-done(((bf16[16,272,128]{2,1,0:T(8,128)(2,1)}), bf16[16,272,128]{2,1,0:T(8,128)(2,1)S(1)}, u32[]{:S(2)}, u32[]{:S(2)}) %all-to-all-start) | async-done | bytes 1114144 | tf_op jit(solution)/shard_map/all_to_all | solution.py:314
  43.3 0.7 copy-done.3
  44.0 7.0 %tile_grads.1 = (bf16[128,512]{1,0:T(8,128)(2,1)S(1)}, bf16[128,512]{1,0:T(8,128)(2,1)S(1)}, bf16[128,512]{1,0:T(8,128)(2,1)S(1)}, bf16[128,512]{1,0:T(8,128)(2,1)S(1)}, bf16[16,256,128]{2,1,0:T(8,128)(2,1)}) custom-call(s32[2]{0:T(128)S(1)} %copy-done.4, s32[2]{0:T(128)S(1)} %copy-done.2, bf16[128,512]{1,0:T(8,128)(2,1)S(1)} %copy-done, ...), custom_call_target="tpu_custom_call" | custom-call | flops 5000000000 | bytes 4000000 | tf_op jit(solution)/shard_map/tile_grads/pallas_call | solution.py:238
  51.0 6.8 %all-to-all-start.1 = ((bf16[16,256,128]{2,1,0:T(8,128)(2,1)}), bf16[16,256,128]{2,1,0:T(8,128)(2,1)}, u32[]{:S(2)}, u32[]{:S(2)}) async-start(bf16[16,256,128]{2,1,0:T(8,128)(2,1)} %get-tuple-element.19), calls=%async_computation.1 | async-start | bytes 2097152 | tf_op jit(solution)/shard_map/all_to_all | solution.py:326
  57.8 0.2 pad_maximum_fusion
  58.0 0.1 constant_dynamic-slice_fusion
  58.1 1.9 %collective-permute-start.6 = (bf16[2048,256]{1,0:T(8,128)(2,1)S(1)}, bf16[2048,256]{1,0:T(8,128)(2,1)S(1)}, u32[]{:S(2)}, u32[]{:S(2)}) collective-permute-start(bf16[2048,256]{1,0:T(8,128)(2,1)S(1)} %bitcast.8), channel_id=1, source_target_pairs={{0,1},{1,0},{2,3},{3,2},{4,5},{5,4},{6,7},{7,6},{8,9},{9,8},{10,11... | collective-permute-start | bytes 3145736 | tf_op jit(solution)/shard_map/ppermute | solution.py:306
  60.1 2.7 %collective-permute-start.3 = (bf16[128,512]{1,0:T(8,128)(2,1)S(1)}, bf16[128,512]{1,0:T(8,128)(2,1)S(1)}, u32[]{:S(2)}, u32[]{:S(2)}) collective-permute-start(bf16[128,512]{1,0:T(8,128)(2,1)S(1)} %get-tuple-element.21), channel_id=1, source_target_pairs={{0,384},{128,0},{256,128},{384,256},{1,385},{129,1},{257,129},{385... | collective-permute-start | bytes 393224 | tf_op jit(solution)/shard_map/ppermute | solution.py:306
  62.8 3.0 %collective-permute-start.4 = (bf16[128,512]{1,0:T(8,128)(2,1)S(1)}, bf16[128,512]{1,0:T(8,128)(2,1)S(1)}, u32[]{:S(2)}, u32[]{:S(2)}) collective-permute-start(bf16[128,512]{1,0:T(8,128)(2,1)S(1)} %get-tuple-element.22), channel_id=1, source_target_pairs={{0,256},{128,384},{256,0},{384,128},{1,257},{129,385},{257,1},{385... | collective-permute-start | bytes 393224 | tf_op jit(solution)/shard_map/ppermute | solution.py:306
  65.8 4.0 %collective-permute-start.5 = (bf16[128,512]{1,0:T(8,128)(2,1)S(1)}, bf16[128,512]{1,0:T(8,128)(2,1)S(1)}, u32[]{:S(2)}, u32[]{:S(2)}) collective-permute-start(bf16[128,512]{1,0:T(8,128)(2,1)S(1)} %get-tuple-element.23), channel_id=1, source_target_pairs={{0,128},{128,256},{256,384},{384,0},{1,129},{129,257},{257,385},{3... | collective-permute-start | bytes 393224 | tf_op jit(solution)/shard_map/ppermute | solution.py:306
  69.9 2.0 %collective-permute-done.4 = bf16[128,512]{1,0:T(8,128)(2,1)S(1)} collective-permute-done((bf16[128,512]{1,0:T(8,128)(2,1)S(1)}, bf16[128,512]{1,0:T(8,128)(2,1)S(1)}, u32[]{:S(2)}, u32[]{:S(2)}) %collective-permute-start.4) | collective-permute-done | bytes 131104 | tf_op jit(solution)/shard_map/ppermute | solution.py:306
  71.9 2.5 %collective-permute-done.5 = bf16[128,512]{1,0:T(8,128)(2,1)S(1)} collective-permute-done((bf16[128,512]{1,0:T(8,128)(2,1)S(1)}, bf16[128,512]{1,0:T(8,128)(2,1)S(1)}, u32[]{:S(2)}, u32[]{:S(2)}) %collective-permute-start.5) | collective-permute-done | bytes 131104 | tf_op jit(solution)/shard_map/ppermute | solution.py:306
  74.4 10.5 %all-to-all-done.1 = bf16[16,256,128]{2,1,0:T(8,128)(2,1)} async-done(((bf16[16,256,128]{2,1,0:T(8,128)(2,1)}), bf16[16,256,128]{2,1,0:T(8,128)(2,1)}, u32[]{:S(2)}, u32[]{:S(2)}) %all-to-all-start.1) | async-done | bytes 1048608 | tf_op jit(solution)/shard_map/all_to_all | solution.py:326
  84.9 1.4 %convert_reduce_fusion = f32[256,128]{1,0:T(8,128)S(1)} fusion(bf16[16,256,128]{2,1,0:T(8,128)(2,1)} %all-to-all-done.1), kind=kLoop, calls=%fused_computation.1 | loop fusion | flops 1015808 | bytes 1179648 | tf_op jit(solution)/shard_map/reduce_sum | solution.py:330
  86.3 1.9 %collective-permute-start.7 = (bf16[128,256]{1,0:T(8,128)(2,1)S(1)}, bf16[128,256]{1,0:T(8,128)(2,1)S(1)}, u32[]{:S(2)}, u32[]{:S(2)}) collective-permute-start(bf16[128,256]{1,0:T(8,128)(2,1)S(1)} %pad_maximum_fusion.1), channel_id=1, source_target_pairs={{0,1},{1,0},{2,3},{3,2},{4,5},{5,4},{6,7},{7,6},{8,9},{9,8},{10,11... | collective-permute-start | bytes 196616 | tf_op jit(solution)/shard_map/ppermute | solution.py:306
  88.2 0.5 fusion.1.own_ref
  88.7 0.7 collective-permute-done.7.other_ref
  89.5 1.3 %partial_hidden.1 = bf16[4,128,512]{2,1,0:T(8,128)(2,1)} custom-call(f32[128,2048]{1,0:T(8,128)S(1)} %fusion.1.own_ref, bf16[128,256]{1,0:T(8,128)(2,1)S(1)} %collective-permute-done.7.other_ref, bf16[2048,256]{1,0:T(8,128)(2,1)S(1)} %collective-permute-done.6.swapped_ref), custom_call_target="tpu_custom_call" | custom-call | tf_op jit(solution)/shard_map/partial_hidden/pallas_call | solution.py:273
  90.7 6.2 %all-to-all-start.2 = ((bf16[4,128,512]{2,1,0:T(8,128)(2,1)}), bf16[4,128,512]{2,1,0:T(8,128)(2,1)S(1)}, u32[]{:S(2)}, u32[]{:S(2)}) async-start(bf16[4,128,512]{2,1,0:T(8,128)(2,1)} %partial_hidden.1), calls=%async_computation.2 | async-start | bytes 1048576 | tf_op jit(solution)/shard_map/all_to_all | solution.py:336
  96.9 0.7 add_convert_fusion
  97.7 16.2 %all-to-all-done.2 = bf16[4,128,512]{2,1,0:T(8,128)(2,1)S(1)} async-done(((bf16[4,128,512]{2,1,0:T(8,128)(2,1)}), bf16[4,128,512]{2,1,0:T(8,128)(2,1)S(1)}, u32[]{:S(2)}, u32[]{:S(2)}) %all-to-all-start.2) | async-done | bytes 524320 | tf_op jit(solution)/shard_map/all_to_all | solution.py:336
  113.9 0.7 reduce_sum.22
  (21 shorter events, 0.1 us)
Async XLA Ops:
  0.6 42.6 %copy-start.2 = (s32[2]{0:T(128)S(1)}, s32[2]{0:T(128)}, u32[]{:S(2)}) copy-start(s32[2]{0:T(128)} %refs_1_.1) | copy-start | bytes 28
  0.6 42.6 %copy-start = (bf16[128,512]{1,0:T(8,128)(2,1)S(1)}, bf16[128,512]{1,0:T(8,128)(2,1)}, u32[]{:S(2)}) copy-start(bf16[128,512]{1,0:T(8,128)(2,1)} %refs_2_.1) | copy-start | bytes 393220
  0.7 42.6 %copy-start.1 = (bf16[128,512]{1,0:T(8,128)(2,1)S(1)}, bf16[128,512]{1,0:T(8,128)(2,1)}, u32[]{:S(2)}) copy-start(bf16[128,512]{1,0:T(8,128)(2,1)} %refs_3_.1) | copy-start | bytes 393220
  0.7 42.6 %copy-start.4 = (s32[2]{0:T(128)S(1)}, s32[2]{0:T(128)}, u32[]{:S(2)}) copy-start(s32[2]{0:T(128)} %refs_0_.1) | copy-start | bytes 28
  2.7 40.6 %all-to-all-start = ((bf16[16,272,128]{2,1,0:T(8,128)(2,1)}), bf16[16,272,128]{2,1,0:T(8,128)(2,1)S(1)}, u32[]{:S(2)}, u32[]{:S(2)}) async-start(bf16[16,272,128]{2,1,0:T(8,128)(2,1)} %pack.1), calls=%async_computation | async-start | bytes 2228224 | tf_op jit(solution)/shard_map/all_to_all | solution.py:314
  16.4 11.5 %collective-permute-start = (bf16[1056,128]{1,0:T(8,128)(2,1)}, bf16[1056,128]{1,0:T(8,128)(2,1)S(1)}, u32[]{:S(2)}, u32[]{:S(2)}) collective-permute-start(bf16[1056,128]{1,0:T(8,128)(2,1)} %get-tuple-element.18), channel_id=1, source_target_pairs={{0,128},{128,256},{256,384},{384,0},{1,129},{129,257},{257,385},{3... | collective-permute-start | bytes 811016 | tf_op jit(solution)/shard_map/ppermute | solution.py:306
  18.8 12.9 %collective-permute-start.1 = (bf16[1056,128]{1,0:T(8,128)(2,1)}, bf16[1056,128]{1,0:T(8,128)(2,1)S(1)}, u32[]{:S(2)}, u32[]{:S(2)}) collective-permute-start(bf16[1056,128]{1,0:T(8,128)(2,1)} %get-tuple-element.18), channel_id=1, source_target_pairs={{0,256},{128,384},{256,0},{384,128},{1,257},{129,385},{257,1},{385... | collective-permute-start | bytes 811016 | tf_op jit(solution)/shard_map/ppermute | solution.py:306
  23.1 12.4 %collective-permute-start.2 = (bf16[1056,128]{1,0:T(8,128)(2,1)}, bf16[1056,128]{1,0:T(8,128)(2,1)S(1)}, u32[]{:S(2)}, u32[]{:S(2)}) collective-permute-start(bf16[1056,128]{1,0:T(8,128)(2,1)} %get-tuple-element.18), channel_id=1, source_target_pairs={{0,384},{128,0},{256,128},{384,256},{1,385},{129,1},{257,129},{385... | collective-permute-start | bytes 811016 | tf_op jit(solution)/shard_map/ppermute | solution.py:306
  43.3 0.7 copy-start.3
  51.0 6.8 %copy-start.5 = (bf16[4096,128]{1,0:T(8,128)(2,1)S(1)}, bf16[4096,128]{1,0:T(8,128)(2,1)}, u32[]{:S(2)}) copy-start(bf16[4096,128]{1,0:T(8,128)(2,1)} %param.19) | copy-start | bytes 3145732
  51.0 6.8 %copy-start.6 = (bf16[4096,128]{1,0:T(8,128)(2,1)S(1)}, bf16[4096,128]{1,0:T(8,128)(2,1)}, u32[]{:S(2)}) copy-start(bf16[4096,128]{1,0:T(8,128)(2,1)} %param.18) | copy-start | bytes 3145732
  51.0 33.9 %all-to-all-start.1 = ((bf16[16,256,128]{2,1,0:T(8,128)(2,1)}), bf16[16,256,128]{2,1,0:T(8,128)(2,1)}, u32[]{:S(2)}, u32[]{:S(2)}) async-start(bf16[16,256,128]{2,1,0:T(8,128)(2,1)} %get-tuple-element.19), calls=%async_computation.1 | async-start | bytes 2097152 | tf_op jit(solution)/shard_map/all_to_all | solution.py:326
  58.1 11.7 %collective-permute-start.6 = (bf16[2048,256]{1,0:T(8,128)(2,1)S(1)}, bf16[2048,256]{1,0:T(8,128)(2,1)S(1)}, u32[]{:S(2)}, u32[]{:S(2)}) collective-permute-start(bf16[2048,256]{1,0:T(8,128)(2,1)S(1)} %bitcast.8), channel_id=1, source_target_pairs={{0,1},{1,0},{2,3},{3,2},{4,5},{5,4},{6,7},{7,6},{8,9},{9,8},{10,11... | collective-permute-start | bytes 3145736 | tf_op jit(solution)/shard_map/ppermute | solution.py:306
  60.1 9.8 %collective-permute-start.3 = (bf16[128,512]{1,0:T(8,128)(2,1)S(1)}, bf16[128,512]{1,0:T(8,128)(2,1)S(1)}, u32[]{:S(2)}, u32[]{:S(2)}) collective-permute-start(bf16[128,512]{1,0:T(8,128)(2,1)S(1)} %get-tuple-element.21), channel_id=1, source_target_pairs={{0,384},{128,0},{256,128},{384,256},{1,385},{129,1},{257,129},{385... | collective-permute-start | bytes 393224 | tf_op jit(solution)/shard_map/ppermute | solution.py:306
  62.8 9.1 %collective-permute-start.4 = (bf16[128,512]{1,0:T(8,128)(2,1)S(1)}, bf16[128,512]{1,0:T(8,128)(2,1)S(1)}, u32[]{:S(2)}, u32[]{:S(2)}) collective-permute-start(bf16[128,512]{1,0:T(8,128)(2,1)S(1)} %get-tuple-element.22), channel_id=1, source_target_pairs={{0,256},{128,384},{256,0},{384,128},{1,257},{129,385},{257,1},{385... | collective-permute-start | bytes 393224 | tf_op jit(solution)/shard_map/ppermute | solution.py:306
  65.8 8.5 %collective-permute-start.5 = (bf16[128,512]{1,0:T(8,128)(2,1)S(1)}, bf16[128,512]{1,0:T(8,128)(2,1)S(1)}, u32[]{:S(2)}, u32[]{:S(2)}) collective-permute-start(bf16[128,512]{1,0:T(8,128)(2,1)S(1)} %get-tuple-element.23), channel_id=1, source_target_pairs={{0,128},{128,256},{256,384},{384,0},{1,129},{129,257},{257,385},{3... | collective-permute-start | bytes 393224 | tf_op jit(solution)/shard_map/ppermute | solution.py:306
  86.3 4.5 %copy-start.7 = (bf16[128,128]{1,0:T(8,128)(2,1)}, bf16[128,128]{1,0:T(8,128)(2,1)S(1)}, u32[]{:S(2)}) copy-start(bf16[128,128]{1,0:T(8,128)(2,1)S(1)} %fusion) | copy-start | bytes 98308
  86.3 4.5 %copy-start.8 = (bf16[128,128]{1,0:T(8,128)(2,1)}, bf16[128,128]{1,0:T(8,128)(2,1)S(1)}, u32[]{:S(2)}) copy-start(bf16[128,128]{1,0:T(8,128)(2,1)S(1)} %slice.15) | copy-start | bytes 98308
  86.3 3.1 %collective-permute-start.7 = (bf16[128,256]{1,0:T(8,128)(2,1)S(1)}, bf16[128,256]{1,0:T(8,128)(2,1)S(1)}, u32[]{:S(2)}, u32[]{:S(2)}) collective-permute-start(bf16[128,256]{1,0:T(8,128)(2,1)S(1)} %pad_maximum_fusion.1), channel_id=1, source_target_pairs={{0,1},{1,0},{2,3},{3,2},{4,5},{5,4},{6,7},{7,6},{8,9},{9,8},{10,11... | collective-permute-start | bytes 196616 | tf_op jit(solution)/shard_map/ppermute | solution.py:306
  90.7 23.1 %all-to-all-start.2 = ((bf16[4,128,512]{2,1,0:T(8,128)(2,1)}), bf16[4,128,512]{2,1,0:T(8,128)(2,1)S(1)}, u32[]{:S(2)}, u32[]{:S(2)}) async-start(bf16[4,128,512]{2,1,0:T(8,128)(2,1)} %partial_hidden.1), calls=%async_computation.2 | async-start | bytes 1048576 | tf_op jit(solution)/shard_map/all_to_all | solution.py:336
